TPU v7x, 128 devices: a whole 4x4x4 slice. The times are simulated.
128 devices in a mesh: rows: 8 (over x, z_hi), ci: 4 (over z_lo, core), cj: 4 (over y).
Axes of the slice: x: 4, y: 4, z: 4 (z_hi: 2, z_lo: 2; z = z_hi * 2 + z_lo), core: 2. Of those that a mesh axis runs over, the one named last changes fastest.
Arguments:
- matrix: float32 [2048, 49152], P('rows', ('ci', 'cj')), may hold values from -585 to 585
- sample: int32 [4, 4, 2048], P('ci', None, 'rows'), may hold values 0 or 1
Outputs:
- cosine: float32 [4, 12288, 4, 384], P('ci', 'rows', 'cj')
All inputs are finite; a program needn't handle non-finite values. No bound on the sum of `sample` on one device may be relied on, other than what follows from the above.
Results may differ from a plain program's by a relative error of at most 0.000054.
Values sent between devices are 32-bit elements; how exact they have to be, the bound alone decides.
No kernel may reach another device: no remote copies, remote signals or barrier semaphores. Data moves between devices by JAX's collectives and lax.ppermute only.
A program may use at most 128 MiB of HBM per device.

v0:
```python
import jax
import jax.numpy as jnp
from jax import lax
from jax.sharding import PartitionSpec as P

QUERY = 1536


EPS = 1e-06
KEEP = 2.0


def from_everyone(shard, axis):
    length = lax.axis_size(axis)
    return lax.all_to_all(
        jnp.broadcast_to(shard[None], (length, *shard.shape)), axis, 0, 0, tiled=True
    )


def taken_together(shard, axis):
    return from_everyone(shard, axis).sum(axis=0)


def in_order(parts, dim):
    parts = jnp.moveaxis(parts, 0, dim)
    lengths = parts.shape
    return parts.reshape(*lengths[:dim], lengths[dim] * lengths[dim + 1], *lengths[dim + 2 :])


def gathered_copies(shard, axis, dim):
    parts = from_everyone(shard, axis)
    return in_order(parts, dim)


def shards(matrix, sample):
    local_squares = jnp.sum(matrix * matrix, axis=0)
    total_squares = taken_together(local_squares, "rows")
    inverse = 1.0 / jnp.sqrt(total_squares + EPS)
    unit = matrix * inverse[None, :]
    count_ci = lax.axis_size("ci")
    count_cj = lax.axis_size("cj")
    count_rows = lax.axis_size("rows")
    row_count = matrix.shape[0]
    query_slab = QUERY // (count_ci * count_cj)
    queries = unit[:, :query_slab] * KEEP
    swapped = lax.all_to_all(unit, "cj", split_axis=0, concat_axis=1, tiled=True)
    ranged = lax.all_to_all(swapped, "rows", split_axis=1, concat_axis=0, tiled=True)
    columns = lax.all_gather(ranged, "cj", axis=0, tiled=True)
    picks = lax.dynamic_index_in_dim(sample[0], lax.axis_index("cj"), 0, keepdims=False).astype(
        jnp.float32
    )
    part_group = gathered_copies(queries, "ci", 1) * picks[:, None]
    masked = lax.all_gather(part_group, "rows", axis=0, tiled=True)
    group_width = masked.shape[1]
    reordered = masked.reshape(count_rows, count_cj, row_count // count_cj, group_width)
    reordered = jnp.transpose(reordered, (1, 0, 2, 3)).reshape(count_rows * row_count, group_width)
    result = jnp.dot(
        jnp.transpose(columns),
        reordered,
        precision=lax.Precision.HIGHEST,
        preferred_element_type=jnp.float32,
    )
    return result[None, :, None, :]


def solution(mesh):
    in_specs = (P("rows", ("ci", "cj")), P("ci", None, "rows"))
    out_specs = P("ci", "rows", "cj", None)
    return jax.shard_map(shards, mesh=mesh, in_specs=in_specs, out_specs=out_specs, check_vma=False)
```

profile of v0, /device:TPU:0, one launch (start us, length us, event | category | flops | bytes accessed | tf_op | source)
XLA Modules:
  0.0 294.6 jit_solution(12025107248302297864)
XLA Ops:
  6.5 0.0 copy-start
  6.5 2.3 multiply_reduce_fusion
  8.8 0.7 broadcast_in_dim.6
  9.5 7.7 %all-to-all-start = ((f32[8,1,3072]{2,1,0:T(1,128)}), f32[8,1,3072]{2,1,0:T(1,128)S(1)}, u32[]{:S(2)}, u32[]{:S(2)}) async-start(f32[8,1,3072]{2,1,0:T(1,128)} %broadcast_in_dim.6), calls=%async_computation | async-start | bytes 196608 | tf_op jit(solution)/shard_map/all_to_all | solution.py:15
  17.2 0.0 copy-done
  17.2 2.4 copy.43
  19.6 5.4 %all-to-all-done = f32[8,1,3072]{2,1,0:T(1,128)S(1)} async-done(((f32[8,1,3072]{2,1,0:T(1,128)}), f32[8,1,3072]{2,1,0:T(1,128)S(1)}, u32[]{:S(2)}, u32[]{:S(2)}) %all-to-all-start) | async-done | bytes 98336 | tf_op jit(solution)/shard_map/all_to_all | solution.py:15
  25.0 0.1 reduce_sum.19
  25.1 2.4 broadcast_multiply_fusion
  27.5 0.8 broadcast_in_dim.7
  28.3 3.5 %all-to-all-start.3 = ((f32[4,256,96]{1,2,0:T(8,128)}), f32[4,256,96]{1,2,0:T(8,128)S(1)}, u32[]{:S(2)}, u32[]{:S(2)}) async-start(f32[4,256,96]{1,2,0:T(8,128)} %broadcast_in_dim.7), calls=%async_computation.3 | async-start | bytes 786432 | tf_op jit(solution)/shard_map/all_to_all | solution.py:15
  31.8 0.0 all-gather.5.cloned.1.call-start
  31.8 0.7 dynamic-slice_convert_fusion
  32.5 6.7 %all-to-all-done.3 = f32[4,256,96]{1,2,0:T(8,128)S(1)} async-done(((f32[4,256,96]{1,2,0:T(8,128)}), f32[4,256,96]{1,2,0:T(8,128)S(1)}, u32[]{:S(2)}, u32[]{:S(2)}) %all-to-all-start.3) | async-done | bytes 393248 | tf_op jit(solution)/shard_map/all_to_all | solution.py:15
  39.2 0.8 bitcast_multiply_fusion
  40.0 0.0 all-gather.5.cloned.1.call-update
  40.0 0.0 all-gather.3.cloned.1.call-start
  40.0 2.4 copy.44
  42.4 41.8 %all_to_all.46 = f32[4,64,3072]{2,1,0:T(8,128)S(1)} all-to-all(f32[4,64,3072]{2,1,0:T(8,128)} %bitcast.19), channel_id=1, replica_groups=mesh['rows'=8,'ci'=4,'cj'=4] {'cj'}, dimensions={0} | all-to-all | bytes 6291456 | tf_op jit(solution)/shard_map/all_to_all | solution.py:46
  84.2 2.0 copy.45
  86.2 2.4 all_to_all.37
  88.7 3.7 %copy.46 = f32[64,8,1536]{2,0,1:T(8,128)S(1)} copy(f32[64,8,1536]{2,1,0:T(8,128)} %all_to_all.37) | data formatting | bytes 6291456 | tf_op jit(solution)/shard_map/all_to_all | solution.py:47
  92.4 45.7 %all_to_all.47 = f32[64,8,1536]{2,0,1:T(8,128)} all-to-all(f32[64,8,1536]{2,0,1:T(8,128)S(1)} %copy.46), channel_id=1, replica_groups=mesh['rows'=8,'ci'=4,'cj'=4] {'rows'}, dimensions={1} | all-to-all | bytes 6291456 | tf_op jit(solution)/shard_map/all_to_all | solution.py:47
  138.1 0.0 all-gather.3.cloned.1.call-update
  138.2 0.0 all-gather.5.cloned.1.call-done
  138.2 2.4 copy.47
  140.6 1.9 copy.48
  142.4 113.0 %all-gather.3.cloned.1.call-done = f32[2048,1536]{1,0:T(8,128)} async-done(((f32[512,1536]{1,0:T(8,128)}), f32[2048,1536]{1,0:T(8,128)}) %all-gather.3.cloned.1.call-update) | async-done | bytes 12582928 | tf_op jit(solution)/shard_map/all_gather | solution.py:48
  255.4 24.2 %convolution_bitcast_fusion = f32[1,1536,1,384]{3,1,2,0:T(8,128)S(1)} fusion(f32[2048,1536]{1,0:T(8,128)} %all-gather.3.cloned.1.call-done, f32[2048,384]{1,0:T(8,128)} %bitcast.22), kind=kOutput, calls=%fused_computation.1 | convolution fusion | flops 14495514624 | bytes 18087936 | tf_op jit(solution)/shard_map/dot_general | solution.py:57
  279.6 8.2 %copy.49 = f32[1,1536,1,384]{3,2,1,0:T(1,128)} copy(f32[1,1536,1,384]{3,1,2,0:T(8,128)S(1)} %convolution_bitcast_fusion) | data formatting | bytes 4718592 | tf_op jit(solution)/shard_map/broadcast_in_dim | solution.py:63
  (2 shorter events, 0.0 us)
Async XLA Ops:
  6.5 10.7 %copy-start = (f32[256,3072]{1,0:T(8,128)S(1)}, f32[256,3072]{1,0:T(8,128)}, u32[]{:S(2)}) copy-start(f32[256,3072]{1,0:T(8,128)} %param.2) | copy-start | bytes 9437188
  9.5 15.5 %all-to-all-start = ((f32[8,1,3072]{2,1,0:T(1,128)}), f32[8,1,3072]{2,1,0:T(1,128)S(1)}, u32[]{:S(2)}, u32[]{:S(2)}) async-start(f32[8,1,3072]{2,1,0:T(1,128)} %broadcast_in_dim.6), calls=%async_computation | async-start | bytes 196608 | tf_op jit(solution)/shard_map/all_to_all | solution.py:15
  28.3 10.9 %all-to-all-start.3 = ((f32[4,256,96]{1,2,0:T(8,128)}), f32[4,256,96]{1,2,0:T(8,128)S(1)}, u32[]{:S(2)}, u32[]{:S(2)}) async-start(f32[4,256,96]{1,2,0:T(8,128)} %broadcast_in_dim.7), calls=%async_computation.3 | async-start | bytes 786432 | tf_op jit(solution)/shard_map/all_to_all | solution.py:15
  31.8 106.4 %all-gather.5.cloned.1.call-start = ((), (), s32[]{:S(2)}) async-start(), calls=%async_computation.5 | async-start | bytes 3538944 | tf_op jit(solution)/shard_map/all_gather | solution.py:53
  40.0 215.4 %all-gather.3.cloned.1.call-start = ((), (), s32[]{:S(2)}) async-start(), calls=%async_computation.4 | async-start | bytes 15728640 | tf_op jit(solution)/shard_map/all_gather | solution.py:48
Sparse Core Ops, SparseCore 0:
  40.1 75.1 all-gather.4
  138.3 117.0 all-gather.2
where the time goes:
time: 296 us; the launch traced here: 295 us
  waiting for transfers between devices  125 us (42%)
  blocking collectives  87.6 us (30%)
  local copies, waits for them, and re-layouts  26.8 us (9%)
  matrix products  24.2 us (8%)
  between operations  13.5 us (5%)
  starting transfers between devices  11.2 us (4%)
  other arithmetic  6.23 us (2%)
    all_gather x1, waiting for transfers between devices, shards(): columns = lax.all_gather(ranged, 'cj', axis=0, tiled=True)  113 us
    all_to_all x1, blocking collectives, shards(): lax.all_to_all(swapped, 'rows', split_axis=1, concat_axis=0, tiled=True)  45.7 us
    all_to_all x1, blocking collectives, shards(): lax.all_to_all(unit, 'cj', split_axis=0, concat_axis=1, tiled=True)  41.8 us
    dot_general x1, matrix products, shards(): jnp.dot(jnp.transpose(columns), reordered, precision=lax.Precision.HIGHES...  24.2 us
    all_to_all x2, waiting for transfers between devices, from_everyone(): lax.all_to_all(jnp.broadcast_to(shard[None], (length, *shard.shape)), axi...  12.1 us
    all_to_all x2, starting transfers between devices, from_everyone(): lax.all_to_all(jnp.broadcast_to(shard[None], (length, *shard.shape)), axi...  11.2 us
    broadcast_in_dim x1, local copies, waits for them, and re-layouts, shards(): return result[None, :, None, :]  8.16 us
    all_to_all x2, local copies, waits for them, and re-layouts, shards(): lax.all_to_all(swapped, 'rows', split_axis=1, concat_axis=0, tiled=True)  6.15 us
  transfers between devices with their start and end apart: 4, of which 3 were waited for; matrix products, arithmetic and copies ran while one was open for 5% of the time, Pallas kernels for 0%

commit v1 on v0

v1 whole, which is shorter than its diff:
```python
import functools

import jax
import jax.numpy as jnp
from jax import lax
from jax.experimental import pallas as pl
from jax.experimental.pallas import tpu as pltpu
from jax.sharding import Mesh, PartitionSpec as P

EPS = 1e-6
LIFT = 2.0**40
AXES = ("x", "zh", "zl", "core", "y")
SIZES = (4, 2, 2, 2, 4)
ROWS, COLS, HALF, QS, GROUP = 256, 3072, 1536, 96, 384
CHUNK, TILE = 768, 256
F32, BF16 = jnp.float32, jnp.bfloat16


def pair(k, c):
    return k + 1 - 2 * (k % 2) if c == 0 else 3 - k


def mate(k, c):
    return 3 - k if c == 0 else k + 1 - 2 * (k % 2)


def moved(array, to):
    table = []
    for x in range(4):
        for zh in range(2):
            for zl in range(2):
                for c in range(2):
                    for y in range(4):
                        n = [v % s for v, s in zip(to(x, zh, zl, c, y), SIZES)]
                        table.append((x, zh, zl, c, y, n))
    def index(x, zh, zl, c, y):
        return (((x * 2 + zh) * 2 + zl) * 2 + c) * 4 + y
    return lax.ppermute(array, AXES, [(index(*t[:5]), index(*t[5])) for t in table])


def along_z(shift):
    def to(x, zh, zl, c, y):
        z = (zh * 2 + zl + shift) % 4
        return x, z // 2, z % 2, c, y
    return to


def split(v):
    hi = v.astype(BF16)
    return hi, (v - hi.astype(F32)).astype(BF16)


def query_kernel(idx_ref, pieces_ref, sample_ref, hi_ref, lo_ref, squares_ref):
    for g in range(2):
        total = [jnp.zeros((QS, 128), F32) for _ in range(4)]
        for b in range(8):
            half = (b // 2) % 2
            picks = sample_ref[idx_ref[32 + b * 2 + g]][:, half * 128 : half * 128 + 128]
            scale = picks.astype(F32) * LIFT
            for i in range(4):
                piece = pieces_ref[idx_ref[b * 4 + i] + g]
                total[i] = total[i] + piece * piece
                hi, lo = split(piece * scale)
                at = g * GROUP + i * QS
                hi_ref[at : at + QS, b * 128 : b * 128 + 128] = hi
                lo_ref[at : at + QS, b * 128 : b * 128 + 128] = lo
        for i in range(4):
            squares_ref[g, i * QS : i * QS + QS, :] = total[i]


def product_kernel(hi_ref, lo_ref, *refs):
    blocks, (own_ref, other_ref, colhi, collo) = refs[:8], refs[8:]
    squares = jnp.zeros((128, TILE), F32)
    for b, ref in enumerate(blocks):
        v = ref[...]
        squares = squares + v * v
        colhi[b * 128 : b * 128 + 128, :], collo[b * 128 : b * 128 + 128, :] = split(v)
    dot = functools.partial(jnp.dot, preferred_element_type=F32)
    for g, out in ((1, other_ref), (0, own_ref)):
        hi, lo = hi_ref[g * GROUP : (g + 1) * GROUP, :], lo_ref[g * GROUP : (g + 1) * GROUP, :]
        out[:GROUP, :] = dot(hi, colhi[...]) + (dot(hi, collo[...]) + dot(lo, colhi[...]))
        out[GROUP:, :] = jnp.broadcast_to(jnp.sum(squares, axis=0, keepdims=True), (8, TILE))


def final_kernel(own0, got0, own1, got1, sq_own, sq_got, out_ref):
    def write(own, got):
        squares = own[GROUP : GROUP + 1, :] + got[GROUP : GROUP + 1, :]
        inverse = 1.0 / jnp.sqrt(squares + EPS)
        qsquares = jnp.sum(sq_own[...] + sq_got[...], axis=1, keepdims=True)
        qinverse = (2.0 / LIFT) / jnp.sqrt(qsquares + EPS)
        value = (own[:GROUP, :] + got[:GROUP, :]) * qinverse * inverse
        for part in range(TILE // 128):
            for j in range(3):
                block = value[j * 128 : j * 128 + 128, part * 128 : part * 128 + 128]
                out_ref[pl.ds(part * 384 + j, 128, stride=3), :] = block.T

    @pl.when(pl.program_id(0) < CHUNK // TILE)
    def _():
        write(own0, got0)

    @pl.when(pl.program_id(0) >= CHUNK // TILE)
    def _():
        write(own1, got1)


def limit(mib=48):
    return pltpu.CompilerParams(vmem_limit_bytes=mib * 2**20)


def shards(matrix, sample):
    ix, ih, il, ic, iy = (lax.axis_index(a) for a in AXES)
    iz = ih * 2 + il
    my_pair = jnp.where(ic == 0, pair(iy, 0), pair(iy, 1))
    my_mate = jnp.where(ic == 0, mate(iy, 0), mate(iy, 1))

    picks = lax.all_gather(sample[0], ("x", "zh"), axis=0, tiled=False)

    own = lax.dynamic_slice(matrix, (0, ih * HALF), (ROWS, HALF))
    away = lax.dynamic_slice(matrix, (0, (1 - ih) * HALF), (ROWS, HALF))
    flip = lambda x, zh, zl, c, y: (x, 1 - zh, zl, c, y)
    got = [moved(away[:, n * CHUNK : (n + 1) * CHUNK], flip) for n in range(2)]

    def spread(rows):
        result = []
        for n in range(2):
            part = rows[n * 128 : n * 128 + 128]
            part = moved(part, lambda x, zh, zl, c, y: (x, zh, zl, c, y + x + 2 * n))
            result.append(moved(part, lambda x, zh, zl, c, y: (y - x - 2 * n, zh, zl, c, y)))
        return result

    def paired(parts):
        return [moved(p, lambda x, zh, zl, c, y: (x, zh, zl, c, pair(y, c))) for p in parts]

    mine = spread(own)
    mine = mine + paired(mine)
    others = [spread(g) for g in got]
    others = [o + paired(o) for o in others]

    raw = jnp.transpose(matrix[:, :QS])
    raw = jnp.stack(
        [
            raw,
            moved(raw, lambda x, zh, zl, c, y: (x, zh, zl, c, mate(y, 0))),
            moved(raw, lambda x, zh, zl, c, y: (x, zh, zl, c, mate(y, 1))),
        ]
    )
    raw = jnp.stack(
        [raw] + [moved(raw, lambda x, zh, zl, c, y, d=d: (x - d, zh, zl, c, y)) for d in (1, 2, 3)]
    )
    near = (ix + jnp.arange(4)) % 4

    def slot(core):
        p = pair(iy, core)
        first = (near == (iy - ix) % 4) | (near == (p - ix) % 4)
        groups = jnp.stack([raw[:, 0], raw[:, 1 + core]], axis=1)
        return jnp.where(first[:, None, None, None], groups[..., :128], groups[..., 128:])

    slots = slot(0), slot(1)
    keep = jnp.where(ic == 0, slots[0], slots[1])
    give = jnp.where(ic == 0, slots[1], slots[0])
    both = jnp.stack([keep, moved(give, lambda x, zh, zl, c, y: (x, zh, zl, 1 - c, y))])
    pieces = jnp.stack([both] + [moved(both, along_z(-d)) for d in (1, 2, 3)])
    pieces = pieces.reshape(64, QS, 128)

    block_x = jnp.stack([iy - ix, iy - ix + 2, my_pair - ix, my_pair - ix + 2]) % 4
    block_x = jnp.repeat(block_x, 2)
    block_zh = jnp.tile(jnp.stack([ih, 1 - ih]), 4)
    zl = jnp.array([0, 0, 1, 1])[None, :]
    core = jnp.array([0, 1, 0, 1])[None, :]
    dz = (block_zh[:, None] * 2 + zl - iz) % 4
    dx = (block_x[:, None] - ix) % 4
    where = ((dz * 2 + (core ^ ic)) * 4 + dx) * 2
    pick_at = (block_x * 2 + block_zh)[:, None] * 4 + jnp.stack([iy, my_mate])[None, :]
    idx = jnp.concatenate([where.reshape(-1), pick_at.reshape(-1)]).astype(jnp.int32)

    vmem = pl.BlockSpec(memory_space=pltpu.VMEM)
    qhi, qlo, qsquares = pl.pallas_call(
        query_kernel,
        out_shape=(
            jax.ShapeDtypeStruct((2 * GROUP, 1024), BF16),
            jax.ShapeDtypeStruct((2 * GROUP, 1024), BF16),
            jax.ShapeDtypeStruct((2, GROUP, 128), F32),
        ),
        in_specs=[pl.BlockSpec(memory_space=pltpu.SMEM), vmem, vmem],
        out_specs=(vmem, vmem, vmem),
        compiler_params=limit(),
        name="query_prepare",
    )(idx, pieces, picks.reshape(32, 1, ROWS))

    to_mate = lambda x, zh, zl, c, y: (x, zh, zl, c, mate(y, c))
    qsquares_got = moved(qsquares[1], to_mate)

    tiles = CHUNK // TILE
    whole = pl.BlockSpec((2 * GROUP, 1024), lambda t: (0, 0))
    ends = []
    for n in range(2):
        operands, specs = [], []
        for p in range(4):
            operands += [mine[p], others[n][p]]
            specs += [
                pl.BlockSpec((128, TILE), lambda t, n=n: (0, n * tiles + t)),
                pl.BlockSpec((128, TILE), lambda t: (0, t)),
            ]
        ours, theirs = pl.pallas_call(
            product_kernel,
            grid=(tiles,),
            out_shape=(jax.ShapeDtypeStruct((GROUP + 8, CHUNK), F32),) * 2,
            in_specs=[whole, whole] + specs,
            out_specs=(pl.BlockSpec((GROUP + 8, TILE), lambda t: (0, t)),) * 2,
            scratch_shapes=[pltpu.VMEM((1024, TILE), BF16), pltpu.VMEM((1024, TILE), BF16)],
            compiler_params=limit(),
            name="product",
        )(qhi, qlo, *operands)
        ends += [ours, moved(theirs, to_mate)]

    low = pl.BlockSpec((GROUP + 8, TILE), lambda t: (0, jnp.minimum(t, tiles - 1)))
    high = pl.BlockSpec((GROUP + 8, TILE), lambda t: (0, jnp.maximum(t - tiles, 0)))
    flat = pl.BlockSpec((GROUP, 128), lambda t: (0, 0))
    result = pl.pallas_call(
        final_kernel,
        grid=(2 * tiles,),
        out_shape=jax.ShapeDtypeStruct((HALF * 3, 128), F32),
        in_specs=[low, low, high, high, flat, flat],
        out_specs=pl.BlockSpec((TILE * 3, 128), lambda t: (t, 0)),
        compiler_params=limit(),
        name="scale_and_turn",
    )(*ends, qsquares[0], qsquares_got)
    return result.reshape(1, HALF, 1, GROUP)


def solution(mesh):
    fine = Mesh(mesh.devices.reshape(SIZES), AXES)
    rows, ci = ("x", "zh"), ("zl", "core")
    return jax.shard_map(
        shards,
        mesh=fine,
        in_specs=(P(rows, ci + ("y",)), P(ci, None, rows)),
        out_specs=P(ci, rows, "y", None),
        check_vma=False,
    )
```

time: 296 us -> 211 us (0.71)
  waiting for transfers between devices: 125 us -> 47 us
  starting transfers between devices: 11.2 us -> 73.4 us
  blocking collectives: 87.6 us -> 37.2 us
  matrix products: 24.2 us -> 0 us
  Pallas kernels: 0 us -> 21.6 us
  between operations: 13.5 us -> 0.32 us
  local copies, waits for them, and re-layouts: 26.8 us -> 16.1 us
  other arithmetic: 6.23 us -> 14 us
    all_gather x2 -> x0, waiting for transfers between devices: 113 us -> none  [the longest x1 113 us: shards(): columns = lax.all_gather(ranged, 'cj', axis=0, tiled=True)]
    all_to_all x2 -> x0, blocking collectives: 87.6 us -> none  [the longest x1 45.7 us: shards(): lax.all_to_all(swapped, 'rows', split_axis=1, concat_axis=0, tiled=True)]
    ppermute x0 -> x32, starting transfers between devices: none -> 73.4 us  [moved(): lax.ppermute(array, AXES, [(index(*t[:5]), index(*t[5])) for t in table])]
    ppermute x0 -> x32, waiting for transfers between devices: none -> 47 us  [moved(): lax.ppermute(array, AXES, [(index(*t[:5]), index(*t[5])) for t in table])]
    all_gather x0 -> x1, blocking collectives: none -> 37.2 us  [shards(): picks = lax.all_gather(sample[0], ('x', 'zh'), axis=0, tiled=False)]
    dot_general x1 -> x0, matrix products: 24.2 us -> none  [shards(): jnp.dot(jnp.transpose(columns), reordered, precision=lax.Precision.HIGHES...]
    pallas_call x0 -> x4, Pallas kernels: none -> 21.6 us  [the longest x2 14.6 us: shards(): pl.pallas_call(product_kernel, grid=(tiles,), out_shape=(jax.ShapeDtypeSt...]
    all_to_all x2 -> x0, waiting for transfers between devices: 12.1 us -> none  [from_everyone(): lax.all_to_all(jnp.broadcast_to(shard[None], (length, *shard.shape)), axi...]
  transfers between devices with their start and end apart: 4 -> 32, of which waited for: 3 -> 7; matrix products, arithmetic and copies ran while one was open for 5% -> 12% of each run, Pallas kernels for 0% -> 8%
where the time goes in v1:
time: 211 us; the launch traced here: 210 us
  starting transfers between devices  73.4 us (35%)
  waiting for transfers between devices  47 us (22%)
  blocking collectives  37.2 us (18%)
  Pallas kernels  21.6 us (10%)
  local copies, waits for them, and re-layouts  16.1 us (8%)
  other arithmetic  14 us (7%)
    ppermute x32, starting transfers between devices, moved(): lax.ppermute(array, AXES, [(index(*t[:5]), index(*t[5])) for t in table])  73.4 us
    ppermute x32, waiting for transfers between devices, moved(): lax.ppermute(array, AXES, [(index(*t[:5]), index(*t[5])) for t in table])  47 us
    all_gather x1, blocking collectives, shards(): picks = lax.all_gather(sample[0], ('x', 'zh'), axis=0, tiled=False)  37.2 us
    pallas_call x2, Pallas kernels, shards(): pl.pallas_call(product_kernel, grid=(tiles,), out_shape=(jax.ShapeDtypeSt...  14.6 us
    another operation x2, other arithmetic, shards(): pieces = jnp.stack([both] + [moved(both, along_z(-d)) for d in (1, 2, 3)])  4.87 us
  transfers between devices with their start and end apart: 32, of which 7 were waited for; matrix products, arithmetic and copies ran while one was open for 12% of the time, Pallas kernels for 8%

profile of v1, /device:TPU:0, one launch (start us, length us, event | category | flops | bytes accessed | tf_op | source)
XLA Modules:
  0.0 209.7 jit_solution(3417371949337905100)
XLA Ops:
  0.0 0.9 slice.56
  1.0 3.2 %collective-permute-start = (f32[96,256]{1,0:T(8,128)S(1)}, f32[96,256]{1,0:T(8,128)S(1)}, u32[]{:S(2)}, u32[]{:S(2)}) collective-permute-start(f32[96,256]{1,0:T(8,128)S(1)} %bitcast.36), channel_id=1, source_target_pairs={{0,3},{1,2},{2,1},{3,0},{4,7},{5,6},{6,5},{7,4},{8,11},{9,10},{10,... | collective-permute-start | bytes 294920 | tf_op jit(solution)/shard_map/ppermute | solution.py:38
  4.3 2.8 %constant_dynamic-slice_fusion.2 = (f32[256,768]{1,0:T(8,128)}, f32[256,768]{1,0:T(8,128)}) fusion(f32[256,3072]{1,0:T(8,128)} %param.4, s32[]{:T(128)S(6)} %add.180, s32[]{:T(128)S(6)} %select_n.107), kind=kLoop, calls=%fused_computation.33 | loop fusion | bytes 3145736 | tf_op jit(solution)/shard_map/slice | solution.py:121
  7.1 3.9 %collective-permute-start.23 = (f32[256,768]{1,0:T(8,128)}, f32[256,768]{1,0:T(8,128)}, u32[]{:S(2)}, u32[]{:S(2)}) collective-permute-start(f32[256,768]{1,0:T(8,128)} %get-tuple-element.25), channel_id=1, source_target_pairs={{0,16},{1,17},{2,18},{3,19},{4,20},{5,21},{6,22},{7,23},{8,24},{9,... | collective-permute-start | bytes 2359304 | tf_op jit(solution)/shard_map/ppermute | solution.py:38
  11.7 1.7 fusion.8
  13.4 3.0 %collective-permute-start.3 = (f32[3,96,256]{2,1,0:T(8,128)}, f32[3,96,256]{2,1,0:T(8,128)}, u32[]{:S(2)}, u32[]{:S(2)}) collective-permute-start(f32[3,96,256]{2,1,0:T(8,128)} %get-tuple-element.40), channel_id=1, source_target_pairs={{0,64},{1,65},{2,66},{3,67},{4,68},{5,69},{6,70},{7,71},{8,72},{9,... | collective-permute-start | bytes 884744 | tf_op jit(solution)/shard_map/ppermute | solution.py:38
  16.5 1.1 collective-permute-start.2
  17.6 0.9 collective-permute-start.4
  18.7 6.5 %collective-permute-done.3 = f32[3,96,256]{2,1,0:T(8,128)} collective-permute-done((f32[3,96,256]{2,1,0:T(8,128)}, f32[3,96,256]{2,1,0:T(8,128)}, u32[]{:S(2)}, u32[]{:S(2)}) %collective-permute-start.3) | collective-permute-done | bytes 294944 | tf_op jit(solution)/shard_map/ppermute | solution.py:38
  25.2 3.4 %collective-permute-start.14 = (f32[128,1536]{1,0:T(8,128)S(1)}, f32[128,1536]{1,0:T(8,128)S(1)}, u32[]{:S(2)}, u32[]{:S(2)}) collective-permute-start(f32[128,1536]{1,0:T(8,128)S(1)} %get-tuple-element.27), channel_id=1, source_target_pairs={{0,2},{1,3},{2,0},{3,1},{4,6},{5,7},{6,4},{7,5},{8,10},{9,11},{10,... | collective-permute-start | bytes 2359304 | tf_op jit(solution)/shard_map/ppermute | solution.py:38
  28.7 1.1 collective-permute-done.2
  30.5 1.2 pad_maximum_fusion.1
  32.2 1.2 fusion.13
  33.4 3.5 %collective-permute-start.26 = (f32[128,768]{1,0:T(8,128)S(1)}, f32[128,768]{1,0:T(8,128)S(1)}, u32[]{:S(2)}, u32[]{:S(2)}) collective-permute-start(f32[128,768]{1,0:T(8,128)S(1)} %get-tuple-element.31), channel_id=1, source_target_pairs={{0,2},{1,3},{2,0},{3,1},{4,6},{5,7},{6,4},{7,5},{8,10},{9,11},{10,... | collective-permute-start | bytes 1179656 | tf_op jit(solution)/shard_map/ppermute | solution.py:38
  36.8 8.5 %collective-permute-done.11 = f32[256,768]{1,0:T(8,128)} collective-permute-done((f32[256,768]{1,0:T(8,128)}, f32[256,768]{1,0:T(8,128)}, u32[]{:S(2)}, u32[]{:S(2)}) %collective-permute-start.11) | collective-permute-done | bytes 786464 | tf_op jit(solution)/shard_map/ppermute | solution.py:38
  46.0 1.2 fusion.14
  47.2 3.5 %collective-permute-start.16 = (f32[128,768]{1,0:T(8,128)S(1)}, f32[128,768]{1,0:T(8,128)}, u32[]{:S(2)}, u32[]{:S(2)}) collective-permute-start(f32[128,768]{1,0:T(8,128)S(1)} %get-tuple-element.33), channel_id=1, source_target_pairs={{0,2},{1,3},{2,0},{3,1},{4,6},{5,7},{6,4},{7,5},{8,10},{9,11},{10,... | collective-permute-start | bytes 1179656 | tf_op jit(solution)/shard_map/ppermute | solution.py:38
  50.7 1.4 collective-permute-start.12
  52.1 1.1 fusion.9
  53.1 3.2 %collective-permute-start.7 = (f32[2,4,2,96,128]{4,3,2,1,0:T(8,128)S(1)}, f32[2,4,2,96,128]{4,3,2,1,0:T(8,128)}, u32[]{:S(2)}, u32[]{:S(2)}) collective-permute-start(f32[2,4,2,96,128]{4,3,2,1,0:T(8,128)S(1)} %get-tuple-element.36), channel_id=1, source_target_pairs={{0,16},{1,17},{2,18},{3,19},{4,20},{5,21},{6,22},{7,23},{8,24},{9,... | collective-permute-start | bytes 2359304 | tf_op jit(solution)/shard_map/ppermute | solution.py:38
  57.2 1.0 collective-permute-start.6
  60.2 1.0 collective-permute-start.8
  61.3 8.0 %collective-permute-start.15 = (f32[128,1536]{1,0:T(8,128)}, f32[128,1536]{1,0:T(8,128)S(1)}, u32[]{:S(2)}, u32[]{:S(2)}) collective-permute-start(f32[128,1536]{1,0:T(8,128)} %copy-done.11), channel_id=1, source_target_pairs={{0,64},{1,97},{2,2},{3,35},{4,68},{5,101},{6,6},{7,39},{8,72},{9,1... | collective-permute-start | bytes 2359304 | tf_op jit(solution)/shard_map/ppermute | solution.py:38
  69.4 1.8 collective-permute-start.10
  71.9 3.4 %collective-permute-done.7 = f32[2,4,2,96,128]{4,3,2,1,0:T(8,128)} collective-permute-done((f32[2,4,2,96,128]{4,3,2,1,0:T(8,128)S(1)}, f32[2,4,2,96,128]{4,3,2,1,0:T(8,128)}, u32[]{:S(2)}, u32[]{:S(2)}) %collective-permute-start.7) | collective-permute-done | bytes 786464 | tf_op jit(solution)/shard_map/ppermute | solution.py:38
  75.3 8.1 %collective-permute-start.27 = (f32[128,768]{1,0:T(8,128)}, f32[128,768]{1,0:T(8,128)S(1)}, u32[]{:S(2)}, u32[]{:S(2)}) collective-permute-start(f32[128,768]{1,0:T(8,128)} %copy-done.13), channel_id=1, source_target_pairs={{0,64},{1,97},{2,2},{3,35},{4,68},{5,101},{6,6},{7,39},{8,72},{9,1... | collective-permute-start | bytes 1179656 | tf_op jit(solution)/shard_map/ppermute | solution.py:38
  83.4 6.5 %collective-permute-done.6 = f32[2,4,2,96,128]{4,3,2,1,0:T(8,128)S(1)} collective-permute-done((f32[2,4,2,96,128]{4,3,2,1,0:T(8,128)S(1)}, f32[2,4,2,96,128]{4,3,2,1,0:T(8,128)S(1)}, u32[]{:S(2)}, u32[]{:S(2)}) %collective-permute-start.6) | collective-permute-done | bytes 786464 | tf_op jit(solution)/shard_map/ppermute | solution.py:38
  90.0 1.6 collective-permute-start.25
  91.6 1.2 broadcast_xor_fusion
  93.5 7.8 %collective-permute-start.17 = (f32[128,768]{1,0:T(8,128)}, f32[128,768]{1,0:T(8,128)}, u32[]{:S(2)}, u32[]{:S(2)}) collective-permute-start(f32[128,768]{1,0:T(8,128)} %collective-permute-done.16), channel_id=1, source_target_pairs={{0,64},{1,97},{2,2},{3,35},{4,68},{5,101},{6,6},{7,39},{8,72},{9,1... | collective-permute-start | bytes 1179656 | tf_op jit(solution)/shard_map/ppermute | solution.py:38
  101.4 4.5 %collective-permute-start.13 = (f32[128,768]{1,0:T(8,128)}, f32[128,768]{1,0:T(8,128)}, u32[]{:S(2)}, u32[]{:S(2)}) collective-permute-start(f32[128,768]{1,0:T(8,128)} %collective-permute-done.12), channel_id=1, source_target_pairs={{0,0},{1,33},{2,66},{3,99},{4,4},{5,37},{6,70},{7,103},{8,8},{9,41... | collective-permute-start | bytes 1179656 | tf_op jit(solution)/shard_map/ppermute | solution.py:38
  105.9 2.0 collective-permute-start.20
  108.0 1.1 and_select_fusion.1
  113.1 1.9 collective-permute-start.28
  115.4 1.6 collective-permute-start.19
  117.8 37.2 %all_gather.3 = s32[8,4,256]{2,1,0:T(4,128)} all-gather(s32[1,4,256]{2,1,0:T(4,128)S(1)} %copy-done.10), channel_id=1, replica_groups=mesh['x'=4,'zh'=2,'zl'=2,'core'=2,'y'=4] {'x','zh'}, dimensions={0}, use_global_device_ids=true | all-gather | bytes 36864 | tf_op jit(solution)/shard_map/all_gather | solution.py:116
  154.9 1.4 reshape.102.sample_ref
  156.4 3.8 %pad_maximum_fusion = f32[4,2,4,2,96,128]{5,4,3,2,1,0:T(8,128)} fusion(f32[1,2,4,2,96,128]{5,4,3,2,1,0:T(8,128)} %bitcast.34, f32[1,2,4,2,96,128]{5,4,3,2,1,0:T(8,128)} %bitcast.20, f32[1,2,4,2,96,128]{5,4,3,2,1,0:T(8,128)} %bitcast.33, f32[1,2,4,2,96,128]{5,4,3,2,1,0:T(8,128)} %get-tuple-element.35), kind=kLoop, calls=%fused_computation | loop fusion | flops 2359296 | bytes 6291456 | tf_op jit(solution)/shard_map/stack | solution.py:162
  160.2 3.0 %query_prepare.1 = (bf16[768,1024]{1,0:T(8,128)(2,1)S(1)}, bf16[768,1024]{1,0:T(8,128)(2,1)S(1)}, f32[2,384,128]{2,1,0:T(8,128)S(1)}) custom-call(s32[48]{0:T(128)S(1)} %pad_add_fusion.2.idx_ref, f32[64,96,128]{2,1,0:T(8,128)} %bitcast.32, s32[32,1,256]{2,1,0:T(1,128)S(1)} %copy-done.4), custom_call_target="tpu_custom_call" | custom-call | tf_op jit(solution)/shard_map/query_prepare/pallas_call | solution.py:177
  163.3 1.1 copy-done
  164.4 1.2 copy-done.1
  165.6 7.3 %product.3 = (f32[392,768]{1,0:T(8,128)S(1)}, f32[392,768]{1,0:T(8,128)}) custom-call(bf16[768,1024]{1,0:T(8,128)(2,1)} %copy-done, bf16[768,1024]{1,0:T(8,128)(2,1)} %copy-done.1, f32[128,1536]{1,0:T(8,128)S(1)} %collective-permute-done.10.refs_0_, f32[128,768]{1,0:T(8,128)S(1)} %copy-done.3, f32[128,1536]{1,0:T(8,128)S(1)} %collective-permute-done.15.refs_2_, ...), custom_call_target="tpu_custom_call" | custom-call | tf_op jit(solution)/shard_map/product/pallas_call | solution.py:204
  172.9 1.4 collective-permute-start.30
  174.3 7.3 %product.2 = (f32[392,768]{1,0:T(8,128)S(1)}, f32[392,768]{1,0:T(8,128)}) custom-call(bf16[768,1024]{1,0:T(8,128)(2,1)} %copy-done, bf16[768,1024]{1,0:T(8,128)(2,1)} %copy-done.1, f32[128,1536]{1,0:T(8,128)S(1)} %collective-permute-done.10.refs_0_, f32[128,768]{1,0:T(8,128)} %collective-permute-done.13.refs_1_, ...), custom_call_target="tpu_custom_call" | custom-call | tf_op jit(solution)/shard_map/product/pallas_call | solution.py:204
  181.7 1.8 collective-permute-start.22
  183.5 1.5 collective-permute-start.31
  185.0 20.8 %collective-permute-done.31.sq_got = f32[384,128]{1,0:T(8,128)S(1)} collective-permute-done((f32[384,128]{1,0:T(8,128)S(1)}, f32[384,128]{1,0:T(8,128)S(1)}, u32[]{:S(2)}, u32[]{:S(2)}) %collective-permute-start.31) | collective-permute-done | bytes 196640 | tf_op jit(solution)/shard_map/ppermute | solution.py:38
  205.8 3.9 %scale_and_turn.1 = f32[4608,128]{1,0:T(8,128)} custom-call(f32[392,768]{1,0:T(8,128)S(1)} %get-tuple-element.14.own0, f32[392,768]{1,0:T(8,128)S(1)} %collective-permute-done.22.got0, f32[392,768]{1,0:T(8,128)S(1)} %get-tuple-element.16.own1, f32[392,768]{1,0:T(8,128)S(1)} %collective-permute-done.30.got1, f32[384,128]{1,0:T(8,128)S(1)} %get-tuple-element.38.sq_own, ...), custom_call_target="tpu_custom_call" | custom-call | tf_op jit(solution)/shard_map/scale_and_turn/pallas_call | solution.py:219
  (88 shorter events, 12.6 us)
Async XLA Ops:
  1.0 10.0 %collective-permute-start = (f32[96,256]{1,0:T(8,128)S(1)}, f32[96,256]{1,0:T(8,128)S(1)}, u32[]{:S(2)}, u32[]{:S(2)}) collective-permute-start(f32[96,256]{1,0:T(8,128)S(1)} %bitcast.36), channel_id=1, source_target_pairs={{0,3},{1,2},{2,1},{3,0},{4,7},{5,6},{6,5},{7,4},{8,11},{9,10},{10,... | collective-permute-start | bytes 294920 | tf_op jit(solution)/shard_map/ppermute | solution.py:38
  4.2 6.9 %collective-permute-start.1 = (f32[96,256]{1,0:T(8,128)S(1)}, f32[96,256]{1,0:T(8,128)S(1)}, u32[]{:S(2)}, u32[]{:S(2)}) collective-permute-start(f32[96,256]{1,0:T(8,128)S(1)} %bitcast.37), channel_id=1, source_target_pairs={{0,1},{1,0},{2,3},{3,2},{4,5},{5,4},{6,7},{7,6},{8,9},{9,8},{10,11... | collective-permute-start | bytes 294920 | tf_op jit(solution)/shard_map/ppermute | solution.py:38
  4.3 14.2 %copy-start.5 = (f32[256,3072]{1,0:T(8,128)S(1)}, f32[256,3072]{1,0:T(8,128)}, u32[]{:S(2)}) copy-start(f32[256,3072]{1,0:T(8,128)} %param.4) | copy-start | bytes 9437188
  7.1 25.0 %collective-permute-start.23 = (f32[256,768]{1,0:T(8,128)}, f32[256,768]{1,0:T(8,128)}, u32[]{:S(2)}, u32[]{:S(2)}) collective-permute-start(f32[256,768]{1,0:T(8,128)} %get-tuple-element.25), channel_id=1, source_target_pairs={{0,16},{1,17},{2,18},{3,19},{4,20},{5,21},{6,22},{7,23},{8,24},{9,... | collective-permute-start | bytes 2359304 | tf_op jit(solution)/shard_map/ppermute | solution.py:38
  11.0 34.3 %collective-permute-start.11 = (f32[256,768]{1,0:T(8,128)}, f32[256,768]{1,0:T(8,128)}, u32[]{:S(2)}, u32[]{:S(2)}) collective-permute-start(f32[256,768]{1,0:T(8,128)} %get-tuple-element.26), channel_id=1, source_target_pairs={{0,16},{1,17},{2,18},{3,19},{4,20},{5,21},{6,22},{7,23},{8,24},{9,... | collective-permute-start | bytes 2359304 | tf_op jit(solution)/shard_map/ppermute | solution.py:38
  11.0 0.7 copy-start.8
  11.1 0.7 copy-start.9
  13.4 11.8 %collective-permute-start.3 = (f32[3,96,256]{2,1,0:T(8,128)}, f32[3,96,256]{2,1,0:T(8,128)}, u32[]{:S(2)}, u32[]{:S(2)}) collective-permute-start(f32[3,96,256]{2,1,0:T(8,128)} %get-tuple-element.40), channel_id=1, source_target_pairs={{0,64},{1,65},{2,66},{3,67},{4,68},{5,69},{6,70},{7,71},{8,72},{9,... | collective-permute-start | bytes 884744 | tf_op jit(solution)/shard_map/ppermute | solution.py:38
  16.5 13.3 %collective-permute-start.2 = (f32[3,96,256]{2,1,0:T(8,128)}, f32[3,96,256]{2,1,0:T(8,128)}, u32[]{:S(2)}, u32[]{:S(2)}) collective-permute-start(f32[3,96,256]{2,1,0:T(8,128)} %get-tuple-element.40), channel_id=1, source_target_pairs={{0,96},{1,97},{2,98},{3,99},{4,100},{5,101},{6,102},{7,103},{8,104... | collective-permute-start | bytes 884744 | tf_op jit(solution)/shard_map/ppermute | solution.py:38
  17.6 12.9 %collective-permute-start.4 = (f32[3,96,256]{2,1,0:T(8,128)}, f32[3,96,256]{2,1,0:T(8,128)}, u32[]{:S(2)}, u32[]{:S(2)}) collective-permute-start(f32[3,96,256]{2,1,0:T(8,128)} %get-tuple-element.40), channel_id=1, source_target_pairs={{0,32},{1,33},{2,34},{3,35},{4,36},{5,37},{6,38},{7,39},{8,40},{9,... | collective-permute-start | bytes 884744 | tf_op jit(solution)/shard_map/ppermute | solution.py:38
  25.2 25.4 %collective-permute-start.14 = (f32[128,1536]{1,0:T(8,128)S(1)}, f32[128,1536]{1,0:T(8,128)S(1)}, u32[]{:S(2)}, u32[]{:S(2)}) collective-permute-start(f32[128,1536]{1,0:T(8,128)S(1)} %get-tuple-element.27), channel_id=1, source_target_pairs={{0,2},{1,3},{2,0},{3,1},{4,6},{5,7},{6,4},{7,5},{8,10},{9,11},{10,... | collective-permute-start | bytes 2359304 | tf_op jit(solution)/shard_map/ppermute | solution.py:38
  29.8 23.4 %collective-permute-start.9 = (f32[128,1536]{1,0:T(8,128)S(1)}, f32[128,1536]{1,0:T(8,128)S(1)}, u32[]{:S(2)}, u32[]{:S(2)}) collective-permute-start(f32[128,1536]{1,0:T(8,128)S(1)} %get-tuple-element.28), channel_id=1, source_target_pairs={{0,0},{1,1},{2,2},{3,3},{4,4},{5,5},{6,6},{7,7},{8,8},{9,9},{10,10... | collective-permute-start | bytes 2359304 | tf_op jit(solution)/shard_map/ppermute | solution.py:38
  32.1 15.1 %collective-permute-start.5 = (f32[4,2,96,128]{3,2,1,0:T(8,128)S(1)}, f32[4,2,96,128]{3,2,1,0:T(8,128)S(1)}, u32[]{:S(2)}, u32[]{:S(2)}) collective-permute-start(f32[4,2,96,128]{3,2,1,0:T(8,128)S(1)} %broadcast_select_fusion), channel_id=1, source_target_pairs={{0,4},{1,5},{2,6},{3,7},{4,0},{5,1},{6,2},{7,3},{8,12},{9,13},{10,... | collective-permute-start | bytes 1179656 | tf_op jit(solution)/shard_map/ppermute | solution.py:38
  33.4 23.0 %collective-permute-start.26 = (f32[128,768]{1,0:T(8,128)S(1)}, f32[128,768]{1,0:T(8,128)S(1)}, u32[]{:S(2)}, u32[]{:S(2)}) collective-permute-start(f32[128,768]{1,0:T(8,128)S(1)} %get-tuple-element.31), channel_id=1, source_target_pairs={{0,2},{1,3},{2,0},{3,1},{4,6},{5,7},{6,4},{7,5},{8,10},{9,11},{10,... | collective-permute-start | bytes 1179656 | tf_op jit(solution)/shard_map/ppermute | solution.py:38
  45.3 14.9 %collective-permute-start.24 = (f32[128,768]{1,0:T(8,128)S(1)}, f32[128,768]{1,0:T(8,128)S(1)}, u32[]{:S(2)}, u32[]{:S(2)}) collective-permute-start(f32[128,768]{1,0:T(8,128)S(1)} %get-tuple-element.32), channel_id=1, source_target_pairs={{0,0},{1,1},{2,2},{3,3},{4,4},{5,5},{6,6},{7,7},{8,8},{9,9},{10,10... | collective-permute-start | bytes 1179656 | tf_op jit(solution)/shard_map/ppermute | solution.py:38
  47.2 14.2 %collective-permute-start.16 = (f32[128,768]{1,0:T(8,128)S(1)}, f32[128,768]{1,0:T(8,128)}, u32[]{:S(2)}, u32[]{:S(2)}) collective-permute-start(f32[128,768]{1,0:T(8,128)S(1)} %get-tuple-element.33), channel_id=1, source_target_pairs={{0,2},{1,3},{2,0},{3,1},{4,6},{5,7},{6,4},{7,5},{8,10},{9,11},{10,... | collective-permute-start | bytes 1179656 | tf_op jit(solution)/shard_map/ppermute | solution.py:38
  50.6 5.8 %copy-start.11 = (f32[128,1536]{1,0:T(8,128)}, f32[128,1536]{1,0:T(8,128)S(1)}, u32[]{:S(2)}) copy-start(f32[128,1536]{1,0:T(8,128)S(1)} %collective-permute-done.14) | copy-start | bytes 2359300
  50.7 18.7 %collective-permute-start.12 = (f32[128,768]{1,0:T(8,128)S(1)}, f32[128,768]{1,0:T(8,128)}, u32[]{:S(2)}, u32[]{:S(2)}) collective-permute-start(f32[128,768]{1,0:T(8,128)S(1)} %get-tuple-element.34), channel_id=1, source_target_pairs={{0,0},{1,1},{2,2},{3,3},{4,4},{5,5},{6,6},{7,7},{8,8},{9,9},{10,10... | collective-permute-start | bytes 1179656 | tf_op jit(solution)/shard_map/ppermute | solution.py:38
  52.1 65.7 %copy-start.10 = (s32[1,4,256]{2,1,0:T(4,128)S(1)}, s32[1,4,256]{2,1,0:T(4,128)}, u32[]{:S(2)}) copy-start(s32[1,4,256]{2,1,0:T(4,128)} %param.5) | copy-start | bytes 12292
  53.1 3.3 %copy-start.12 = (f32[128,1536]{1,0:T(8,128)}, f32[128,1536]{1,0:T(8,128)S(1)}, u32[]{:S(2)}) copy-start(f32[128,1536]{1,0:T(8,128)S(1)} %collective-permute-done.9) | copy-start | bytes 2359300
  53.1 22.1 %collective-permute-start.7 = (f32[2,4,2,96,128]{4,3,2,1,0:T(8,128)S(1)}, f32[2,4,2,96,128]{4,3,2,1,0:T(8,128)}, u32[]{:S(2)}, u32[]{:S(2)}) collective-permute-start(f32[2,4,2,96,128]{4,3,2,1,0:T(8,128)S(1)} %get-tuple-element.36), channel_id=1, source_target_pairs={{0,16},{1,17},{2,18},{3,19},{4,20},{5,21},{6,22},{7,23},{8,24},{9,... | collective-permute-start | bytes 2359304 | tf_op jit(solution)/shard_map/ppermute | solution.py:38
  56.4 0.8 copy-start.13
  57.2 32.8 %collective-permute-start.6 = (f32[2,4,2,96,128]{4,3,2,1,0:T(8,128)S(1)}, f32[2,4,2,96,128]{4,3,2,1,0:T(8,128)S(1)}, u32[]{:S(2)}, u32[]{:S(2)}) collective-permute-start(f32[2,4,2,96,128]{4,3,2,1,0:T(8,128)S(1)} %get-tuple-element.36), channel_id=1, source_target_pairs={{0,24},{1,25},{2,26},{3,27},{4,28},{5,29},{6,30},{7,31},{8,0},{9,1... | collective-permute-start | bytes 2359304 | tf_op jit(solution)/shard_map/ppermute | solution.py:38
  60.2 1.0 copy-start.14
  60.2 33.3 %collective-permute-start.8 = (f32[2,4,2,96,128]{4,3,2,1,0:T(8,128)S(1)}, f32[2,4,2,96,128]{4,3,2,1,0:T(8,128)S(1)}, u32[]{:S(2)}, u32[]{:S(2)}) collective-permute-start(f32[2,4,2,96,128]{4,3,2,1,0:T(8,128)S(1)} %get-tuple-element.36), channel_id=1, source_target_pairs={{0,8},{1,9},{2,10},{3,11},{4,12},{5,13},{6,14},{7,15},{8,16},{9,17... | collective-permute-start | bytes 2359304 | tf_op jit(solution)/shard_map/ppermute | solution.py:38
  61.3 44.6 %collective-permute-start.15 = (f32[128,1536]{1,0:T(8,128)}, f32[128,1536]{1,0:T(8,128)S(1)}, u32[]{:S(2)}, u32[]{:S(2)}) collective-permute-start(f32[128,1536]{1,0:T(8,128)} %copy-done.11), channel_id=1, source_target_pairs={{0,64},{1,97},{2,2},{3,35},{4,68},{5,101},{6,6},{7,39},{8,72},{9,1... | collective-permute-start | bytes 2359304 | tf_op jit(solution)/shard_map/ppermute | solution.py:38
  69.4 38.6 %collective-permute-start.10 = (f32[128,1536]{1,0:T(8,128)}, f32[128,1536]{1,0:T(8,128)S(1)}, u32[]{:S(2)}, u32[]{:S(2)}) collective-permute-start(f32[128,1536]{1,0:T(8,128)} %copy-done.12), channel_id=1, source_target_pairs={{0,0},{1,33},{2,66},{3,99},{4,4},{5,37},{6,70},{7,103},{8,8},{9,41... | collective-permute-start | bytes 2359304 | tf_op jit(solution)/shard_map/ppermute | solution.py:38
  75.3 26.1 %collective-permute-start.27 = (f32[128,768]{1,0:T(8,128)}, f32[128,768]{1,0:T(8,128)S(1)}, u32[]{:S(2)}, u32[]{:S(2)}) collective-permute-start(f32[128,768]{1,0:T(8,128)} %copy-done.13), channel_id=1, source_target_pairs={{0,64},{1,97},{2,2},{3,35},{4,68},{5,101},{6,6},{7,39},{8,72},{9,1... | collective-permute-start | bytes 1179656 | tf_op jit(solution)/shard_map/ppermute | solution.py:38
  89.9 15.9 %copy-start.6 = (f32[2,4,2,96,128]{4,3,2,1,0:T(8,128)}, f32[2,4,2,96,128]{4,3,2,1,0:T(8,128)S(1)}, u32[]{:S(2)}) copy-start(f32[2,4,2,96,128]{4,3,2,1,0:T(8,128)S(1)} %collective-permute-done.6) | copy-start | bytes 2359300
  90.0 15.9 %collective-permute-start.25 = (f32[128,768]{1,0:T(8,128)}, f32[128,768]{1,0:T(8,128)S(1)}, u32[]{:S(2)}, u32[]{:S(2)}) collective-permute-start(f32[128,768]{1,0:T(8,128)} %copy-done.14), channel_id=1, source_target_pairs={{0,0},{1,33},{2,66},{3,99},{4,4},{5,37},{6,70},{7,103},{8,8},{9,41... | collective-permute-start | bytes 1179656 | tf_op jit(solution)/shard_map/ppermute | solution.py:38
  93.5 14.5 %copy-start.7 = (f32[2,4,2,96,128]{4,3,2,1,0:T(8,128)}, f32[2,4,2,96,128]{4,3,2,1,0:T(8,128)S(1)}, u32[]{:S(2)}) copy-start(f32[2,4,2,96,128]{4,3,2,1,0:T(8,128)S(1)} %collective-permute-done.8) | copy-start | bytes 2359300
  93.5 19.5 %collective-permute-start.17 = (f32[128,768]{1,0:T(8,128)}, f32[128,768]{1,0:T(8,128)}, u32[]{:S(2)}, u32[]{:S(2)}) collective-permute-start(f32[128,768]{1,0:T(8,128)} %collective-permute-done.16), channel_id=1, source_target_pairs={{0,64},{1,97},{2,2},{3,35},{4,68},{5,101},{6,6},{7,39},{8,72},{9,1... | collective-permute-start | bytes 1179656 | tf_op jit(solution)/shard_map/ppermute | solution.py:38
  101.4 13.6 %collective-permute-start.13 = (f32[128,768]{1,0:T(8,128)}, f32[128,768]{1,0:T(8,128)}, u32[]{:S(2)}, u32[]{:S(2)}) collective-permute-start(f32[128,768]{1,0:T(8,128)} %collective-permute-done.12), channel_id=1, source_target_pairs={{0,0},{1,33},{2,66},{3,99},{4,4},{5,37},{6,70},{7,103},{8,8},{9,41... | collective-permute-start | bytes 1179656 | tf_op jit(solution)/shard_map/ppermute | solution.py:38
  105.9 2.0 copy-start.2
  105.9 9.6 %collective-permute-start.29 = (f32[128,768]{1,0:T(8,128)S(1)}, f32[128,768]{1,0:T(8,128)}, u32[]{:S(2)}, u32[]{:S(2)}) collective-permute-start(f32[128,768]{1,0:T(8,128)S(1)} %collective-permute-done.27.refs_3_), channel_id=1, source_target_pairs={{0,1},{1,0},{2,3},{3,2},{4,7},{5,6},{6,5},{7,4},{8,9},{9,8},{10,11... | collective-permute-start | bytes 1179656 | tf_op jit(solution)/shard_map/ppermute | solution.py:38
  105.9 59.7 %collective-permute-start.20 = (f32[128,1536]{1,0:T(8,128)S(1)}, f32[128,1536]{1,0:T(8,128)S(1)}, u32[]{:S(2)}, u32[]{:S(2)}) collective-permute-start(f32[128,1536]{1,0:T(8,128)S(1)} %collective-permute-done.15.refs_2_), channel_id=1, source_target_pairs={{0,1},{1,0},{2,3},{3,2},{4,7},{5,6},{6,5},{7,4},{8,9},{9,8},{10,11... | collective-permute-start | bytes 2359304 | tf_op jit(solution)/shard_map/ppermute | solution.py:38
  107.9 57.7 %collective-permute-start.18 = (f32[128,1536]{1,0:T(8,128)S(1)}, f32[128,1536]{1,0:T(8,128)S(1)}, u32[]{:S(2)}, u32[]{:S(2)}) collective-permute-start(f32[128,1536]{1,0:T(8,128)S(1)} %collective-permute-done.10.refs_0_), channel_id=1, source_target_pairs={{0,1},{1,0},{2,3},{3,2},{4,7},{5,6},{6,5},{7,4},{8,9},{9,8},{10,11... | collective-permute-start | bytes 2359304 | tf_op jit(solution)/shard_map/ppermute | solution.py:38
  113.1 52.5 %collective-permute-start.28 = (f32[128,768]{1,0:T(8,128)}, f32[128,768]{1,0:T(8,128)}, u32[]{:S(2)}, u32[]{:S(2)}) collective-permute-start(f32[128,768]{1,0:T(8,128)} %copy-done.2), channel_id=1, source_target_pairs={{0,1},{1,0},{2,3},{3,2},{4,7},{5,6},{6,5},{7,4},{8,9},{9,8},{10,11... | collective-permute-start | bytes 1179656 | tf_op jit(solution)/shard_map/ppermute | solution.py:38
  115.0 59.3 %collective-permute-start.21 = (f32[128,768]{1,0:T(8,128)}, f32[128,768]{1,0:T(8,128)}, u32[]{:S(2)}, u32[]{:S(2)}) collective-permute-start(f32[128,768]{1,0:T(8,128)} %collective-permute-done.17.refs_3_), channel_id=1, source_target_pairs={{0,1},{1,0},{2,3},{3,2},{4,7},{5,6},{6,5},{7,4},{8,9},{9,8},{10,11... | collective-permute-start | bytes 1179656 | tf_op jit(solution)/shard_map/ppermute | solution.py:38
  115.4 58.9 %collective-permute-start.19 = (f32[128,768]{1,0:T(8,128)}, f32[128,768]{1,0:T(8,128)}, u32[]{:S(2)}, u32[]{:S(2)}) collective-permute-start(f32[128,768]{1,0:T(8,128)} %collective-permute-done.13.refs_1_), channel_id=1, source_target_pairs={{0,1},{1,0},{2,3},{3,2},{4,7},{5,6},{6,5},{7,4},{8,9},{9,8},{10,11... | collective-permute-start | bytes 1179656 | tf_op jit(solution)/shard_map/ppermute | solution.py:38
  156.4 3.8 %copy-start.4 = (s32[32,1,256]{2,1,0:T(1,128)S(1)}, s32[32,1,256]{2,1,0:T(1,128)}, u32[]{:S(2)}) copy-start(s32[32,1,256]{2,1,0:T(1,128)} %reshape.102.sample_ref) | copy-start | bytes 98308
  160.2 5.4 %copy-start.3 = (f32[128,768]{1,0:T(8,128)S(1)}, f32[128,768]{1,0:T(8,128)}, u32[]{:S(2)}) copy-start(f32[128,768]{1,0:T(8,128)} %copy-done.2) | copy-start | bytes 1179652
  163.3 1.1 copy-start
  164.4 1.2 copy-start.1
  172.9 32.9 %collective-permute-start.30 = (f32[392,768]{1,0:T(8,128)}, f32[392,768]{1,0:T(8,128)S(1)}, u32[]{:S(2)}, u32[]{:S(2)}) collective-permute-start(f32[392,768]{1,0:T(8,128)} %get-tuple-element.17), channel_id=1, source_target_pairs={{0,3},{1,2},{2,1},{3,0},{4,5},{5,4},{6,7},{7,6},{8,11},{9,10},{10,... | collective-permute-start | bytes 3612680 | tf_op jit(solution)/shard_map/ppermute | solution.py:38
  181.7 24.1 %collective-permute-start.22 = (f32[392,768]{1,0:T(8,128)}, f32[392,768]{1,0:T(8,128)S(1)}, u32[]{:S(2)}, u32[]{:S(2)}) collective-permute-start(f32[392,768]{1,0:T(8,128)} %get-tuple-element.15), channel_id=1, source_target_pairs={{0,3},{1,2},{2,1},{3,0},{4,5},{5,4},{6,7},{7,6},{8,11},{9,10},{10,... | collective-permute-start | bytes 3612680 | tf_op jit(solution)/shard_map/ppermute | solution.py:38
  183.5 22.3 %collective-permute-start.31 = (f32[384,128]{1,0:T(8,128)S(1)}, f32[384,128]{1,0:T(8,128)S(1)}, u32[]{:S(2)}, u32[]{:S(2)}) collective-permute-start(f32[384,128]{1,0:T(8,128)S(1)} %get-tuple-element.37), channel_id=1, source_target_pairs={{0,3},{1,2},{2,1},{3,0},{4,5},{5,4},{6,7},{7,6},{8,11},{9,10},{10,... | collective-permute-start | bytes 589832 | tf_op jit(solution)/shard_map/ppermute | solution.py:38

commit v2 on v1

--- a/solution.py
+++ b/solution.py
@@ -56,7 +56,7 @@
         for b in range(8):
             half = (b // 2) % 2
             picks = sample_ref[idx_ref[32 + b * 2 + g]][:, half * 128 : half * 128 + 128]
-            scale = picks.astype(F32) * LIFT
+            scale = picks * LIFT
             for i in range(4):
                 piece = pieces_ref[idx_ref[b * 4 + i] + g]
                 total[i] = total[i] + piece * piece
@@ -113,40 +113,43 @@
     my_pair = jnp.where(ic == 0, pair(iy, 0), pair(iy, 1))
     my_mate = jnp.where(ic == 0, mate(iy, 0), mate(iy, 1))
 
-    picks = lax.all_gather(sample[0], ("x", "zh"), axis=0, tiled=False)
-
-    own = lax.dynamic_slice(matrix, (0, ih * HALF), (ROWS, HALF))
-    away = lax.dynamic_slice(matrix, (0, (1 - ih) * HALF), (ROWS, HALF))
-    flip = lambda x, zh, zl, c, y: (x, 1 - zh, zl, c, y)
-    got = [moved(away[:, n * CHUNK : (n + 1) * CHUNK], flip) for n in range(2)]
-
-    def spread(rows):
+    def half_of(side):
+        return lax.dynamic_slice(matrix, (0, side * HALF), (ROWS, HALF))
+
+    def spread(rows, flip):
         result = []
         for n in range(2):
             part = rows[n * 128 : n * 128 + 128]
             part = moved(part, lambda x, zh, zl, c, y: (x, zh, zl, c, y + x + 2 * n))
-            result.append(moved(part, lambda x, zh, zl, c, y: (y - x - 2 * n, zh, zl, c, y)))
+            result.append(
+                moved(part, lambda x, zh, zl, c, y: (y - x - 2 * n, zh + flip, zl, c, y))
+            )
         return result
 
     def paired(parts):
         return [moved(p, lambda x, zh, zl, c, y: (x, zh, zl, c, pair(y, c))) for p in parts]
 
-    mine = spread(own)
+    others = spread(half_of(1 - ih), 1)
+    others = others + paired(others)
+    mine = spread(half_of(ih), 0)
     mine = mine + paired(mine)
-    others = [spread(g) for g in got]
-    others = [o + paired(o) for o in others]
 
     raw = jnp.transpose(matrix[:, :QS])
-    raw = jnp.stack(
+    picks = sample[0].astype(F32)
+    raw = jnp.concatenate(
         [
             raw,
             moved(raw, lambda x, zh, zl, c, y: (x, zh, zl, c, mate(y, 0))),
             moved(raw, lambda x, zh, zl, c, y: (x, zh, zl, c, mate(y, 1))),
+            picks,
+            moved(picks, lambda x, zh, zl, c, y: (x, 1 - zh, zl, c, y)),
         ]
     )
     raw = jnp.stack(
         [raw] + [moved(raw, lambda x, zh, zl, c, y, d=d: (x - d, zh, zl, c, y)) for d in (1, 2, 3)]
     )
+    picks = raw[:, 3 * QS :].reshape(32, 1, ROWS)
+    raw = raw[:, : 3 * QS].reshape(4, 3, QS, ROWS)
     near = (ix + jnp.arange(4)) % 4
 
     def slot(core):
@@ -170,7 +173,7 @@
     dz = (block_zh[:, None] * 2 + zl - iz) % 4
     dx = (block_x[:, None] - ix) % 4
     where = ((dz * 2 + (core ^ ic)) * 4 + dx) * 2
-    pick_at = (block_x * 2 + block_zh)[:, None] * 4 + jnp.stack([iy, my_mate])[None, :]
+    pick_at = (dx * 2 + jnp.arange(8)[:, None] % 2) * 4 + jnp.stack([iy, my_mate])[None, :]
     idx = jnp.concatenate([where.reshape(-1), pick_at.reshape(-1)]).astype(jnp.int32)
 
     vmem = pl.BlockSpec(memory_space=pltpu.VMEM)
@@ -185,7 +188,7 @@
         out_specs=(vmem, vmem, vmem),
         compiler_params=limit(),
         name="query_prepare",
-    )(idx, pieces, picks.reshape(32, 1, ROWS))
+    )(idx, pieces, picks)
 
     to_mate = lambda x, zh, zl, c, y: (x, zh, zl, c, mate(y, c))
     qsquares_got = moved(qsquares[1], to_mate)
@@ -196,11 +199,8 @@
     for n in range(2):
         operands, specs = [], []
         for p in range(4):
-            operands += [mine[p], others[n][p]]
-            specs += [
-                pl.BlockSpec((128, TILE), lambda t, n=n: (0, n * tiles + t)),
-                pl.BlockSpec((128, TILE), lambda t: (0, t)),
-            ]
+            operands += [mine[p], others[p]]
+            specs += [pl.BlockSpec((128, TILE), lambda t, n=n: (0, n * tiles + t))] * 2
         ours, theirs = pl.pallas_call(
             product_kernel,
             grid=(tiles,),

time: 211 us -> 178 us (0.84)
  blocking collectives: 37.2 us -> 0 us
  waiting for transfers between devices: 47 us -> 56 us
  local copies, waits for them, and re-layouts: 16.1 us -> 9.39 us
  starting transfers between devices: 73.4 us -> 79.9 us
  other arithmetic: 14 us -> 9.41 us
    all_gather x1 -> x0, blocking collectives: 37.2 us -> none  [shards(): picks = lax.all_gather(sample[0], ('x', 'zh'), axis=0, tiled=False)]
    ppermute x32 -> x25, waiting for transfers between devices: 47 us -> 56 us  [moved(): lax.ppermute(array, AXES, [(index(*t[:5]), index(*t[5])) for t in table])]
    ppermute x32 -> x25, starting transfers between devices: 73.4 us -> 79.9 us  [moved(): lax.ppermute(array, AXES, [(index(*t[:5]), index(*t[5])) for t in table])]
    another operation x2 -> x1, other arithmetic: 2.94 us -> 0.13 us  [shards(): jnp.stack([raw] + [moved(raw, lambda x, zh, zl, c, y, d=d: (x - d, zh, zl...]
    slice x1, local copies, waits for them, and re-layouts: 2.8 us -> 0.1 us  [shards(): raw = raw[:, :3 * QS].reshape(4, 3, QS, ROWS)]
    add x4, local copies, waits for them, and re-layouts: 2.56 us -> 0.24 us  [shards(): where = ((dz * 2 + (core ^ ic)) * 4 + dx) * 2]
    unnamed x31 -> x21, local copies, waits for them, and re-layouts: 3.86 us -> 4.25 us
  transfers between devices with their start and end apart: 32 -> 25, of which waited for: 7 -> 8; matrix products, arithmetic and copies ran while one was open for 12% -> 8% of each run, Pallas kernels for 8% -> 6%
where the time goes in v2:
time: 178 us; the launch traced here: 177 us
  starting transfers between devices  79.9 us (45%)
  waiting for transfers between devices  56 us (31%)
  Pallas kernels  21.8 us (12%)
  other arithmetic  9.41 us (5%)
  local copies, waits for them, and re-layouts  9.39 us (5%)
    ppermute x25, starting transfers between devices, moved(): lax.ppermute(array, AXES, [(index(*t[:5]), index(*t[5])) for t in table])  79.9 us
    ppermute x25, waiting for transfers between devices, moved(): lax.ppermute(array, AXES, [(index(*t[:5]), index(*t[5])) for t in table])  56 us
    pallas_call x2, Pallas kernels, shards(): pl.pallas_call(product_kernel, grid=(tiles,), out_shape=(jax.ShapeDtypeSt...  14.9 us
    another operation x2, other arithmetic, shards(): pieces = jnp.stack([both] + [moved(both, along_z(-d)) for d in (1, 2, 3)])  6.27 us
    unnamed x21, local copies, waits for them, and re-layouts  4.25 us
    pallas_call x1, Pallas kernels, shards(): pl.pallas_call(final_kernel, grid=(2 * tiles,), out_shape=jax.ShapeDtypeS...  3.86 us
  transfers between devices with their start and end apart: 25, of which 8 were waited for; matrix products, arithmetic and copies ran while one was open for 8% of the time, Pallas kernels for 6%

profile of v2, /device:TPU:0, one launch (start us, length us, event | category | flops | bytes accessed | tf_op | source)
XLA Modules:
  0.0 176.7 jit_solution(16960915623948872344)
XLA Ops:
  0.0 0.9 slice.50
  1.0 1.7 collective-permute-start.1
  2.8 2.2 %collective-permute-start = (f32[96,256]{1,0:T(8,128)S(1)}, f32[96,256]{1,0:T(8,128)S(1)}, u32[]{:S(2)}, u32[]{:S(2)}) collective-permute-start(f32[96,256]{1,0:T(8,128)S(1)} %bitcast.43), channel_id=1, source_target_pairs={{0,3},{1,2},{2,1},{3,0},{4,7},{5,6},{6,5},{7,4},{8,11},{9,10},{10,... | collective-permute-start | bytes 294920 | tf_op jit(solution)/shard_map/ppermute | solution.py:38
  4.9 3.3 %fusion.13 = (f32[128,1536]{1,0:T(8,128)}, f32[128,1536]{1,0:T(8,128)}, f32[128,1536]{1,0:T(8,128)S(1)}, f32[128,1536]{1,0:T(8,128)S(1)}) fusion(f32[256,3072]{1,0:T(8,128)} %param.4, s32[]{:T(128)S(6)} %add.192, s32[]{:T(128)S(6)} %select_n.120, s32[]{:T(128)S(6)} %select_n.119), kind=kLoop, calls=%fused_computation.49 | loop fusion | bytes 6291468 | tf_op jit(solution)/shard_map/slice | solution.py:122
  8.3 2.6 %collective-permute-start.16 = (f32[128,1536]{1,0:T(8,128)}, f32[128,1536]{1,0:T(8,128)}, u32[]{:S(2)}, u32[]{:S(2)}) collective-permute-start(f32[128,1536]{1,0:T(8,128)} %get-tuple-element.23), channel_id=1, source_target_pairs={{0,2},{1,3},{2,0},{3,1},{4,6},{5,7},{6,4},{7,5},{8,10},{9,11},{10,... | collective-permute-start | bytes 2359304 | tf_op jit(solution)/shard_map/ppermute | solution.py:38
  10.9 4.0 %collective-permute-start.2 = (f32[4,256]{1,0:T(4,128)S(1)}, f32[4,256]{1,0:T(4,128)S(1)}, u32[]{:S(2)}, u32[]{:S(2)}) collective-permute-start(f32[4,256]{1,0:T(4,128)S(1)} %convert_bitcast_fusion), channel_id=1, source_target_pairs={{0,16},{1,17},{2,18},{3,19},{4,20},{5,21},{6,22},{7,23},{8,24},{9,... | collective-permute-start | bytes 12296 | tf_op jit(solution)/shard_map/ppermute | solution.py:38
  14.9 1.6 collective-permute-done.2
  16.5 1.9 %collective-permute-start.5 = (f32[296,256]{1,0:T(8,128)S(1)}, f32[296,256]{1,0:T(8,128)S(1)}, u32[]{:S(2)}, u32[]{:S(2)}) collective-permute-start(f32[296,256]{1,0:T(8,128)S(1)} %concatenate.7), channel_id=1, source_target_pairs={{0,32},{1,33},{2,34},{3,35},{4,36},{5,37},{6,38},{7,39},{8,40},{9,... | collective-permute-start | bytes 909320 | tf_op jit(solution)/shard_map/ppermute | solution.py:38
  18.4 6.0 %collective-permute-start.4 = (f32[296,256]{1,0:T(8,128)S(1)}, f32[296,256]{1,0:T(8,128)S(1)}, u32[]{:S(2)}, u32[]{:S(2)}) collective-permute-start(f32[296,256]{1,0:T(8,128)S(1)} %concatenate.7), channel_id=1, source_target_pairs={{0,64},{1,65},{2,66},{3,67},{4,68},{5,69},{6,70},{7,71},{8,72},{9,... | collective-permute-start | bytes 909320 | tf_op jit(solution)/shard_map/ppermute | solution.py:38
  24.4 2.5 %collective-permute-start.3 = (f32[296,256]{1,0:T(8,128)S(1)}, f32[296,256]{1,0:T(8,128)S(1)}, u32[]{:S(2)}, u32[]{:S(2)}) collective-permute-start(f32[296,256]{1,0:T(8,128)S(1)} %concatenate.7), channel_id=1, source_target_pairs={{0,96},{1,97},{2,98},{3,99},{4,100},{5,101},{6,102},{7,103},{8,104... | collective-permute-start | bytes 909320 | tf_op jit(solution)/shard_map/ppermute | solution.py:38
  26.9 7.4 %collective-permute-start.12 = (f32[128,1536]{1,0:T(8,128)}, f32[128,1536]{1,0:T(8,128)}, u32[]{:S(2)}, u32[]{:S(2)}) collective-permute-start(f32[128,1536]{1,0:T(8,128)} %get-tuple-element.24), channel_id=1, source_target_pairs={{0,0},{1,1},{2,2},{3,3},{4,4},{5,5},{6,6},{7,7},{8,8},{9,9},{10,10... | collective-permute-start | bytes 2359304 | tf_op jit(solution)/shard_map/ppermute | solution.py:38
  34.4 1.5 collective-permute-start.10
  35.9 0.6 collective-permute-done.4
  36.5 2.9 %collective-permute-start.14 = (f32[128,1536]{1,0:T(8,128)S(1)}, f32[128,1536]{1,0:T(8,128)}, u32[]{:S(2)}, u32[]{:S(2)}) collective-permute-start(f32[128,1536]{1,0:T(8,128)S(1)} %get-tuple-element.26), channel_id=1, source_target_pairs={{0,2},{1,3},{2,0},{3,1},{4,6},{5,7},{6,4},{7,5},{8,10},{9,11},{10,... | collective-permute-start | bytes 2359304 | tf_op jit(solution)/shard_map/ppermute | solution.py:38
  39.5 0.1 pad_maximum_fusion.1
  39.6 0.6 copy-done.6
  40.2 0.1 slice.65
  40.4 6.1 %collective-permute-start.17 = (f32[128,1536]{1,0:T(8,128)}, f32[128,1536]{1,0:T(8,128)S(1)}, u32[]{:S(2)}, u32[]{:S(2)}) collective-permute-start(f32[128,1536]{1,0:T(8,128)} %collective-permute-done.16), channel_id=1, source_target_pairs={{0,80},{1,113},{2,18},{3,51},{4,84},{5,117},{6,22},{7,55},{8,88},{... | collective-permute-start | bytes 2359304 | tf_op jit(solution)/shard_map/ppermute | solution.py:38
  46.4 0.9 select_bitcast_fusion
  47.3 0.9 broadcast_select_fusion
  48.3 0.3 collective-permute-start.13
  48.6 1.8 %collective-permute-start.11 = (f32[128,1536]{1,0:T(8,128)}, f32[128,1536]{1,0:T(8,128)S(1)}, u32[]{:S(2)}, u32[]{:S(2)}) collective-permute-start(f32[128,1536]{1,0:T(8,128)} %collective-permute-done.10), channel_id=1, source_target_pairs={{0,0},{1,33},{2,66},{3,99},{4,4},{5,37},{6,70},{7,103},{8,8},{9,41... | collective-permute-start | bytes 2359304 | tf_op jit(solution)/shard_map/ppermute | solution.py:38
  50.4 6.9 %collective-permute-done.14 = f32[128,1536]{1,0:T(8,128)} collective-permute-done((f32[128,1536]{1,0:T(8,128)S(1)}, f32[128,1536]{1,0:T(8,128)}, u32[]{:S(2)}, u32[]{:S(2)}) %collective-permute-start.14) | collective-permute-done | bytes 786464 | tf_op jit(solution)/shard_map/ppermute | solution.py:38
  57.2 10.6 %collective-permute-start.15 = (f32[128,1536]{1,0:T(8,128)}, f32[128,1536]{1,0:T(8,128)S(1)}, u32[]{:S(2)}, u32[]{:S(2)}) collective-permute-start(f32[128,1536]{1,0:T(8,128)} %collective-permute-done.14), channel_id=1, source_target_pairs={{0,64},{1,97},{2,2},{3,35},{4,68},{5,101},{6,6},{7,39},{8,72},{9,1... | collective-permute-start | bytes 2359304 | tf_op jit(solution)/shard_map/ppermute | solution.py:38
  67.9 2.5 %fusion.11 = (f32[1,2,4,2,96,128]{5,4,3,2,1,0:T(8,128)}, f32[2,4,2,96,128]{4,3,2,1,0:T(8,128)}) fusion(f32[1,4,2,96,128]{4,3,2,1,0:T(8,128)} %bitcast.16, f32[1,4,2,96,128]{4,3,2,1,0:T(8,128)} %get-tuple-element.19), kind=kLoop, calls=%fused_computation.48 | loop fusion | flops 196608 | bytes 2359296 | tf_op jit(solution)/shard_map/stack | solution.py:165
  70.3 3.2 %collective-permute-start.8 = (f32[2,4,2,96,128]{4,3,2,1,0:T(8,128)}, f32[2,4,2,96,128]{4,3,2,1,0:T(8,128)}, u32[]{:S(2)}, u32[]{:S(2)}) collective-permute-start(f32[2,4,2,96,128]{4,3,2,1,0:T(8,128)} %get-tuple-element.30), channel_id=1, source_target_pairs={{0,16},{1,17},{2,18},{3,19},{4,20},{5,21},{6,22},{7,23},{8,24},{9,... | collective-permute-start | bytes 2359304 | tf_op jit(solution)/shard_map/ppermute | solution.py:38
  73.6 0.7 collective-permute-start.7
  74.9 4.1 %collective-permute-done.13.refs_1_ = f32[128,1536]{1,0:T(8,128)S(1)} collective-permute-done((f32[128,1536]{1,0:T(8,128)}, f32[128,1536]{1,0:T(8,128)S(1)}, u32[]{:S(2)}, u32[]{:S(2)}) %collective-permute-start.13) | collective-permute-done | bytes 786464 | tf_op jit(solution)/shard_map/ppermute | solution.py:38
  79.0 1.1 collective-permute-start.9
  80.3 15.6 %collective-permute-start.21 = (f32[128,1536]{1,0:T(8,128)S(1)}, f32[128,1536]{1,0:T(8,128)}, u32[]{:S(2)}, u32[]{:S(2)}) collective-permute-start(f32[128,1536]{1,0:T(8,128)S(1)} %collective-permute-done.17.refs_3_), channel_id=1, source_target_pairs={{0,1},{1,0},{2,3},{3,2},{4,7},{5,6},{6,5},{7,4},{8,9},{9,8},{10,11... | collective-permute-start | bytes 2359304 | tf_op jit(solution)/shard_map/ppermute | solution.py:38
  95.9 0.1 collective-permute-done.8
  96.0 1.9 %collective-permute-start.18 = (f32[128,1536]{1,0:T(8,128)S(1)}, f32[128,1536]{1,0:T(8,128)}, u32[]{:S(2)}, u32[]{:S(2)}) collective-permute-start(f32[128,1536]{1,0:T(8,128)S(1)} %collective-permute-done.11.refs_0_), channel_id=1, source_target_pairs={{0,1},{1,0},{2,3},{3,2},{4,7},{5,6},{6,5},{7,4},{8,9},{9,8},{10,11... | collective-permute-start | bytes 2359304 | tf_op jit(solution)/shard_map/ppermute | solution.py:38
  97.9 15.0 %collective-permute-done.7 = f32[2,4,2,96,128]{4,3,2,1,0:T(8,128)} collective-permute-done((f32[2,4,2,96,128]{4,3,2,1,0:T(8,128)}, f32[2,4,2,96,128]{4,3,2,1,0:T(8,128)}, u32[]{:S(2)}, u32[]{:S(2)}) %collective-permute-start.7) | collective-permute-done | bytes 786464 | tf_op jit(solution)/shard_map/ppermute | solution.py:38
  112.9 0.3 collective-permute-start.20
  113.6 0.7 pad_maximum_fusion.4
  114.4 3.8 %pad_maximum_fusion = f32[4,2,4,2,96,128]{5,4,3,2,1,0:T(8,128)} fusion(f32[1,2,4,2,96,128]{5,4,3,2,1,0:T(8,128)} %bitcast.20, f32[1,2,4,2,96,128]{5,4,3,2,1,0:T(8,128)} %bitcast.19, f32[1,2,4,2,96,128]{5,4,3,2,1,0:T(8,128)} %bitcast.18, f32[1,2,4,2,96,128]{5,4,3,2,1,0:T(8,128)} %get-tuple-element.29), kind=kLoop, calls=%fused_computation | loop fusion | flops 2359296 | bytes 6291456 | tf_op jit(solution)/shard_map/stack | solution.py:165
  118.2 3.0 %query_prepare.1 = (bf16[768,1024]{1,0:T(8,128)(2,1)S(1)}, bf16[768,1024]{1,0:T(8,128)(2,1)S(1)}, f32[2,384,128]{2,1,0:T(8,128)S(1)}) custom-call(s32[48]{0:T(128)S(1)} %pad_add_fusion.1.idx_ref, f32[64,96,128]{2,1,0:T(8,128)} %bitcast.30, f32[32,1,256]{2,1,0:T(1,128)S(1)} %reshape.113.sample_ref), custom_call_target="tpu_custom_call" | custom-call | tf_op jit(solution)/shard_map/query_prepare/pallas_call | solution.py:180
  121.3 1.1 copy-done
  122.4 1.2 copy-done.1
  123.6 7.6 %collective-permute-done.20.refs_6_ = f32[128,1536]{1,0:T(8,128)} collective-permute-done((f32[128,1536]{1,0:T(8,128)S(1)}, f32[128,1536]{1,0:T(8,128)}, u32[]{:S(2)}, u32[]{:S(2)}) %collective-permute-start.20) | collective-permute-done | bytes 786464 | tf_op jit(solution)/shard_map/ppermute | solution.py:38
  131.2 7.4 %product.3 = (f32[392,768]{1,0:T(8,128)}, f32[392,768]{1,0:T(8,128)}) custom-call(bf16[768,1024]{1,0:T(8,128)(2,1)} %copy-done, bf16[768,1024]{1,0:T(8,128)(2,1)} %copy-done.1, f32[128,1536]{1,0:T(8,128)S(1)} %collective-permute-done.11.refs_0_, f32[128,1536]{1,0:T(8,128)S(1)} %collective-permute-done.13.refs_1_, ...), custom_call_target="tpu_custom_call" | custom-call | tf_op jit(solution)/shard_map/product/pallas_call | solution.py:204
  138.6 2.1 %collective-permute-start.23 = (f32[392,768]{1,0:T(8,128)}, f32[392,768]{1,0:T(8,128)S(1)}, u32[]{:S(2)}, u32[]{:S(2)}) collective-permute-start(f32[392,768]{1,0:T(8,128)} %get-tuple-element.17), channel_id=1, source_target_pairs={{0,3},{1,2},{2,1},{3,0},{4,5},{5,4},{6,7},{7,6},{8,11},{9,10},{10,... | collective-permute-start | bytes 3612680 | tf_op jit(solution)/shard_map/ppermute | solution.py:38
  140.7 7.5 %product.2 = (f32[392,768]{1,0:T(8,128)}, f32[392,768]{1,0:T(8,128)}) custom-call(bf16[768,1024]{1,0:T(8,128)(2,1)} %copy-done, bf16[768,1024]{1,0:T(8,128)(2,1)} %copy-done.1, f32[128,1536]{1,0:T(8,128)S(1)} %collective-permute-done.11.refs_0_, f32[128,1536]{1,0:T(8,128)S(1)} %collective-permute-done.13.refs_1_, ...), custom_call_target="tpu_custom_call" | custom-call | tf_op jit(solution)/shard_map/product/pallas_call | solution.py:204
  148.3 1.1 collective-permute-start.22
  149.4 2.2 %collective-permute-start.24 = (f32[384,128]{1,0:T(8,128)S(1)}, f32[384,128]{1,0:T(8,128)S(1)}, u32[]{:S(2)}, u32[]{:S(2)}) collective-permute-start(f32[384,128]{1,0:T(8,128)S(1)} %get-tuple-element.31), channel_id=1, source_target_pairs={{0,3},{1,2},{2,1},{3,0},{4,5},{5,4},{6,7},{7,6},{8,11},{9,10},{10,... | collective-permute-start | bytes 589832 | tf_op jit(solution)/shard_map/ppermute | solution.py:38
  151.6 19.9 %collective-permute-done.24.sq_got = f32[384,128]{1,0:T(8,128)S(1)} collective-permute-done((f32[384,128]{1,0:T(8,128)S(1)}, f32[384,128]{1,0:T(8,128)S(1)}, u32[]{:S(2)}, u32[]{:S(2)}) %collective-permute-start.24) | collective-permute-done | bytes 196640 | tf_op jit(solution)/shard_map/ppermute | solution.py:38
  171.6 1.3 copy-done.3
  172.8 3.9 %scale_and_turn.1 = f32[4608,128]{1,0:T(8,128)} custom-call(f32[392,768]{1,0:T(8,128)S(1)} %copy-done.3, f32[392,768]{1,0:T(8,128)S(1)} %collective-permute-done.22.got0, f32[392,768]{1,0:T(8,128)S(1)} %copy-done.2, f32[392,768]{1,0:T(8,128)S(1)} %collective-permute-done.23.got1, f32[384,128]{1,0:T(8,128)S(1)} %get-tuple-element.32.sq_own, ...), custom_call_target="tpu_custom_call" | custom-call | tf_op jit(solution)/shard_map/scale_and_turn/pallas_call | solution.py:219
  (61 shorter events, 1.5 us)
Async XLA Ops:
  1.0 15.4 %collective-permute-start.1 = (f32[96,256]{1,0:T(8,128)S(1)}, f32[96,256]{1,0:T(8,128)S(1)}, u32[]{:S(2)}, u32[]{:S(2)}) collective-permute-start(f32[96,256]{1,0:T(8,128)S(1)} %bitcast.42), channel_id=1, source_target_pairs={{0,1},{1,0},{2,3},{3,2},{4,5},{5,4},{6,7},{7,6},{8,9},{9,8},{10,11... | collective-permute-start | bytes 294920 | tf_op jit(solution)/shard_map/ppermute | solution.py:38
  2.8 13.7 %collective-permute-start = (f32[96,256]{1,0:T(8,128)S(1)}, f32[96,256]{1,0:T(8,128)S(1)}, u32[]{:S(2)}, u32[]{:S(2)}) collective-permute-start(f32[96,256]{1,0:T(8,128)S(1)} %bitcast.43), channel_id=1, source_target_pairs={{0,3},{1,2},{2,1},{3,0},{4,7},{5,6},{6,5},{7,4},{8,11},{9,10},{10,... | collective-permute-start | bytes 294920 | tf_op jit(solution)/shard_map/ppermute | solution.py:38
  4.9 6.0 %copy-start.7 = (s32[1,4,256]{2,1,0:T(4,128)S(1)}, s32[1,4,256]{2,1,0:T(4,128)}, u32[]{:S(2)}) copy-start(s32[1,4,256]{2,1,0:T(4,128)} %param.5) | copy-start | bytes 12292
  8.3 32.1 %collective-permute-start.16 = (f32[128,1536]{1,0:T(8,128)}, f32[128,1536]{1,0:T(8,128)}, u32[]{:S(2)}, u32[]{:S(2)}) collective-permute-start(f32[128,1536]{1,0:T(8,128)} %get-tuple-element.23), channel_id=1, source_target_pairs={{0,2},{1,3},{2,0},{3,1},{4,6},{5,7},{6,4},{7,5},{8,10},{9,11},{10,... | collective-permute-start | bytes 2359304 | tf_op jit(solution)/shard_map/ppermute | solution.py:38
  10.9 5.5 %collective-permute-start.2 = (f32[4,256]{1,0:T(4,128)S(1)}, f32[4,256]{1,0:T(4,128)S(1)}, u32[]{:S(2)}, u32[]{:S(2)}) collective-permute-start(f32[4,256]{1,0:T(4,128)S(1)} %convert_bitcast_fusion), channel_id=1, source_target_pairs={{0,16},{1,17},{2,18},{3,19},{4,20},{5,21},{6,22},{7,23},{8,24},{9,... | collective-permute-start | bytes 12296 | tf_op jit(solution)/shard_map/ppermute | solution.py:38
  16.5 17.9 %collective-permute-start.5 = (f32[296,256]{1,0:T(8,128)S(1)}, f32[296,256]{1,0:T(8,128)S(1)}, u32[]{:S(2)}, u32[]{:S(2)}) collective-permute-start(f32[296,256]{1,0:T(8,128)S(1)} %concatenate.7), channel_id=1, source_target_pairs={{0,32},{1,33},{2,34},{3,35},{4,36},{5,37},{6,38},{7,39},{8,40},{9,... | collective-permute-start | bytes 909320 | tf_op jit(solution)/shard_map/ppermute | solution.py:38
  18.4 18.2 %collective-permute-start.4 = (f32[296,256]{1,0:T(8,128)S(1)}, f32[296,256]{1,0:T(8,128)S(1)}, u32[]{:S(2)}, u32[]{:S(2)}) collective-permute-start(f32[296,256]{1,0:T(8,128)S(1)} %concatenate.7), channel_id=1, source_target_pairs={{0,64},{1,65},{2,66},{3,67},{4,68},{5,69},{6,70},{7,71},{8,72},{9,... | collective-permute-start | bytes 909320 | tf_op jit(solution)/shard_map/ppermute | solution.py:38
  24.4 15.1 %collective-permute-start.3 = (f32[296,256]{1,0:T(8,128)S(1)}, f32[296,256]{1,0:T(8,128)S(1)}, u32[]{:S(2)}, u32[]{:S(2)}) collective-permute-start(f32[296,256]{1,0:T(8,128)S(1)} %concatenate.7), channel_id=1, source_target_pairs={{0,96},{1,97},{2,98},{3,99},{4,100},{5,101},{6,102},{7,103},{8,104... | collective-permute-start | bytes 909320 | tf_op jit(solution)/shard_map/ppermute | solution.py:38
  26.9 21.4 %collective-permute-start.12 = (f32[128,1536]{1,0:T(8,128)}, f32[128,1536]{1,0:T(8,128)}, u32[]{:S(2)}, u32[]{:S(2)}) collective-permute-start(f32[128,1536]{1,0:T(8,128)} %get-tuple-element.24), channel_id=1, source_target_pairs={{0,0},{1,1},{2,2},{3,3},{4,4},{5,5},{6,6},{7,7},{8,8},{9,9},{10,10... | collective-permute-start | bytes 2359304 | tf_op jit(solution)/shard_map/ppermute | solution.py:38
  34.4 5.2 %copy-start.4 = (f32[296,256]{1,0:T(8,128)}, f32[296,256]{1,0:T(8,128)S(1)}, u32[]{:S(2)}) copy-start(f32[296,256]{1,0:T(8,128)S(1)} %collective-permute-done.5) | copy-start | bytes 909316
  34.4 14.2 %collective-permute-start.10 = (f32[128,1536]{1,0:T(8,128)S(1)}, f32[128,1536]{1,0:T(8,128)}, u32[]{:S(2)}, u32[]{:S(2)}) collective-permute-start(f32[128,1536]{1,0:T(8,128)S(1)} %get-tuple-element.25), channel_id=1, source_target_pairs={{0,0},{1,1},{2,2},{3,3},{4,4},{5,5},{6,6},{7,7},{8,8},{9,9},{10,10... | collective-permute-start | bytes 2359304 | tf_op jit(solution)/shard_map/ppermute | solution.py:38
  36.5 3.1 %copy-start.5 = (f32[296,256]{1,0:T(8,128)}, f32[296,256]{1,0:T(8,128)S(1)}, u32[]{:S(2)}) copy-start(f32[296,256]{1,0:T(8,128)S(1)} %collective-permute-done.4) | copy-start | bytes 909316
  36.5 20.7 %collective-permute-start.14 = (f32[128,1536]{1,0:T(8,128)S(1)}, f32[128,1536]{1,0:T(8,128)}, u32[]{:S(2)}, u32[]{:S(2)}) collective-permute-start(f32[128,1536]{1,0:T(8,128)S(1)} %get-tuple-element.26), channel_id=1, source_target_pairs={{0,2},{1,3},{2,0},{3,1},{4,6},{5,7},{6,4},{7,5},{8,10},{9,11},{10,... | collective-permute-start | bytes 2359304 | tf_op jit(solution)/shard_map/ppermute | solution.py:38
  39.5 0.7 copy-start.6
  40.4 33.2 %collective-permute-start.17 = (f32[128,1536]{1,0:T(8,128)}, f32[128,1536]{1,0:T(8,128)S(1)}, u32[]{:S(2)}, u32[]{:S(2)}) collective-permute-start(f32[128,1536]{1,0:T(8,128)} %collective-permute-done.16), channel_id=1, source_target_pairs={{0,80},{1,113},{2,18},{3,51},{4,84},{5,117},{6,22},{7,55},{8,88},{... | collective-permute-start | bytes 2359304 | tf_op jit(solution)/shard_map/ppermute | solution.py:38
  48.2 19.7 %collective-permute-start.6 = (f32[4,2,96,128]{3,2,1,0:T(8,128)}, f32[4,2,96,128]{3,2,1,0:T(8,128)}, u32[]{:S(2)}, u32[]{:S(2)}) collective-permute-start(f32[4,2,96,128]{3,2,1,0:T(8,128)} %broadcast_select_fusion), channel_id=1, source_target_pairs={{0,4},{1,5},{2,6},{3,7},{4,0},{5,1},{6,2},{7,3},{8,12},{9,13},{10,... | collective-permute-start | bytes 1179656 | tf_op jit(solution)/shard_map/ppermute | solution.py:38
  48.2 31.9 %copy-start.8 = (s32[4]{0:T(128)S(1)}, s32[4]{0:T(128)}, u32[]{:S(2)}) copy-start(s32[4]{0:T(128)} %constant.107.clone) | copy-start | bytes 52
  48.3 30.7 %collective-permute-start.13 = (f32[128,1536]{1,0:T(8,128)}, f32[128,1536]{1,0:T(8,128)S(1)}, u32[]{:S(2)}, u32[]{:S(2)}) collective-permute-start(f32[128,1536]{1,0:T(8,128)} %collective-permute-done.12), channel_id=1, source_target_pairs={{0,16},{1,49},{2,82},{3,115},{4,20},{5,53},{6,86},{7,119},{8,24},{... | collective-permute-start | bytes 2359304 | tf_op jit(solution)/shard_map/ppermute | solution.py:38
  48.6 31.7 %collective-permute-start.11 = (f32[128,1536]{1,0:T(8,128)}, f32[128,1536]{1,0:T(8,128)S(1)}, u32[]{:S(2)}, u32[]{:S(2)}) collective-permute-start(f32[128,1536]{1,0:T(8,128)} %collective-permute-done.10), channel_id=1, source_target_pairs={{0,0},{1,33},{2,66},{3,99},{4,4},{5,37},{6,70},{7,103},{8,8},{9,41... | collective-permute-start | bytes 2359304 | tf_op jit(solution)/shard_map/ppermute | solution.py:38
  57.2 38.6 %collective-permute-start.15 = (f32[128,1536]{1,0:T(8,128)}, f32[128,1536]{1,0:T(8,128)S(1)}, u32[]{:S(2)}, u32[]{:S(2)}) collective-permute-start(f32[128,1536]{1,0:T(8,128)} %collective-permute-done.14), channel_id=1, source_target_pairs={{0,64},{1,97},{2,2},{3,35},{4,68},{5,101},{6,6},{7,39},{8,72},{9,1... | collective-permute-start | bytes 2359304 | tf_op jit(solution)/shard_map/ppermute | solution.py:38
  67.9 45.4 %copy-start.9 = (s32[4]{0:T(128)S(1)}, s32[4]{0:T(128)}, u32[]{:S(2)}) copy-start(s32[4]{0:T(128)} %constant.108.clone) | copy-start | bytes 52
  70.3 25.7 %collective-permute-start.8 = (f32[2,4,2,96,128]{4,3,2,1,0:T(8,128)}, f32[2,4,2,96,128]{4,3,2,1,0:T(8,128)}, u32[]{:S(2)}, u32[]{:S(2)}) collective-permute-start(f32[2,4,2,96,128]{4,3,2,1,0:T(8,128)} %get-tuple-element.30), channel_id=1, source_target_pairs={{0,16},{1,17},{2,18},{3,19},{4,20},{5,21},{6,22},{7,23},{8,24},{9,... | collective-permute-start | bytes 2359304 | tf_op jit(solution)/shard_map/ppermute | solution.py:38
  73.6 39.3 %collective-permute-start.7 = (f32[2,4,2,96,128]{4,3,2,1,0:T(8,128)}, f32[2,4,2,96,128]{4,3,2,1,0:T(8,128)}, u32[]{:S(2)}, u32[]{:S(2)}) collective-permute-start(f32[2,4,2,96,128]{4,3,2,1,0:T(8,128)} %get-tuple-element.30), channel_id=1, source_target_pairs={{0,24},{1,25},{2,26},{3,27},{4,28},{5,29},{6,30},{7,31},{8,0},{9,1... | collective-permute-start | bytes 2359304 | tf_op jit(solution)/shard_map/ppermute | solution.py:38
  79.0 35.4 %collective-permute-start.9 = (f32[2,4,2,96,128]{4,3,2,1,0:T(8,128)}, f32[2,4,2,96,128]{4,3,2,1,0:T(8,128)}, u32[]{:S(2)}, u32[]{:S(2)}) collective-permute-start(f32[2,4,2,96,128]{4,3,2,1,0:T(8,128)} %get-tuple-element.30), channel_id=1, source_target_pairs={{0,8},{1,9},{2,10},{3,11},{4,12},{5,13},{6,14},{7,15},{8,16},{9,17... | collective-permute-start | bytes 2359304 | tf_op jit(solution)/shard_map/ppermute | solution.py:38
  80.3 43.3 %collective-permute-start.21 = (f32[128,1536]{1,0:T(8,128)S(1)}, f32[128,1536]{1,0:T(8,128)}, u32[]{:S(2)}, u32[]{:S(2)}) collective-permute-start(f32[128,1536]{1,0:T(8,128)S(1)} %collective-permute-done.17.refs_3_), channel_id=1, source_target_pairs={{0,1},{1,0},{2,3},{3,2},{4,7},{5,6},{6,5},{7,4},{8,9},{9,8},{10,11... | collective-permute-start | bytes 2359304 | tf_op jit(solution)/shard_map/ppermute | solution.py:38
  95.9 27.7 %collective-permute-start.19 = (f32[128,1536]{1,0:T(8,128)S(1)}, f32[128,1536]{1,0:T(8,128)}, u32[]{:S(2)}, u32[]{:S(2)}) collective-permute-start(f32[128,1536]{1,0:T(8,128)S(1)} %collective-permute-done.13.refs_1_), channel_id=1, source_target_pairs={{0,1},{1,0},{2,3},{3,2},{4,7},{5,6},{6,5},{7,4},{8,9},{9,8},{10,11... | collective-permute-start | bytes 2359304 | tf_op jit(solution)/shard_map/ppermute | solution.py:38
  96.0 27.6 %collective-permute-start.18 = (f32[128,1536]{1,0:T(8,128)S(1)}, f32[128,1536]{1,0:T(8,128)}, u32[]{:S(2)}, u32[]{:S(2)}) collective-permute-start(f32[128,1536]{1,0:T(8,128)S(1)} %collective-permute-done.11.refs_0_), channel_id=1, source_target_pairs={{0,1},{1,0},{2,3},{3,2},{4,7},{5,6},{6,5},{7,4},{8,9},{9,8},{10,11... | collective-permute-start | bytes 2359304 | tf_op jit(solution)/shard_map/ppermute | solution.py:38
  112.9 18.3 %collective-permute-start.20 = (f32[128,1536]{1,0:T(8,128)S(1)}, f32[128,1536]{1,0:T(8,128)}, u32[]{:S(2)}, u32[]{:S(2)}) collective-permute-start(f32[128,1536]{1,0:T(8,128)S(1)} %collective-permute-done.15.refs_2_), channel_id=1, source_target_pairs={{0,1},{1,0},{2,3},{3,2},{4,7},{5,6},{6,5},{7,4},{8,9},{9,8},{10,11... | collective-permute-start | bytes 2359304 | tf_op jit(solution)/shard_map/ppermute | solution.py:38
  121.3 1.1 copy-start
  122.4 1.2 copy-start.1
  138.6 32.9 %collective-permute-start.23 = (f32[392,768]{1,0:T(8,128)}, f32[392,768]{1,0:T(8,128)S(1)}, u32[]{:S(2)}, u32[]{:S(2)}) collective-permute-start(f32[392,768]{1,0:T(8,128)} %get-tuple-element.17), channel_id=1, source_target_pairs={{0,3},{1,2},{2,1},{3,0},{4,5},{5,4},{6,7},{7,6},{8,11},{9,10},{10,... | collective-permute-start | bytes 3612680 | tf_op jit(solution)/shard_map/ppermute | solution.py:38
  140.7 30.8 %copy-start.2 = (f32[392,768]{1,0:T(8,128)S(1)}, f32[392,768]{1,0:T(8,128)}, u32[]{:S(2)}) copy-start(f32[392,768]{1,0:T(8,128)} %get-tuple-element.16.own1) | copy-start | bytes 3612676
  148.3 23.3 %collective-permute-start.22 = (f32[392,768]{1,0:T(8,128)}, f32[392,768]{1,0:T(8,128)S(1)}, u32[]{:S(2)}, u32[]{:S(2)}) collective-permute-start(f32[392,768]{1,0:T(8,128)} %get-tuple-element.15), channel_id=1, source_target_pairs={{0,3},{1,2},{2,1},{3,0},{4,5},{5,4},{6,7},{7,6},{8,11},{9,10},{10,... | collective-permute-start | bytes 3612680 | tf_op jit(solution)/shard_map/ppermute | solution.py:38
  149.4 22.1 %collective-permute-start.24 = (f32[384,128]{1,0:T(8,128)S(1)}, f32[384,128]{1,0:T(8,128)S(1)}, u32[]{:S(2)}, u32[]{:S(2)}) collective-permute-start(f32[384,128]{1,0:T(8,128)S(1)} %get-tuple-element.31), channel_id=1, source_target_pairs={{0,3},{1,2},{2,1},{3,0},{4,5},{5,4},{6,7},{7,6},{8,11},{9,10},{10,... | collective-permute-start | bytes 589832 | tf_op jit(solution)/shard_map/ppermute | solution.py:38
  171.6 1.3 copy-start.3

commit v3 on v2

v3 whole, which is shorter than its diff:
```python
import functools

import jax
import jax.numpy as jnp
from jax import lax
from jax.experimental import pallas as pl
from jax.experimental.pallas import tpu as pltpu
from jax.sharding import Mesh, PartitionSpec as P

EPS = 1e-6
LIFT = 2.0**40
AXES = ("x", "zh", "zl", "core", "y")
SIZES = (4, 2, 2, 2, 4)
ROWS, COLS, HALF, QS, GROUP = 256, 3072, 1536, 96, 384
CHUNK, TILE = 768, 256
F32, BF16 = jnp.float32, jnp.bfloat16


def pair(k, c):
    return k + 1 - 2 * (k % 2) if c == 0 else 3 - k


def mate(k, c):
    return 3 - k if c == 0 else k + 1 - 2 * (k % 2)


def moved(array, to):
    table = []
    for x in range(4):
        for zh in range(2):
            for zl in range(2):
                for c in range(2):
                    for y in range(4):
                        n = [v % s for v, s in zip(to(x, zh, zl, c, y), SIZES)]
                        table.append((x, zh, zl, c, y, n))
    def index(x, zh, zl, c, y):
        return (((x * 2 + zh) * 2 + zl) * 2 + c) * 4 + y
    return lax.ppermute(array, AXES, [(index(*t[:5]), index(*t[5])) for t in table])


def split(v):
    hi = v.astype(BF16)
    return hi, (v - hi.astype(F32)).astype(BF16)


def query_kernel(at_ref, pieces_ref, hilo_ref, norms_ref, squares_ref):
    total = [[jnp.zeros((QS, 128), F32) for _ in range(4)] for _ in range(2)]
    for b in range(8):
        x, zh = at_ref[b], at_ref[8 + b]
        for g in range(2):
            row = pl.multiple_of(8 * QS + (x * 4 + at_ref[16 + g]) * 8, 8)
            picks = pieces_ref[zh * 4 + at_ref[18], pl.ds(row, 8), :]
            picks = picks[b % 2 : b % 2 + 1, :] * LIFT
            for i in range(4):
                row = pl.multiple_of((x * 2 + g) * QS, 8)
                piece = pieces_ref[zh * 4 + i, pl.ds(row, QS), :]
                total[g][i] = total[g][i] + piece * piece
                hi, lo = split(piece * picks)
                to = g * GROUP + i * QS
                hilo_ref[to : to + QS, b * 128 : b * 128 + 128] = hi
                to += 2 * GROUP
                hilo_ref[to : to + QS, b * 128 : b * 128 + 128] = lo
    norms_ref[...] = jnp.zeros_like(norms_ref)
    for g in range(2):
        for i in range(4):
            squares_ref[i * QS : i * QS + QS, :] = total[g][i]
        for j in range(3):
            part = squares_ref[j * 128 : j * 128 + 128, :].T
            norms_ref[g, j + 1 : j + 2, :] = jnp.sum(part, axis=0, keepdims=True)


def products(hilo_ref, blocks, colhi, collo):
    squares = jnp.zeros((128, TILE), F32)
    for b, ref in enumerate(blocks):
        v = ref[...]
        squares = squares + v * v
        colhi[b * 128 : b * 128 + 128, :], collo[b * 128 : b * 128 + 128, :] = split(v)
    dot = functools.partial(jnp.dot, preferred_element_type=F32)
    both = dot(hilo_ref[...], colhi[...])
    value = both[: 2 * GROUP, :] + (both[2 * GROUP :, :] + dot(hilo_ref[: 2 * GROUP, :], collo[...]))
    return value, jnp.sum(squares, axis=0, keepdims=True)


def first_kernel(hilo_ref, *refs):
    blocks, (out_ref, colhi, collo) = refs[:4], refs[4:]
    value, squares = products(hilo_ref, blocks, colhi, collo)
    out_ref[: 2 * GROUP, :] = value
    out_ref[2 * GROUP :, :] = jnp.broadcast_to(squares, (8, TILE))


def second_kernel(hilo_ref, norms_ref, before_ref, *refs):
    blocks, (own_ref, other_ref, colhi, collo) = refs[:4], refs[4:]
    value, squares = products(hilo_ref, blocks, colhi, collo)
    squares = before_ref[2 * GROUP :, :] + squares
    row = lax.broadcasted_iota(jnp.int32, (8, TILE), 0)
    for g, out in ((0, own_ref), (1, other_ref)):
        here = slice(g * GROUP, (g + 1) * GROUP)
        out[:GROUP, :] = before_ref[here, :] + value[here, :]
        norms = jnp.concatenate([norms_ref[g]] * (TILE // 128), axis=1)
        out[GROUP:, :] = jnp.where(row == 0, squares, norms)


def final_kernel(own, got, *refs):
    out_ref = refs[-1]
    squares = own[GROUP:, :] + got[GROUP:, :]
    inverse = 1.0 / jnp.sqrt(squares[:1, :] + EPS)
    value = (own[:GROUP, :] + got[:GROUP, :]) * inverse
    for j in range(3):
        scale = (2.0 / LIFT) / jnp.sqrt(squares[j + 1 : j + 2, :128] + EPS)
        for part in range(TILE // 128):
            block = value[j * 128 : j * 128 + 128, part * 128 : part * 128 + 128]
            out_ref[pl.ds(part * 384 + j, 128, stride=3), :] = block.T * scale


def limit(mib=48):
    return pltpu.CompilerParams(vmem_limit_bytes=mib * 2**20)


def shards(matrix, sample):
    ix, ih, il, ic, iy = (lax.axis_index(a) for a in AXES)
    my_pair = jnp.where(ic == 0, pair(iy, 0), pair(iy, 1))
    my_mate = jnp.where(ic == 0, mate(iy, 0), mate(iy, 1))

    def half_of(side):
        return lax.dynamic_slice(matrix, (0, side * HALF), (ROWS, HALF))

    def first_step(part, n):
        return moved(part, lambda x, zh, zl, c, y: (x, zh, zl, c, y + x + 2 * n))

    def second_step(part, n):
        return moved(part, lambda x, zh, zl, c, y: (y - x - 2 * n, zh, zl, c, y))

    def paired(parts):
        return [moved(p, lambda x, zh, zl, c, y: (x, zh, zl, c, pair(y, c))) for p in parts]

    near, away = half_of(ih), half_of(1 - ih)
    away = moved(away, lambda x, zh, zl, c, y: (x, 1 - zh, zl, c, y))

    raw = jnp.transpose(matrix[:, :QS])
    mates = [moved(raw, lambda x, zh, zl, c, y, k=k: (x, zh, zl, c, mate(y, k))) for k in (0, 1)]
    mates, near = lax.optimization_barrier((mates, near))
    raw = jnp.concatenate([raw, *mates, sample[0].astype(F32), jnp.zeros((4, ROWS), F32)])
    raw = jnp.broadcast_to(raw[None], (4, *raw.shape))
    raw = lax.all_to_all(raw, "x", 0, 0, tiled=True)

    steps = [first_step(near[:128], 0), first_step(near[128:], 1)]
    raw, steps, away = lax.optimization_barrier((raw, steps, away))
    mine = [second_step(steps[n], n) for n in range(2)]
    others = [first_step(away[n * 128 : n * 128 + 128], n) for n in range(2)]
    mine, others = lax.optimization_barrier((mine, others))
    mine = mine + paired(mine)
    others = [second_step(others[n], n) for n in range(2)]
    others = others + paired(others)

    picks = raw[:, 3 * QS : 3 * QS + 4].reshape(16, 2, 128)
    picks = jnp.pad(picks, ((0, 0), (0, 6), (0, 0))).reshape(128, 128)
    raw = raw[:, : 3 * QS].reshape(4, 3, QS, ROWS)

    def slot(core):
        first = (jnp.arange(4) - iy + ix) % 4
        first = (first == 0) | (first == (pair(iy, core) - iy) % 4)
        groups = jnp.stack([raw[:, 0], raw[:, 1 + core]], axis=1)
        groups = jnp.where(first[:, None, None, None], groups[..., :128], groups[..., 128:])
        return jnp.concatenate([groups.reshape(8 * QS, 128), picks])

    slots = jnp.stack([slot(0), slot(1)])
    slots = jnp.broadcast_to(slots[None], (4, *slots.shape)).reshape(8, *slots.shape[1:])
    pieces = lax.all_to_all(slots, ("zh", "zl", "core"), 0, 0, tiled=True)

    block_x = jnp.stack([iy - ix, iy - ix + 2, my_pair - ix, my_pair - ix + 2]) % 4
    at = [block_x, block_x, jnp.repeat(jnp.stack([ih, 1 - ih]), 4)]
    at = jnp.concatenate(at + [jnp.stack([iy, my_mate, il * 2 + ic])]).astype(jnp.int32)

    vmem = pl.BlockSpec(memory_space=pltpu.VMEM)
    hilo, norms = pl.pallas_call(
        query_kernel,
        out_shape=(
            jax.ShapeDtypeStruct((4 * GROUP, 1024), BF16),
            jax.ShapeDtypeStruct((2, 8, 128), F32),
        ),
        in_specs=[pl.BlockSpec(memory_space=pltpu.SMEM), vmem],
        out_specs=(vmem, vmem),
        scratch_shapes=[pltpu.VMEM((GROUP, 128), F32)],
        compiler_params=limit(),
        name="query_prepare",
    )(at, pieces)

    tiles = CHUNK // TILE
    cols = [pltpu.VMEM((512, TILE), BF16), pltpu.VMEM((512, TILE), BF16)]
    tile = lambda rows, shift=0: pl.BlockSpec((rows, TILE), lambda t: (0, t + shift))
    partial = pl.pallas_call(
        first_kernel,
        grid=(HALF // TILE,),
        out_shape=jax.ShapeDtypeStruct((2 * GROUP + 8, HALF), F32),
        in_specs=[pl.BlockSpec((4 * GROUP, 512), lambda t: (0, 0))] + [tile(128)] * 4,
        out_specs=tile(2 * GROUP + 8),
        scratch_shapes=cols,
        compiler_params=limit(),
        name="product_first_rows",
    )(hilo, *mine)

    to_mate = lambda x, zh, zl, c, y: (x, zh, zl, c, mate(y, c))
    ends = []
    for n in range(2):
        ours, theirs = pl.pallas_call(
            second_kernel,
            grid=(tiles,),
            out_shape=(jax.ShapeDtypeStruct((GROUP + 8, CHUNK), F32),) * 2,
            in_specs=[
                pl.BlockSpec((4 * GROUP, 512), lambda t: (0, 1)),
                pl.BlockSpec((2, 8, 128), lambda t: (0, 0, 0)),
                tile(2 * GROUP + 8, n * tiles),
            ]
            + [tile(128, n * tiles)] * 4,
            out_specs=(tile(GROUP + 8),) * 2,
            scratch_shapes=cols,
            compiler_params=limit(),
            name="product_other_rows",
        )(hilo, norms, partial, *others)
        ends.append((ours, moved(theirs, to_mate)))

    result = []
    for n in range(2):
        result = pl.pallas_call(
            final_kernel,
            grid=(tiles,),
            out_shape=jax.ShapeDtypeStruct((HALF * 3, 128), F32),
            in_specs=[tile(GROUP + 8)] * 2 + [pl.BlockSpec(memory_space=pl.ANY)] * n,
            out_specs=pl.BlockSpec((TILE * 3, 128), lambda t, n=n: (t + n * tiles, 0)),
            input_output_aliases={2: 0} if n else {},
            compiler_params=limit(),
            name="scale_and_turn",
        )(*ends[n], *([result] if n else []))
    return result.reshape(1, HALF, 1, GROUP)


def solution(mesh):
    fine = Mesh(mesh.devices.reshape(SIZES), AXES)
    rows, ci = ("x", "zh"), ("zl", "core")
    return jax.shard_map(
        shards,
        mesh=fine,
        in_specs=(P(rows, ci + ("y",)), P(ci, None, rows)),
        out_specs=P(ci, rows, "y", None),
        check_vma=False,
    )
```

time: 178 us -> 169 us (0.949)
  starting transfers between devices: 79.9 us -> 60.8 us
  waiting for transfers between devices: 56 us -> 67.9 us
  other arithmetic: 9.41 us -> 0.51 us
  local copies, waits for them, and re-layouts: 9.39 us -> 12.8 us
  Pallas kernels: 21.8 us -> 24.8 us
    ppermute x25 -> x17, starting transfers between devices: 79.9 us -> 52 us  [moved(): lax.ppermute(array, AXES, [(index(*t[:5]), index(*t[5])) for t in table])]
    ppermute x25 -> x17, waiting for transfers between devices: 56 us -> 67.9 us  [moved(): lax.ppermute(array, AXES, [(index(*t[:5]), index(*t[5])) for t in table])]
    all_to_all x0 -> x2, starting transfers between devices: none -> 8.79 us  [the longest x1 4.5 us: shards(): pieces = lax.all_to_all(slots, ('zh', 'zl', 'core'), 0, 0, tiled=True)]
    another operation x5 -> x3, other arithmetic: 7.38 us -> 0.2 us  [the longest x2 0.12 us: shards(): slots = jnp.stack([slot(0), slot(1)])]
    dynamic_slice x0 -> x1, local copies, waits for them, and re-layouts: none -> 3.24 us  [half_of(): return lax.dynamic_slice(matrix, (0, side * HALF), (ROWS, HALF))]
    broadcast_in_dim x1 -> x4, local copies, waits for them, and re-layouts: 0.07 us -> 3.27 us  [the longest x1 2.07 us: shards(): jnp.broadcast_to(slots[None], (4, *slots.shape))]
    pallas_call x4 -> x6, Pallas kernels: 21.8 us -> 24.8 us  [the longest x2 9.13 us: shards(): pl.pallas_call(second_kernel, grid=(tiles,), out_shape=(jax.ShapeDtypeStr...]
    unnamed x21 -> x8, local copies, waits for them, and re-layouts: 4.25 us -> 1.66 us
  transfers between devices with their start and end apart: 25 -> 19, of which waited for: 8 -> 8; matrix products, arithmetic and copies ran while one was open for 8% -> 3% of each run, Pallas kernels for 6% -> 11%
where the time goes in v3:
time: 169 us; the launch traced here: 167 us
  waiting for transfers between devices  67.9 us (40%)
  starting transfers between devices  60.8 us (36%)
  Pallas kernels  24.8 us (15%)
  local copies, waits for them, and re-layouts  12.8 us (8%)
    ppermute x17, waiting for transfers between devices, moved(): lax.ppermute(array, AXES, [(index(*t[:5]), index(*t[5])) for t in table])  67.9 us
    ppermute x17, starting transfers between devices, moved(): lax.ppermute(array, AXES, [(index(*t[:5]), index(*t[5])) for t in table])  52 us
    pallas_call x2, Pallas kernels, shards(): pl.pallas_call(second_kernel, grid=(tiles,), out_shape=(jax.ShapeDtypeStr...  9.13 us
    pallas_call x1, Pallas kernels, shards(): pl.pallas_call(first_kernel, grid=(HALF // TILE,), out_shape=jax.ShapeDty...  8.76 us
    all_to_all x1, starting transfers between devices, shards(): pieces = lax.all_to_all(slots, ('zh', 'zl', 'core'), 0, 0, tiled=True)  4.5 us
    all_to_all x1, starting transfers between devices, shards(): raw = lax.all_to_all(raw, 'x', 0, 0, tiled=True)  4.29 us
    pallas_call x2, Pallas kernels, shards(): pl.pallas_call(final_kernel, grid=(tiles,), out_shape=jax.ShapeDtypeStruc...  4 us
  transfers between devices with their start and end apart: 19, of which 8 were waited for; matrix products, arithmetic and copies ran while one was open for 3% of the time, Pallas kernels for 11%

profile of v3, /device:TPU:0, one launch (start us, length us, event | category | flops | bytes accessed | tf_op | source)
XLA Modules:
  0.0 167.1 jit_solution(12871860611067072077)
XLA Ops:
  0.0 3.2 %constant_dynamic-slice_fusion = (f32[256,1536]{1,0:T(8,128)}, f32[256,1536]{1,0:T(8,128)S(1)}) fusion(f32[256,3072]{1,0:T(8,128)} %param.2, s32[]{:T(128)S(6)} %select_n.64, s32[]{:T(128)S(6)} %select_n.63), kind=kLoop, calls=%fused_computation.25 | loop fusion | bytes 6291464 | tf_op jit(solution)/shard_map/dynamic_slice | solution.py:125
  3.2 4.0 %collective-permute-start.4 = (f32[256,1536]{1,0:T(8,128)}, f32[256,1536]{1,0:T(8,128)}, u32[]{:S(2)}, u32[]{:S(2)}) collective-permute-start(f32[256,1536]{1,0:T(8,128)} %get-tuple-element.39), channel_id=1, source_target_pairs={{0,16},{1,17},{2,18},{3,19},{4,20},{5,21},{6,22},{7,23},{8,24},{9,... | collective-permute-start | bytes 4718600 | tf_op jit(solution)/shard_map/ppermute | solution.py:38
  7.2 0.9 slice_bitcast_fusion
  8.1 3.1 %collective-permute-start = (f32[96,256]{0,1:T(8,128)S(1)}, f32[96,256]{0,1:T(8,128)S(1)}, u32[]{:S(2)}, u32[]{:S(2)}) collective-permute-start(f32[96,256]{0,1:T(8,128)S(1)} %slice_bitcast_fusion), channel_id=1, source_target_pairs={{0,3},{1,2},{2,1},{3,0},{4,7},{5,6},{6,5},{7,4},{8,11},{9,10},{10,... | collective-permute-start | bytes 294920 | tf_op jit(solution)/shard_map/ppermute | solution.py:38
  11.2 0.1 collective-permute-start.1
  11.4 0.1 copy.4
  11.5 2.9 %collective-permute-done = f32[96,256]{0,1:T(8,128)S(1)} collective-permute-done((f32[96,256]{0,1:T(8,128)S(1)}, f32[96,256]{0,1:T(8,128)S(1)}, u32[]{:S(2)}, u32[]{:S(2)}) %collective-permute-start) | collective-permute-done | bytes 98336 | tf_op jit(solution)/shard_map/ppermute | solution.py:38
  14.4 1.8 %collective-permute-done.1 = f32[96,256]{0,1:T(8,128)S(1)} collective-permute-done((f32[96,256]{0,1:T(8,128)S(1)}, f32[96,256]{0,1:T(8,128)S(1)}, u32[]{:S(2)}, u32[]{:S(2)}) %collective-permute-start.1) | collective-permute-done | bytes 98336 | tf_op jit(solution)/shard_map/ppermute | solution.py:38
  16.2 0.3 concatenate.13
  16.4 0.1 copy.5
  16.6 1.1 broadcast_in_dim.36
  17.7 4.3 %all-to-all-start = ((f32[4,296,256]{2,1,0:T(8,128)}), f32[4,296,256]{2,1,0:T(8,128)S(1)}, u32[]{:S(2)}, u32[]{:S(2)}) async-start(f32[4,296,256]{2,1,0:T(8,128)} %broadcast_in_dim.36), calls=%async_computation | async-start | bytes 2424832 | tf_op jit(solution)/shard_map/all_to_all | solution.py:144
  22.0 1.3 fusion.7
  23.3 1.8 %collective-permute-start.2 = (f32[128,1536]{1,0:T(8,128)}, f32[128,1536]{1,0:T(8,128)S(1)}, u32[]{:S(2)}, u32[]{:S(2)}) collective-permute-start(f32[128,1536]{1,0:T(8,128)} %get-tuple-element.44), channel_id=1, source_target_pairs={{0,0},{1,1},{2,2},{3,3},{4,4},{5,5},{6,6},{7,7},{8,8},{9,9},{10,10... | collective-permute-start | bytes 2359304 | tf_op jit(solution)/shard_map/ppermute | solution.py:38
  25.1 2.5 %collective-permute-start.3 = (f32[128,1536]{1,0:T(8,128)}, f32[128,1536]{1,0:T(8,128)}, u32[]{:S(2)}, u32[]{:S(2)}) collective-permute-start(f32[128,1536]{1,0:T(8,128)} %get-tuple-element.43), channel_id=1, source_target_pairs={{0,2},{1,3},{2,0},{3,1},{4,6},{5,7},{6,4},{7,5},{8,10},{9,11},{10,... | collective-permute-start | bytes 2359304 | tf_op jit(solution)/shard_map/ppermute | solution.py:38
  27.7 18.8 %collective-permute-done.3 = f32[128,1536]{1,0:T(8,128)} collective-permute-done((f32[128,1536]{1,0:T(8,128)}, f32[128,1536]{1,0:T(8,128)}, u32[]{:S(2)}, u32[]{:S(2)}) %collective-permute-start.3) | collective-permute-done | bytes 786464 | tf_op jit(solution)/shard_map/ppermute | solution.py:38
  46.5 0.1 slice.47
  46.7 0.1 slice_select_fusion
  46.8 0.1 fusion.3
  47.1 2.1 %broadcast_in_dim.38 = f32[4,2,896,128]{3,2,1,0:T(8,128)} broadcast(f32[2,896,128]{2,1,0:T(8,128)S(1)} %pad_maximum_fusion), dimensions={1,2,3} | broadcast | bytes 4587520 | tf_op jit(solution)/shard_map/broadcast_in_dim | solution.py:167
  49.1 4.5 %all-to-all-start.1 = ((f32[8,896,128]{2,1,0:T(8,128)}), f32[8,896,128]{2,1,0:T(8,128)}, u32[]{:S(2)}, u32[]{:S(2)}) async-start(f32[8,896,128]{2,1,0:T(8,128)} %bitcast.24), calls=%async_computation.1 | async-start | bytes 7340032 | tf_op jit(solution)/shard_map/all_to_all | solution.py:168
  53.6 1.5 fusion.6
  55.2 0.7 collective-permute-start.7
  55.9 2.6 %collective-permute-start.8 = (f32[128,1536]{1,0:T(8,128)S(1)}, f32[128,1536]{1,0:T(8,128)S(1)}, u32[]{:S(2)}, u32[]{:S(2)}) collective-permute-start(f32[128,1536]{1,0:T(8,128)S(1)} %get-tuple-element.41), channel_id=1, source_target_pairs={{0,2},{1,3},{2,0},{3,1},{4,6},{5,7},{6,4},{7,5},{8,10},{9,11},{10,... | collective-permute-start | bytes 2359304 | tf_op jit(solution)/shard_map/ppermute | solution.py:38
  58.5 1.6 collective-permute-start.5
  60.1 4.0 %collective-permute-start.6 = (f32[128,1536]{1,0:T(8,128)}, f32[128,1536]{1,0:T(8,128)}, u32[]{:S(2)}, u32[]{:S(2)}) collective-permute-start(f32[128,1536]{1,0:T(8,128)} %collective-permute-done.3), channel_id=1, source_target_pairs={{0,64},{1,97},{2,2},{3,35},{4,68},{5,101},{6,6},{7,39},{8,72},{9,1... | collective-permute-start | bytes 2359304 | tf_op jit(solution)/shard_map/ppermute | solution.py:38
  64.1 15.0 %collective-permute-done.8 = f32[128,1536]{1,0:T(8,128)S(1)} collective-permute-done((f32[128,1536]{1,0:T(8,128)S(1)}, f32[128,1536]{1,0:T(8,128)S(1)}, u32[]{:S(2)}, u32[]{:S(2)}) %collective-permute-start.8) | collective-permute-done | bytes 786464 | tf_op jit(solution)/shard_map/ppermute | solution.py:38
  79.1 4.2 %collective-permute-done.6.refs_1_ = f32[128,1536]{1,0:T(8,128)} collective-permute-done((f32[128,1536]{1,0:T(8,128)}, f32[128,1536]{1,0:T(8,128)}, u32[]{:S(2)}, u32[]{:S(2)}) %collective-permute-start.6) | collective-permute-done | bytes 786464 | tf_op jit(solution)/shard_map/ppermute | solution.py:38
  83.3 0.7 collective-permute-start.11
  84.0 4.0 %collective-permute-start.12 = (f32[128,1536]{1,0:T(8,128)S(1)}, f32[128,1536]{1,0:T(8,128)S(1)}, u32[]{:S(2)}, u32[]{:S(2)}) collective-permute-start(f32[128,1536]{1,0:T(8,128)S(1)} %collective-permute-done.8), channel_id=1, source_target_pairs={{0,64},{1,97},{2,2},{3,35},{4,68},{5,101},{6,6},{7,39},{8,72},{9,1... | collective-permute-start | bytes 2359304 | tf_op jit(solution)/shard_map/ppermute | solution.py:38
  88.0 6.4 %collective-permute-start.10 = (f32[128,1536]{1,0:T(8,128)}, f32[128,1536]{1,0:T(8,128)}, u32[]{:S(2)}, u32[]{:S(2)}) collective-permute-start(f32[128,1536]{1,0:T(8,128)} %collective-permute-done.6.refs_1_), channel_id=1, source_target_pairs={{0,1},{1,0},{2,3},{3,2},{4,7},{5,6},{6,5},{7,4},{8,9},{9,8},{10,11... | collective-permute-start | bytes 2359304 | tf_op jit(solution)/shard_map/ppermute | solution.py:38
  94.4 0.1 collective-permute-start.9
  94.5 12.9 %collective-permute-start.13 = (f32[128,1536]{1,0:T(8,128)S(1)}, f32[128,1536]{1,0:T(8,128)S(1)}, u32[]{:S(2)}, u32[]{:S(2)}) collective-permute-start(f32[128,1536]{1,0:T(8,128)S(1)} %collective-permute-done.11.refs_0_), channel_id=1, source_target_pairs={{0,1},{1,0},{2,3},{3,2},{4,7},{5,6},{6,5},{7,4},{8,9},{9,8},{10,11... | collective-permute-start | bytes 2359304 | tf_op jit(solution)/shard_map/ppermute | solution.py:38
  107.4 4.2 %collective-permute-start.14 = (f32[128,1536]{1,0:T(8,128)S(1)}, f32[128,1536]{1,0:T(8,128)S(1)}, u32[]{:S(2)}, u32[]{:S(2)}) collective-permute-start(f32[128,1536]{1,0:T(8,128)S(1)} %collective-permute-done.12.refs_1_), channel_id=1, source_target_pairs={{0,1},{1,0},{2,3},{3,2},{4,7},{5,6},{6,5},{7,4},{8,9},{9,8},{10,11... | collective-permute-start | bytes 2359304 | tf_op jit(solution)/shard_map/ppermute | solution.py:38
  111.7 0.1 reshape.50
  111.9 0.1 concatenate.12.at_ref
  112.0 2.9 %query_prepare.1 = (bf16[1536,1024]{1,0:T(8,128)(2,1)S(1)}, f32[2,8,128]{2,1,0:T(8,128)S(1)}) custom-call(s32[19]{0:T(128)S(1)} %concatenate.12.at_ref, f32[8,896,128]{2,1,0:T(8,128)} %all-to-all-done.1.pieces_ref), custom_call_target="tpu_custom_call" | custom-call | tf_op jit(solution)/shard_map/query_prepare/pallas_call | solution.py:175
  114.9 1.6 copy-done
  116.6 8.8 %product_first_rows.1.before_ref = f32[776,1536]{1,0:T(8,128)} custom-call(bf16[1536,1024]{1,0:T(8,128)(2,1)} %copy-done, f32[128,1536]{1,0:T(8,128)} %collective-permute-done.5.refs_0_, f32[128,1536]{1,0:T(8,128)} %collective-permute-done.6.refs_1_, f32[128,1536]{1,0:T(8,128)} %collective-permute-done.9.refs_2_, f32[128,1536]{1,0:T(8,128)} %collective-permute-done.10.refs_3_), custom_call_target="tpu_custom_call" | custom-call | tf_op jit(solution)/shard_map/product_first_rows/pallas_call | solution.py:191
  125.3 4.5 %collective-permute-done.14.refs_3_ = f32[128,1536]{1,0:T(8,128)S(1)} collective-permute-done((f32[128,1536]{1,0:T(8,128)S(1)}, f32[128,1536]{1,0:T(8,128)S(1)}, u32[]{:S(2)}, u32[]{:S(2)}) %collective-permute-start.14) | collective-permute-done | bytes 786464 | tf_op jit(solution)/shard_map/ppermute | solution.py:38
  129.9 4.6 %product_other_rows.3 = (f32[392,768]{1,0:T(8,128)S(1)}, f32[392,768]{1,0:T(8,128)S(1)}) custom-call(bf16[1536,1024]{1,0:T(8,128)(2,1)} %copy-done, f32[2,8,128]{2,1,0:T(8,128)S(1)} %get-tuple-element.27.norms_ref, f32[776,1536]{1,0:T(8,128)} %product_first_rows.1.before_ref, f32[128,1536]{1,0:T(8,128)S(1)} %collective-permute-done.11.refs_0_, ...), custom_call_target="tpu_custom_call" | custom-call | tf_op jit(solution)/shard_map/product_other_rows/pallas_call | solution.py:205
  134.4 2.3 %collective-permute-start.16 = (f32[392,768]{1,0:T(8,128)S(1)}, f32[392,768]{1,0:T(8,128)S(1)}, u32[]{:S(2)}, u32[]{:S(2)}) collective-permute-start(f32[392,768]{1,0:T(8,128)S(1)} %get-tuple-element.38), channel_id=1, source_target_pairs={{0,3},{1,2},{2,1},{3,0},{4,5},{5,4},{6,7},{7,6},{8,11},{9,10},{10,... | collective-permute-start | bytes 3612680 | tf_op jit(solution)/shard_map/ppermute | solution.py:38
  136.8 4.6 %product_other_rows.2 = (f32[392,768]{1,0:T(8,128)S(1)}, f32[392,768]{1,0:T(8,128)S(1)}) custom-call(bf16[1536,1024]{1,0:T(8,128)(2,1)} %copy-done, f32[2,8,128]{2,1,0:T(8,128)S(1)} %get-tuple-element.27.norms_ref, f32[776,1536]{1,0:T(8,128)} %product_first_rows.1.before_ref, f32[128,1536]{1,0:T(8,128)S(1)} %collective-permute-done.11.refs_0_, ...), custom_call_target="tpu_custom_call" | custom-call | tf_op jit(solution)/shard_map/product_other_rows/pallas_call | solution.py:205
  141.3 1.1 collective-permute-start.15
  142.4 9.8 %collective-permute-done.16.got = f32[392,768]{1,0:T(8,128)S(1)} collective-permute-done((f32[392,768]{1,0:T(8,128)S(1)}, f32[392,768]{1,0:T(8,128)S(1)}, u32[]{:S(2)}, u32[]{:S(2)}) %collective-permute-start.16) | collective-permute-done | bytes 1204256 | tf_op jit(solution)/shard_map/ppermute | solution.py:38
  152.2 2.0 %scale_and_turn.2.refs_0_ = f32[4608,128]{1,0:T(8,128)} custom-call(f32[392,768]{1,0:T(8,128)S(1)} %get-tuple-element.37.own, f32[392,768]{1,0:T(8,128)S(1)} %collective-permute-done.16.got), custom_call_target="tpu_custom_call" | custom-call | tf_op jit(solution)/shard_map/scale_and_turn/pallas_call | solution.py:224
  154.2 10.9 %collective-permute-done.15.got = f32[392,768]{1,0:T(8,128)S(1)} collective-permute-done((f32[392,768]{1,0:T(8,128)S(1)}, f32[392,768]{1,0:T(8,128)S(1)}, u32[]{:S(2)}, u32[]{:S(2)}) %collective-permute-start.15) | collective-permute-done | bytes 1204256 | tf_op jit(solution)/shard_map/ppermute | solution.py:38
  165.1 2.0 %scale_and_turn.3 = f32[4608,128]{1,0:T(8,128)} custom-call(f32[392,768]{1,0:T(8,128)S(1)} %get-tuple-element.35.own, f32[392,768]{1,0:T(8,128)S(1)} %collective-permute-done.15.got, f32[4608,128]{1,0:T(8,128)} %scale_and_turn.2.refs_0_), custom_call_target="tpu_custom_call", output_to_operand_aliasing={{}: (2, {})} | custom-call | tf_op jit(solution)/shard_map/scale_and_turn/pallas_call | solution.py:224
  (30 shorter events, 0.5 us)
Async XLA Ops:
  0.0 11.4 %copy-start.1 = (s32[1,4,256]{2,1,0:T(4,128)S(1)}, s32[1,4,256]{2,1,0:T(4,128)}, u32[]{:S(2)}) copy-start(s32[1,4,256]{2,1,0:T(4,128)} %param.3) | copy-start | bytes 12292
  3.2 43.2 %collective-permute-start.4 = (f32[256,1536]{1,0:T(8,128)}, f32[256,1536]{1,0:T(8,128)}, u32[]{:S(2)}, u32[]{:S(2)}) collective-permute-start(f32[256,1536]{1,0:T(8,128)} %get-tuple-element.39), channel_id=1, source_target_pairs={{0,16},{1,17},{2,18},{3,19},{4,20},{5,21},{6,22},{7,23},{8,24},{9,... | collective-permute-start | bytes 4718600 | tf_op jit(solution)/shard_map/ppermute | solution.py:38
  8.1 6.3 %collective-permute-start = (f32[96,256]{0,1:T(8,128)S(1)}, f32[96,256]{0,1:T(8,128)S(1)}, u32[]{:S(2)}, u32[]{:S(2)}) collective-permute-start(f32[96,256]{0,1:T(8,128)S(1)} %slice_bitcast_fusion), channel_id=1, source_target_pairs={{0,3},{1,2},{2,1},{3,0},{4,7},{5,6},{6,5},{7,4},{8,11},{9,10},{10,... | collective-permute-start | bytes 294920 | tf_op jit(solution)/shard_map/ppermute | solution.py:38
  11.2 5.0 %collective-permute-start.1 = (f32[96,256]{0,1:T(8,128)S(1)}, f32[96,256]{0,1:T(8,128)S(1)}, u32[]{:S(2)}, u32[]{:S(2)}) collective-permute-start(f32[96,256]{0,1:T(8,128)S(1)} %slice_bitcast_fusion), channel_id=1, source_target_pairs={{0,1},{1,0},{2,3},{3,2},{4,5},{5,4},{6,7},{7,6},{8,9},{9,8},{10,11... | collective-permute-start | bytes 294920 | tf_op jit(solution)/shard_map/ppermute | solution.py:38
  17.7 28.7 %all-to-all-start = ((f32[4,296,256]{2,1,0:T(8,128)}), f32[4,296,256]{2,1,0:T(8,128)S(1)}, u32[]{:S(2)}, u32[]{:S(2)}) async-start(f32[4,296,256]{2,1,0:T(8,128)} %broadcast_in_dim.36), calls=%async_computation | async-start | bytes 2424832 | tf_op jit(solution)/shard_map/all_to_all | solution.py:144
  23.3 4.4 %collective-permute-start.2 = (f32[128,1536]{1,0:T(8,128)}, f32[128,1536]{1,0:T(8,128)S(1)}, u32[]{:S(2)}, u32[]{:S(2)}) collective-permute-start(f32[128,1536]{1,0:T(8,128)} %get-tuple-element.44), channel_id=1, source_target_pairs={{0,0},{1,1},{2,2},{3,3},{4,4},{5,5},{6,6},{7,7},{8,8},{9,9},{10,10... | collective-permute-start | bytes 2359304 | tf_op jit(solution)/shard_map/ppermute | solution.py:38
  25.1 21.4 %collective-permute-start.3 = (f32[128,1536]{1,0:T(8,128)}, f32[128,1536]{1,0:T(8,128)}, u32[]{:S(2)}, u32[]{:S(2)}) collective-permute-start(f32[128,1536]{1,0:T(8,128)} %get-tuple-element.43), channel_id=1, source_target_pairs={{0,2},{1,3},{2,0},{3,1},{4,6},{5,7},{6,4},{7,5},{8,10},{9,11},{10,... | collective-permute-start | bytes 2359304 | tf_op jit(solution)/shard_map/ppermute | solution.py:38
  27.7 18.9 %copy-start.2 = (f32[128,1536]{1,0:T(8,128)}, f32[128,1536]{1,0:T(8,128)S(1)}, u32[]{:S(2)}) copy-start(f32[128,1536]{1,0:T(8,128)S(1)} %collective-permute-done.2) | copy-start | bytes 2359300
  49.1 62.9 %all-to-all-start.1 = ((f32[8,896,128]{2,1,0:T(8,128)}), f32[8,896,128]{2,1,0:T(8,128)}, u32[]{:S(2)}, u32[]{:S(2)}) async-start(f32[8,896,128]{2,1,0:T(8,128)} %bitcast.24), calls=%async_computation.1 | async-start | bytes 7340032 | tf_op jit(solution)/shard_map/all_to_all | solution.py:168
  53.6 4.8 %copy-start.3 = (f32[128,1536]{1,0:T(8,128)S(1)}, f32[128,1536]{1,0:T(8,128)}, u32[]{:S(2)}) copy-start(f32[128,1536]{1,0:T(8,128)} %copy-done.2) | copy-start | bytes 2359300
  55.2 8.9 %collective-permute-start.7 = (f32[128,1536]{1,0:T(8,128)S(1)}, f32[128,1536]{1,0:T(8,128)S(1)}, u32[]{:S(2)}, u32[]{:S(2)}) collective-permute-start(f32[128,1536]{1,0:T(8,128)S(1)} %get-tuple-element.42), channel_id=1, source_target_pairs={{0,0},{1,1},{2,2},{3,3},{4,4},{5,5},{6,6},{7,7},{8,8},{9,9},{10,10... | collective-permute-start | bytes 2359304 | tf_op jit(solution)/shard_map/ppermute | solution.py:38
  55.9 23.2 %collective-permute-start.8 = (f32[128,1536]{1,0:T(8,128)S(1)}, f32[128,1536]{1,0:T(8,128)S(1)}, u32[]{:S(2)}, u32[]{:S(2)}) collective-permute-start(f32[128,1536]{1,0:T(8,128)S(1)} %get-tuple-element.41), channel_id=1, source_target_pairs={{0,2},{1,3},{2,0},{3,1},{4,6},{5,7},{6,4},{7,5},{8,10},{9,11},{10,... | collective-permute-start | bytes 2359304 | tf_op jit(solution)/shard_map/ppermute | solution.py:38
  58.5 20.6 %collective-permute-start.5 = (f32[128,1536]{1,0:T(8,128)S(1)}, f32[128,1536]{1,0:T(8,128)}, u32[]{:S(2)}, u32[]{:S(2)}) collective-permute-start(f32[128,1536]{1,0:T(8,128)S(1)} %copy-done.3), channel_id=1, source_target_pairs={{0,0},{1,33},{2,66},{3,99},{4,4},{5,37},{6,70},{7,103},{8,8},{9,41... | collective-permute-start | bytes 2359304 | tf_op jit(solution)/shard_map/ppermute | solution.py:38
  60.1 23.2 %collective-permute-start.6 = (f32[128,1536]{1,0:T(8,128)}, f32[128,1536]{1,0:T(8,128)}, u32[]{:S(2)}, u32[]{:S(2)}) collective-permute-start(f32[128,1536]{1,0:T(8,128)} %collective-permute-done.3), channel_id=1, source_target_pairs={{0,64},{1,97},{2,2},{3,35},{4,68},{5,101},{6,6},{7,39},{8,72},{9,1... | collective-permute-start | bytes 2359304 | tf_op jit(solution)/shard_map/ppermute | solution.py:38
  83.3 11.2 %collective-permute-start.11 = (f32[128,1536]{1,0:T(8,128)S(1)}, f32[128,1536]{1,0:T(8,128)S(1)}, u32[]{:S(2)}, u32[]{:S(2)}) collective-permute-start(f32[128,1536]{1,0:T(8,128)S(1)} %collective-permute-done.7), channel_id=1, source_target_pairs={{0,0},{1,33},{2,66},{3,99},{4,4},{5,37},{6,70},{7,103},{8,8},{9,41... | collective-permute-start | bytes 2359304 | tf_op jit(solution)/shard_map/ppermute | solution.py:38
  84.0 23.4 %collective-permute-start.12 = (f32[128,1536]{1,0:T(8,128)S(1)}, f32[128,1536]{1,0:T(8,128)S(1)}, u32[]{:S(2)}, u32[]{:S(2)}) collective-permute-start(f32[128,1536]{1,0:T(8,128)S(1)} %collective-permute-done.8), channel_id=1, source_target_pairs={{0,64},{1,97},{2,2},{3,35},{4,68},{5,101},{6,6},{7,39},{8,72},{9,1... | collective-permute-start | bytes 2359304 | tf_op jit(solution)/shard_map/ppermute | solution.py:38
  88.0 28.5 %collective-permute-start.10 = (f32[128,1536]{1,0:T(8,128)}, f32[128,1536]{1,0:T(8,128)}, u32[]{:S(2)}, u32[]{:S(2)}) collective-permute-start(f32[128,1536]{1,0:T(8,128)} %collective-permute-done.6.refs_1_), channel_id=1, source_target_pairs={{0,1},{1,0},{2,3},{3,2},{4,7},{5,6},{6,5},{7,4},{8,9},{9,8},{10,11... | collective-permute-start | bytes 2359304 | tf_op jit(solution)/shard_map/ppermute | solution.py:38
  94.4 22.2 %collective-permute-start.9 = (f32[128,1536]{1,0:T(8,128)}, f32[128,1536]{1,0:T(8,128)}, u32[]{:S(2)}, u32[]{:S(2)}) collective-permute-start(f32[128,1536]{1,0:T(8,128)} %collective-permute-done.5.refs_0_), channel_id=1, source_target_pairs={{0,1},{1,0},{2,3},{3,2},{4,7},{5,6},{6,5},{7,4},{8,9},{9,8},{10,11... | collective-permute-start | bytes 2359304 | tf_op jit(solution)/shard_map/ppermute | solution.py:38
  94.5 30.8 %collective-permute-start.13 = (f32[128,1536]{1,0:T(8,128)S(1)}, f32[128,1536]{1,0:T(8,128)S(1)}, u32[]{:S(2)}, u32[]{:S(2)}) collective-permute-start(f32[128,1536]{1,0:T(8,128)S(1)} %collective-permute-done.11.refs_0_), channel_id=1, source_target_pairs={{0,1},{1,0},{2,3},{3,2},{4,7},{5,6},{6,5},{7,4},{8,9},{9,8},{10,11... | collective-permute-start | bytes 2359304 | tf_op jit(solution)/shard_map/ppermute | solution.py:38
  107.4 22.5 %collective-permute-start.14 = (f32[128,1536]{1,0:T(8,128)S(1)}, f32[128,1536]{1,0:T(8,128)S(1)}, u32[]{:S(2)}, u32[]{:S(2)}) collective-permute-start(f32[128,1536]{1,0:T(8,128)S(1)} %collective-permute-done.12.refs_1_), channel_id=1, source_target_pairs={{0,1},{1,0},{2,3},{3,2},{4,7},{5,6},{6,5},{7,4},{8,9},{9,8},{10,11... | collective-permute-start | bytes 2359304 | tf_op jit(solution)/shard_map/ppermute | solution.py:38
  114.9 1.7 copy-start
  134.4 17.8 %collective-permute-start.16 = (f32[392,768]{1,0:T(8,128)S(1)}, f32[392,768]{1,0:T(8,128)S(1)}, u32[]{:S(2)}, u32[]{:S(2)}) collective-permute-start(f32[392,768]{1,0:T(8,128)S(1)} %get-tuple-element.38), channel_id=1, source_target_pairs={{0,3},{1,2},{2,1},{3,0},{4,5},{5,4},{6,7},{7,6},{8,11},{9,10},{10,... | collective-permute-start | bytes 3612680 | tf_op jit(solution)/shard_map/ppermute | solution.py:38
  141.3 23.7 %collective-permute-start.15 = (f32[392,768]{1,0:T(8,128)S(1)}, f32[392,768]{1,0:T(8,128)S(1)}, u32[]{:S(2)}, u32[]{:S(2)}) collective-permute-start(f32[392,768]{1,0:T(8,128)S(1)} %get-tuple-element.36), channel_id=1, source_target_pairs={{0,3},{1,2},{2,1},{3,0},{4,5},{5,4},{6,7},{7,6},{8,11},{9,10},{10,... | collective-permute-start | bytes 3612680 | tf_op jit(solution)/shard_map/ppermute | solution.py:38

commit v4 on v3

--- a/solution.py
+++ b/solution.py
@@ -12,7 +12,7 @@
 AXES = ("x", "zh", "zl", "core", "y")
 SIZES = (4, 2, 2, 2, 4)
 ROWS, COLS, HALF, QS, GROUP = 256, 3072, 1536, 96, 384
-CHUNK, TILE = 768, 256
+CHUNK, TILE = 768, 768
 F32, BF16 = jnp.float32, jnp.bfloat16
 
 
@@ -57,9 +57,9 @@
                 total[g][i] = total[g][i] + piece * piece
                 hi, lo = split(piece * picks)
                 to = g * GROUP + i * QS
-                hilo_ref[to : to + QS, b * 128 : b * 128 + 128] = hi
-                to += 2 * GROUP
-                hilo_ref[to : to + QS, b * 128 : b * 128 + 128] = lo
+                at = (b // 4) * 1536 + (b % 4) * 128
+                for n, v in enumerate((hi, lo, hi)):
+                    hilo_ref[to : to + QS, at + n * 512 : at + n * 512 + 128] = v
     norms_ref[...] = jnp.zeros_like(norms_ref)
     for g in range(2):
         for i in range(4):
@@ -69,28 +69,28 @@
             norms_ref[g, j + 1 : j + 2, :] = jnp.sum(part, axis=0, keepdims=True)
 
 
-def products(hilo_ref, blocks, colhi, collo):
+def products(hilo_ref, blocks, cols):
     squares = jnp.zeros((128, TILE), F32)
     for b, ref in enumerate(blocks):
         v = ref[...]
         squares = squares + v * v
-        colhi[b * 128 : b * 128 + 128, :], collo[b * 128 : b * 128 + 128, :] = split(v)
-    dot = functools.partial(jnp.dot, preferred_element_type=F32)
-    both = dot(hilo_ref[...], colhi[...])
-    value = both[: 2 * GROUP, :] + (both[2 * GROUP :, :] + dot(hilo_ref[: 2 * GROUP, :], collo[...]))
+        hi, lo = split(v)
+        for n, w in enumerate((hi, hi, lo)):
+            cols[n * 512 + b * 128 : n * 512 + b * 128 + 128, :] = w
+    value = jnp.dot(hilo_ref[...], cols[...], preferred_element_type=F32)
     return value, jnp.sum(squares, axis=0, keepdims=True)
 
 
 def first_kernel(hilo_ref, *refs):
-    blocks, (out_ref, colhi, collo) = refs[:4], refs[4:]
-    value, squares = products(hilo_ref, blocks, colhi, collo)
+    blocks, (out_ref, cols) = refs[:4], refs[4:]
+    value, squares = products(hilo_ref, blocks, cols)
     out_ref[: 2 * GROUP, :] = value
     out_ref[2 * GROUP :, :] = jnp.broadcast_to(squares, (8, TILE))
 
 
 def second_kernel(hilo_ref, norms_ref, before_ref, *refs):
-    blocks, (own_ref, other_ref, colhi, collo) = refs[:4], refs[4:]
-    value, squares = products(hilo_ref, blocks, colhi, collo)
+    blocks, (own_ref, other_ref, cols) = refs[:4], refs[4:]
+    value, squares = products(hilo_ref, blocks, cols)
     squares = before_ref[2 * GROUP :, :] + squares
     row = lax.broadcasted_iota(jnp.int32, (8, TILE), 0)
     for g, out in ((0, own_ref), (1, other_ref)):
@@ -147,7 +147,7 @@
     raw, steps, away = lax.optimization_barrier((raw, steps, away))
     mine = [second_step(steps[n], n) for n in range(2)]
     others = [first_step(away[n * 128 : n * 128 + 128], n) for n in range(2)]
-    mine, others = lax.optimization_barrier((mine, others))
+    mine, _ = lax.optimization_barrier((mine, others))
     mine = mine + paired(mine)
     others = [second_step(others[n], n) for n in range(2)]
     others = others + paired(others)
@@ -175,7 +175,7 @@
     hilo, norms = pl.pallas_call(
         query_kernel,
         out_shape=(
-            jax.ShapeDtypeStruct((4 * GROUP, 1024), BF16),
+            jax.ShapeDtypeStruct((2 * GROUP, 3072), BF16),
             jax.ShapeDtypeStruct((2, 8, 128), F32),
         ),
         in_specs=[pl.BlockSpec(memory_space=pltpu.SMEM), vmem],
@@ -186,13 +186,13 @@
     )(at, pieces)
 
     tiles = CHUNK // TILE
-    cols = [pltpu.VMEM((512, TILE), BF16), pltpu.VMEM((512, TILE), BF16)]
+    cols = [pltpu.VMEM((1536, TILE), BF16)]
     tile = lambda rows, shift=0: pl.BlockSpec((rows, TILE), lambda t: (0, t + shift))
     partial = pl.pallas_call(
         first_kernel,
         grid=(HALF // TILE,),
         out_shape=jax.ShapeDtypeStruct((2 * GROUP + 8, HALF), F32),
-        in_specs=[pl.BlockSpec((4 * GROUP, 512), lambda t: (0, 0))] + [tile(128)] * 4,
+        in_specs=[pl.BlockSpec((2 * GROUP, 1536), lambda t: (0, 0))] + [tile(128)] * 4,
         out_specs=tile(2 * GROUP + 8),
         scratch_shapes=cols,
         compiler_params=limit(),
@@ -207,7 +207,7 @@
             grid=(tiles,),
             out_shape=(jax.ShapeDtypeStruct((GROUP + 8, CHUNK), F32),) * 2,
             in_specs=[
-                pl.BlockSpec((4 * GROUP, 512), lambda t: (0, 1)),
+                pl.BlockSpec((2 * GROUP, 1536), lambda t: (0, 1)),
                 pl.BlockSpec((2, 8, 128), lambda t: (0, 0, 0)),
                 tile(2 * GROUP + 8, n * tiles),
             ]

time: 169 us -> 163 us (0.964)
  starting transfers between devices: 60.8 us -> 57.1 us
  local copies, waits for them, and re-layouts: 12.8 us -> 11.1 us
    ppermute x17, starting transfers between devices: 52 us -> 48.3 us  [moved(): lax.ppermute(array, AXES, [(index(*t[:5]), index(*t[5])) for t in table])]
    pallas_call x1, Pallas kernels: 2.93 us -> 5.11 us  [shards(): pl.pallas_call(query_kernel, out_shape=(jax.ShapeDtypeStruct((2 * GROUP,...]
  transfers between devices with their start and end apart: 19 -> 19, of which waited for: 8 -> 9; matrix products, arithmetic and copies ran while one was open for 3% -> 4% of each run, Pallas kernels for 11% -> 12%
where the time goes in v4:
time: 163 us; the launch traced here: 162 us
  waiting for transfers between devices  67.5 us (41%)
  starting transfers between devices  57.1 us (35%)
  Pallas kernels  25 us (15%)
  local copies, waits for them, and re-layouts  11.1 us (7%)
    ppermute x17, waiting for transfers between devices, moved(): lax.ppermute(array, AXES, [(index(*t[:5]), index(*t[5])) for t in table])  67.5 us
    ppermute x17, starting transfers between devices, moved(): lax.ppermute(array, AXES, [(index(*t[:5]), index(*t[5])) for t in table])  48.3 us
    pallas_call x2, Pallas kernels, shards(): pl.pallas_call(second_kernel, grid=(tiles,), out_shape=(jax.ShapeDtypeStr...  9.09 us
    pallas_call x1, Pallas kernels, shards(): pl.pallas_call(first_kernel, grid=(HALF // TILE,), out_shape=jax.ShapeDty...  8.04 us
    pallas_call x1, Pallas kernels, shards(): pl.pallas_call(query_kernel, out_shape=(jax.ShapeDtypeStruct((2 * GROUP,...  5.11 us
    all_to_all x1, starting transfers between devices, shards(): pieces = lax.all_to_all(slots, ('zh', 'zl', 'core'), 0, 0, tiled=True)  4.5 us
    all_to_all x1, starting transfers between devices, shards(): raw = lax.all_to_all(raw, 'x', 0, 0, tiled=True)  4.29 us
  transfers between devices with their start and end apart: 19, of which 9 were waited for; matrix products, arithmetic and copies ran while one was open for 4% of the time, Pallas kernels for 12%

profile of v4, /device:TPU:0, one launch (start us, length us, event | category | flops | bytes accessed | tf_op | source)
XLA Modules:
  0.0 161.6 jit_solution(5775694498635507267)
XLA Ops:
  0.0 3.2 %constant_dynamic-slice_fusion = (f32[256,1536]{1,0:T(8,128)}, f32[256,1536]{1,0:T(8,128)S(1)}) fusion(f32[256,3072]{1,0:T(8,128)} %param.2, s32[]{:T(128)S(6)} %select_n.64, s32[]{:T(128)S(6)} %select_n.63), kind=kLoop, calls=%fused_computation.25 | loop fusion | bytes 6291464 | tf_op jit(solution)/shard_map/dynamic_slice | solution.py:125
  3.2 4.0 %collective-permute-start.4 = (f32[256,1536]{1,0:T(8,128)}, f32[256,1536]{1,0:T(8,128)}, u32[]{:S(2)}, u32[]{:S(2)}) collective-permute-start(f32[256,1536]{1,0:T(8,128)} %get-tuple-element.35), channel_id=1, source_target_pairs={{0,16},{1,17},{2,18},{3,19},{4,20},{5,21},{6,22},{7,23},{8,24},{9,... | collective-permute-start | bytes 4718600 | tf_op jit(solution)/shard_map/ppermute | solution.py:38
  7.2 0.9 slice_bitcast_fusion
  8.1 3.1 %collective-permute-start = (f32[96,256]{0,1:T(8,128)S(1)}, f32[96,256]{0,1:T(8,128)S(1)}, u32[]{:S(2)}, u32[]{:S(2)}) collective-permute-start(f32[96,256]{0,1:T(8,128)S(1)} %slice_bitcast_fusion), channel_id=1, source_target_pairs={{0,3},{1,2},{2,1},{3,0},{4,7},{5,6},{6,5},{7,4},{8,11},{9,10},{10,... | collective-permute-start | bytes 294920 | tf_op jit(solution)/shard_map/ppermute | solution.py:38
  11.2 0.1 collective-permute-start.1
  11.4 0.1 copy.4
  11.5 2.9 %collective-permute-done = f32[96,256]{0,1:T(8,128)S(1)} collective-permute-done((f32[96,256]{0,1:T(8,128)S(1)}, f32[96,256]{0,1:T(8,128)S(1)}, u32[]{:S(2)}, u32[]{:S(2)}) %collective-permute-start) | collective-permute-done | bytes 98336 | tf_op jit(solution)/shard_map/ppermute | solution.py:38
  14.4 1.8 %collective-permute-done.1 = f32[96,256]{0,1:T(8,128)S(1)} collective-permute-done((f32[96,256]{0,1:T(8,128)S(1)}, f32[96,256]{0,1:T(8,128)S(1)}, u32[]{:S(2)}, u32[]{:S(2)}) %collective-permute-start.1) | collective-permute-done | bytes 98336 | tf_op jit(solution)/shard_map/ppermute | solution.py:38
  16.2 0.3 concatenate.13
  16.4 0.1 copy.5
  16.6 1.1 broadcast_in_dim.36
  17.7 4.3 %all-to-all-start = ((f32[4,296,256]{2,1,0:T(8,128)}), f32[4,296,256]{2,1,0:T(8,128)S(1)}, u32[]{:S(2)}, u32[]{:S(2)}) async-start(f32[4,296,256]{2,1,0:T(8,128)} %broadcast_in_dim.36), calls=%async_computation | async-start | bytes 2424832 | tf_op jit(solution)/shard_map/all_to_all | solution.py:144
  22.0 1.3 fusion.7
  23.3 1.8 %collective-permute-start.2 = (f32[128,1536]{1,0:T(8,128)}, f32[128,1536]{1,0:T(8,128)S(1)}, u32[]{:S(2)}, u32[]{:S(2)}) collective-permute-start(f32[128,1536]{1,0:T(8,128)} %get-tuple-element.40), channel_id=1, source_target_pairs={{0,0},{1,1},{2,2},{3,3},{4,4},{5,5},{6,6},{7,7},{8,8},{9,9},{10,10... | collective-permute-start | bytes 2359304 | tf_op jit(solution)/shard_map/ppermute | solution.py:38
  25.1 2.5 %collective-permute-start.3 = (f32[128,1536]{1,0:T(8,128)}, f32[128,1536]{1,0:T(8,128)}, u32[]{:S(2)}, u32[]{:S(2)}) collective-permute-start(f32[128,1536]{1,0:T(8,128)} %get-tuple-element.39), channel_id=1, source_target_pairs={{0,2},{1,3},{2,0},{3,1},{4,6},{5,7},{6,4},{7,5},{8,10},{9,11},{10,... | collective-permute-start | bytes 2359304 | tf_op jit(solution)/shard_map/ppermute | solution.py:38
  27.7 18.8 %collective-permute-done.3 = f32[128,1536]{1,0:T(8,128)} collective-permute-done((f32[128,1536]{1,0:T(8,128)}, f32[128,1536]{1,0:T(8,128)}, u32[]{:S(2)}, u32[]{:S(2)}) %collective-permute-start.3) | collective-permute-done | bytes 786464 | tf_op jit(solution)/shard_map/ppermute | solution.py:38
  46.5 0.1 slice.47
  46.7 0.1 slice_select_fusion
  46.8 0.1 fusion.3
  47.1 2.1 %broadcast_in_dim.38 = f32[4,2,896,128]{3,2,1,0:T(8,128)} broadcast(f32[2,896,128]{2,1,0:T(8,128)S(1)} %pad_maximum_fusion), dimensions={1,2,3} | broadcast | bytes 4587520 | tf_op jit(solution)/shard_map/broadcast_in_dim | solution.py:167
  49.1 4.5 %all-to-all-start.1 = ((f32[8,896,128]{2,1,0:T(8,128)}), f32[8,896,128]{2,1,0:T(8,128)}, u32[]{:S(2)}, u32[]{:S(2)}) async-start(f32[8,896,128]{2,1,0:T(8,128)} %bitcast.24), calls=%async_computation.1 | async-start | bytes 7340032 | tf_op jit(solution)/shard_map/all_to_all | solution.py:168
  53.7 1.5 fusion.6
  55.2 0.7 collective-permute-start.7
  55.9 2.6 %collective-permute-start.8 = (f32[128,1536]{1,0:T(8,128)S(1)}, f32[128,1536]{1,0:T(8,128)S(1)}, u32[]{:S(2)}, u32[]{:S(2)}) collective-permute-start(f32[128,1536]{1,0:T(8,128)S(1)} %get-tuple-element.37), channel_id=1, source_target_pairs={{0,2},{1,3},{2,0},{3,1},{4,6},{5,7},{6,4},{7,5},{8,10},{9,11},{10,... | collective-permute-start | bytes 2359304 | tf_op jit(solution)/shard_map/ppermute | solution.py:38
  58.5 1.5 collective-permute-start.5
  60.0 4.0 %collective-permute-start.6 = (f32[128,1536]{1,0:T(8,128)}, f32[128,1536]{1,0:T(8,128)}, u32[]{:S(2)}, u32[]{:S(2)}) collective-permute-start(f32[128,1536]{1,0:T(8,128)} %collective-permute-done.3), channel_id=1, source_target_pairs={{0,64},{1,97},{2,2},{3,35},{4,68},{5,101},{6,6},{7,39},{8,72},{9,1... | collective-permute-start | bytes 2359304 | tf_op jit(solution)/shard_map/ppermute | solution.py:38
  64.1 0.7 collective-permute-start.11
  64.8 14.3 %collective-permute-done.8 = f32[128,1536]{1,0:T(8,128)S(1)} collective-permute-done((f32[128,1536]{1,0:T(8,128)S(1)}, f32[128,1536]{1,0:T(8,128)S(1)}, u32[]{:S(2)}, u32[]{:S(2)}) %collective-permute-start.8) | collective-permute-done | bytes 786464 | tf_op jit(solution)/shard_map/ppermute | solution.py:38
  79.1 4.0 %collective-permute-start.12 = (f32[128,1536]{1,0:T(8,128)S(1)}, f32[128,1536]{1,0:T(8,128)S(1)}, u32[]{:S(2)}, u32[]{:S(2)}) collective-permute-start(f32[128,1536]{1,0:T(8,128)S(1)} %collective-permute-done.8), channel_id=1, source_target_pairs={{0,64},{1,97},{2,2},{3,35},{4,68},{5,101},{6,6},{7,39},{8,72},{9,1... | collective-permute-start | bytes 2359304 | tf_op jit(solution)/shard_map/ppermute | solution.py:38
  83.2 0.1 collective-permute-done.6.refs_1_
  83.3 4.0 %collective-permute-start.10 = (f32[128,1536]{1,0:T(8,128)}, f32[128,1536]{1,0:T(8,128)}, u32[]{:S(2)}, u32[]{:S(2)}) collective-permute-start(f32[128,1536]{1,0:T(8,128)} %collective-permute-done.6.refs_1_), channel_id=1, source_target_pairs={{0,1},{1,0},{2,3},{3,2},{4,7},{5,6},{6,5},{7,4},{8,9},{9,8},{10,11... | collective-permute-start | bytes 2359304 | tf_op jit(solution)/shard_map/ppermute | solution.py:38
  87.3 11.4 %collective-permute-start.13 = (f32[128,1536]{1,0:T(8,128)S(1)}, f32[128,1536]{1,0:T(8,128)S(1)}, u32[]{:S(2)}, u32[]{:S(2)}) collective-permute-start(f32[128,1536]{1,0:T(8,128)S(1)} %collective-permute-done.11.refs_0_), channel_id=1, source_target_pairs={{0,1},{1,0},{2,3},{3,2},{4,7},{5,6},{6,5},{7,4},{8,9},{9,8},{10,11... | collective-permute-start | bytes 2359304 | tf_op jit(solution)/shard_map/ppermute | solution.py:38
  98.6 3.0 %collective-permute-done.12.refs_1_ = f32[128,1536]{1,0:T(8,128)S(1)} collective-permute-done((f32[128,1536]{1,0:T(8,128)S(1)}, f32[128,1536]{1,0:T(8,128)S(1)}, u32[]{:S(2)}, u32[]{:S(2)}) %collective-permute-start.12) | collective-permute-done | bytes 786464 | tf_op jit(solution)/shard_map/ppermute | solution.py:38
  101.6 2.2 %collective-permute-start.14 = (f32[128,1536]{1,0:T(8,128)S(1)}, f32[128,1536]{1,0:T(8,128)S(1)}, u32[]{:S(2)}, u32[]{:S(2)}) collective-permute-start(f32[128,1536]{1,0:T(8,128)S(1)} %collective-permute-done.12.refs_1_), channel_id=1, source_target_pairs={{0,1},{1,0},{2,3},{3,2},{4,7},{5,6},{6,5},{7,4},{8,9},{9,8},{10,11... | collective-permute-start | bytes 2359304 | tf_op jit(solution)/shard_map/ppermute | solution.py:38
  103.9 0.1 reshape.50
  104.0 0.1 and_select_fusion.1
  104.1 0.1 concatenate.12.at_ref
  104.2 5.1 %query_prepare.1 = (bf16[768,3072]{1,0:T(8,128)(2,1)}, f32[2,8,128]{2,1,0:T(8,128)S(1)}) custom-call(s32[19]{0:T(128)S(1)} %concatenate.12.at_ref, f32[8,896,128]{2,1,0:T(8,128)} %all-to-all-done.1.pieces_ref), custom_call_target="tpu_custom_call" | custom-call | tf_op jit(solution)/shard_map/query_prepare/pallas_call | solution.py:175
  109.3 8.0 %product_first_rows.1.before_ref = f32[776,1536]{1,0:T(8,128)} custom-call(bf16[768,3072]{1,0:T(8,128)(2,1)} %get-tuple-element.24.hilo_ref, f32[128,1536]{1,0:T(8,128)} %collective-permute-done.5.refs_0_, f32[128,1536]{1,0:T(8,128)} %collective-permute-done.6.refs_1_, f32[128,1536]{1,0:T(8,128)} %collective-permute-done.9.refs_2_, ...), custom_call_target="tpu_custom_call" | custom-call | tf_op jit(solution)/shard_map/product_first_rows/pallas_call | solution.py:191
  117.3 5.3 %collective-permute-done.14.refs_3_ = f32[128,1536]{1,0:T(8,128)S(1)} collective-permute-done((f32[128,1536]{1,0:T(8,128)S(1)}, f32[128,1536]{1,0:T(8,128)S(1)}, u32[]{:S(2)}, u32[]{:S(2)}) %collective-permute-start.14) | collective-permute-done | bytes 786464 | tf_op jit(solution)/shard_map/ppermute | solution.py:38
  122.7 4.5 %product_other_rows.3 = (f32[392,768]{1,0:T(8,128)S(1)}, f32[392,768]{1,0:T(8,128)S(1)}) custom-call(bf16[768,3072]{1,0:T(8,128)(2,1)} %get-tuple-element.24.hilo_ref, f32[2,8,128]{2,1,0:T(8,128)S(1)} %get-tuple-element.25.norms_ref, f32[776,1536]{1,0:T(8,128)} %product_first_rows.1.before_ref, f32[128,1536]{1,0:T(8,128)S(1)} %collective-permute-done.11.refs_0_, ...), custom_call_target="tpu_custom_call" | custom-call | tf_op jit(solution)/shard_map/product_other_rows/pallas_call | solution.py:205
  127.2 5.6 %collective-permute-start.16 = (f32[392,768]{1,0:T(8,128)S(1)}, f32[392,768]{1,0:T(8,128)S(1)}, u32[]{:S(2)}, u32[]{:S(2)}) collective-permute-start(f32[392,768]{1,0:T(8,128)S(1)} %get-tuple-element.34), channel_id=1, source_target_pairs={{0,3},{1,2},{2,1},{3,0},{4,5},{5,4},{6,7},{7,6},{8,11},{9,10},{10,... | collective-permute-start | bytes 3612680 | tf_op jit(solution)/shard_map/ppermute | solution.py:38
  132.9 4.5 %product_other_rows.2 = (f32[392,768]{1,0:T(8,128)S(1)}, f32[392,768]{1,0:T(8,128)S(1)}) custom-call(bf16[768,3072]{1,0:T(8,128)(2,1)} %get-tuple-element.24.hilo_ref, f32[2,8,128]{2,1,0:T(8,128)S(1)} %get-tuple-element.25.norms_ref, f32[776,1536]{1,0:T(8,128)} %product_first_rows.1.before_ref, f32[128,1536]{1,0:T(8,128)S(1)} %collective-permute-done.11.refs_0_, ...), custom_call_target="tpu_custom_call" | custom-call | tf_op jit(solution)/shard_map/product_other_rows/pallas_call | solution.py:205
  137.4 0.1 collective-permute-start.15
  137.5 9.8 %collective-permute-done.16.got = f32[392,768]{1,0:T(8,128)S(1)} collective-permute-done((f32[392,768]{1,0:T(8,128)S(1)}, f32[392,768]{1,0:T(8,128)S(1)}, u32[]{:S(2)}, u32[]{:S(2)}) %collective-permute-start.16) | collective-permute-done | bytes 1204256 | tf_op jit(solution)/shard_map/ppermute | solution.py:38
  147.3 1.4 scale_and_turn.2.refs_0_
  148.7 11.5 %collective-permute-done.15.got = f32[392,768]{1,0:T(8,128)S(1)} collective-permute-done((f32[392,768]{1,0:T(8,128)S(1)}, f32[392,768]{1,0:T(8,128)S(1)}, u32[]{:S(2)}, u32[]{:S(2)}) %collective-permute-start.15) | collective-permute-done | bytes 1204256 | tf_op jit(solution)/shard_map/ppermute | solution.py:38
  160.2 1.4 scale_and_turn.3
  (28 shorter events, 0.5 us)
Async XLA Ops:
  0.0 11.4 %copy-start = (s32[1,4,256]{2,1,0:T(4,128)S(1)}, s32[1,4,256]{2,1,0:T(4,128)}, u32[]{:S(2)}) copy-start(s32[1,4,256]{2,1,0:T(4,128)} %param.3) | copy-start | bytes 12292
  3.2 43.2 %collective-permute-start.4 = (f32[256,1536]{1,0:T(8,128)}, f32[256,1536]{1,0:T(8,128)}, u32[]{:S(2)}, u32[]{:S(2)}) collective-permute-start(f32[256,1536]{1,0:T(8,128)} %get-tuple-element.35), channel_id=1, source_target_pairs={{0,16},{1,17},{2,18},{3,19},{4,20},{5,21},{6,22},{7,23},{8,24},{9,... | collective-permute-start | bytes 4718600 | tf_op jit(solution)/shard_map/ppermute | solution.py:38
  8.1 6.3 %collective-permute-start = (f32[96,256]{0,1:T(8,128)S(1)}, f32[96,256]{0,1:T(8,128)S(1)}, u32[]{:S(2)}, u32[]{:S(2)}) collective-permute-start(f32[96,256]{0,1:T(8,128)S(1)} %slice_bitcast_fusion), channel_id=1, source_target_pairs={{0,3},{1,2},{2,1},{3,0},{4,7},{5,6},{6,5},{7,4},{8,11},{9,10},{10,... | collective-permute-start | bytes 294920 | tf_op jit(solution)/shard_map/ppermute | solution.py:38
  11.2 5.0 %collective-permute-start.1 = (f32[96,256]{0,1:T(8,128)S(1)}, f32[96,256]{0,1:T(8,128)S(1)}, u32[]{:S(2)}, u32[]{:S(2)}) collective-permute-start(f32[96,256]{0,1:T(8,128)S(1)} %slice_bitcast_fusion), channel_id=1, source_target_pairs={{0,1},{1,0},{2,3},{3,2},{4,5},{5,4},{6,7},{7,6},{8,9},{9,8},{10,11... | collective-permute-start | bytes 294920 | tf_op jit(solution)/shard_map/ppermute | solution.py:38
  17.7 28.7 %all-to-all-start = ((f32[4,296,256]{2,1,0:T(8,128)}), f32[4,296,256]{2,1,0:T(8,128)S(1)}, u32[]{:S(2)}, u32[]{:S(2)}) async-start(f32[4,296,256]{2,1,0:T(8,128)} %broadcast_in_dim.36), calls=%async_computation | async-start | bytes 2424832 | tf_op jit(solution)/shard_map/all_to_all | solution.py:144
  23.3 4.4 %collective-permute-start.2 = (f32[128,1536]{1,0:T(8,128)}, f32[128,1536]{1,0:T(8,128)S(1)}, u32[]{:S(2)}, u32[]{:S(2)}) collective-permute-start(f32[128,1536]{1,0:T(8,128)} %get-tuple-element.40), channel_id=1, source_target_pairs={{0,0},{1,1},{2,2},{3,3},{4,4},{5,5},{6,6},{7,7},{8,8},{9,9},{10,10... | collective-permute-start | bytes 2359304 | tf_op jit(solution)/shard_map/ppermute | solution.py:38
  25.1 21.4 %collective-permute-start.3 = (f32[128,1536]{1,0:T(8,128)}, f32[128,1536]{1,0:T(8,128)}, u32[]{:S(2)}, u32[]{:S(2)}) collective-permute-start(f32[128,1536]{1,0:T(8,128)} %get-tuple-element.39), channel_id=1, source_target_pairs={{0,2},{1,3},{2,0},{3,1},{4,6},{5,7},{6,4},{7,5},{8,10},{9,11},{10,... | collective-permute-start | bytes 2359304 | tf_op jit(solution)/shard_map/ppermute | solution.py:38
  27.7 18.9 %copy-start.1 = (f32[128,1536]{1,0:T(8,128)}, f32[128,1536]{1,0:T(8,128)S(1)}, u32[]{:S(2)}) copy-start(f32[128,1536]{1,0:T(8,128)S(1)} %collective-permute-done.2) | copy-start | bytes 2359300
  49.1 55.1 %all-to-all-start.1 = ((f32[8,896,128]{2,1,0:T(8,128)}), f32[8,896,128]{2,1,0:T(8,128)}, u32[]{:S(2)}, u32[]{:S(2)}) async-start(f32[8,896,128]{2,1,0:T(8,128)} %bitcast.24), calls=%async_computation.1 | async-start | bytes 7340032 | tf_op jit(solution)/shard_map/all_to_all | solution.py:168
  53.6 4.8 %copy-start.2 = (f32[128,1536]{1,0:T(8,128)S(1)}, f32[128,1536]{1,0:T(8,128)}, u32[]{:S(2)}) copy-start(f32[128,1536]{1,0:T(8,128)} %copy-done.1) | copy-start | bytes 2359300
  55.2 8.9 %collective-permute-start.7 = (f32[128,1536]{1,0:T(8,128)S(1)}, f32[128,1536]{1,0:T(8,128)S(1)}, u32[]{:S(2)}, u32[]{:S(2)}) collective-permute-start(f32[128,1536]{1,0:T(8,128)S(1)} %get-tuple-element.38), channel_id=1, source_target_pairs={{0,0},{1,1},{2,2},{3,3},{4,4},{5,5},{6,6},{7,7},{8,8},{9,9},{10,10... | collective-permute-start | bytes 2359304 | tf_op jit(solution)/shard_map/ppermute | solution.py:38
  55.9 23.2 %collective-permute-start.8 = (f32[128,1536]{1,0:T(8,128)S(1)}, f32[128,1536]{1,0:T(8,128)S(1)}, u32[]{:S(2)}, u32[]{:S(2)}) collective-permute-start(f32[128,1536]{1,0:T(8,128)S(1)} %get-tuple-element.37), channel_id=1, source_target_pairs={{0,2},{1,3},{2,0},{3,1},{4,6},{5,7},{6,4},{7,5},{8,10},{9,11},{10,... | collective-permute-start | bytes 2359304 | tf_op jit(solution)/shard_map/ppermute | solution.py:38
  58.5 24.7 %collective-permute-start.5 = (f32[128,1536]{1,0:T(8,128)S(1)}, f32[128,1536]{1,0:T(8,128)}, u32[]{:S(2)}, u32[]{:S(2)}) collective-permute-start(f32[128,1536]{1,0:T(8,128)S(1)} %copy-done.2), channel_id=1, source_target_pairs={{0,0},{1,33},{2,66},{3,99},{4,4},{5,37},{6,70},{7,103},{8,8},{9,41... | collective-permute-start | bytes 2359304 | tf_op jit(solution)/shard_map/ppermute | solution.py:38
  60.0 23.2 %collective-permute-start.6 = (f32[128,1536]{1,0:T(8,128)}, f32[128,1536]{1,0:T(8,128)}, u32[]{:S(2)}, u32[]{:S(2)}) collective-permute-start(f32[128,1536]{1,0:T(8,128)} %collective-permute-done.3), channel_id=1, source_target_pairs={{0,64},{1,97},{2,2},{3,35},{4,68},{5,101},{6,6},{7,39},{8,72},{9,1... | collective-permute-start | bytes 2359304 | tf_op jit(solution)/shard_map/ppermute | solution.py:38
  64.1 23.2 %collective-permute-start.11 = (f32[128,1536]{1,0:T(8,128)S(1)}, f32[128,1536]{1,0:T(8,128)S(1)}, u32[]{:S(2)}, u32[]{:S(2)}) collective-permute-start(f32[128,1536]{1,0:T(8,128)S(1)} %collective-permute-done.7), channel_id=1, source_target_pairs={{0,0},{1,33},{2,66},{3,99},{4,4},{5,37},{6,70},{7,103},{8,8},{9,41... | collective-permute-start | bytes 2359304 | tf_op jit(solution)/shard_map/ppermute | solution.py:38
  79.1 22.5 %collective-permute-start.12 = (f32[128,1536]{1,0:T(8,128)S(1)}, f32[128,1536]{1,0:T(8,128)S(1)}, u32[]{:S(2)}, u32[]{:S(2)}) collective-permute-start(f32[128,1536]{1,0:T(8,128)S(1)} %collective-permute-done.8), channel_id=1, source_target_pairs={{0,64},{1,97},{2,2},{3,35},{4,68},{5,101},{6,6},{7,39},{8,72},{9,1... | collective-permute-start | bytes 2359304 | tf_op jit(solution)/shard_map/ppermute | solution.py:38
  83.3 26.0 %collective-permute-start.10 = (f32[128,1536]{1,0:T(8,128)}, f32[128,1536]{1,0:T(8,128)}, u32[]{:S(2)}, u32[]{:S(2)}) collective-permute-start(f32[128,1536]{1,0:T(8,128)} %collective-permute-done.6.refs_1_), channel_id=1, source_target_pairs={{0,1},{1,0},{2,3},{3,2},{4,7},{5,6},{6,5},{7,4},{8,9},{9,8},{10,11... | collective-permute-start | bytes 2359304 | tf_op jit(solution)/shard_map/ppermute | solution.py:38
  87.2 22.1 %collective-permute-start.9 = (f32[128,1536]{1,0:T(8,128)}, f32[128,1536]{1,0:T(8,128)}, u32[]{:S(2)}, u32[]{:S(2)}) collective-permute-start(f32[128,1536]{1,0:T(8,128)} %collective-permute-done.5.refs_0_), channel_id=1, source_target_pairs={{0,1},{1,0},{2,3},{3,2},{4,7},{5,6},{6,5},{7,4},{8,9},{9,8},{10,11... | collective-permute-start | bytes 2359304 | tf_op jit(solution)/shard_map/ppermute | solution.py:38
  87.3 30.1 %collective-permute-start.13 = (f32[128,1536]{1,0:T(8,128)S(1)}, f32[128,1536]{1,0:T(8,128)S(1)}, u32[]{:S(2)}, u32[]{:S(2)}) collective-permute-start(f32[128,1536]{1,0:T(8,128)S(1)} %collective-permute-done.11.refs_0_), channel_id=1, source_target_pairs={{0,1},{1,0},{2,3},{3,2},{4,7},{5,6},{6,5},{7,4},{8,9},{9,8},{10,11... | collective-permute-start | bytes 2359304 | tf_op jit(solution)/shard_map/ppermute | solution.py:38
  101.6 21.1 %collective-permute-start.14 = (f32[128,1536]{1,0:T(8,128)S(1)}, f32[128,1536]{1,0:T(8,128)S(1)}, u32[]{:S(2)}, u32[]{:S(2)}) collective-permute-start(f32[128,1536]{1,0:T(8,128)S(1)} %collective-permute-done.12.refs_1_), channel_id=1, source_target_pairs={{0,1},{1,0},{2,3},{3,2},{4,7},{5,6},{6,5},{7,4},{8,9},{9,8},{10,11... | collective-permute-start | bytes 2359304 | tf_op jit(solution)/shard_map/ppermute | solution.py:38
  127.2 20.1 %collective-permute-start.16 = (f32[392,768]{1,0:T(8,128)S(1)}, f32[392,768]{1,0:T(8,128)S(1)}, u32[]{:S(2)}, u32[]{:S(2)}) collective-permute-start(f32[392,768]{1,0:T(8,128)S(1)} %get-tuple-element.34), channel_id=1, source_target_pairs={{0,3},{1,2},{2,1},{3,0},{4,5},{5,4},{6,7},{7,6},{8,11},{9,10},{10,... | collective-permute-start | bytes 3612680 | tf_op jit(solution)/shard_map/ppermute | solution.py:38
  137.4 22.8 %collective-permute-start.15 = (f32[392,768]{1,0:T(8,128)S(1)}, f32[392,768]{1,0:T(8,128)S(1)}, u32[]{:S(2)}, u32[]{:S(2)}) collective-permute-start(f32[392,768]{1,0:T(8,128)S(1)} %get-tuple-element.32), channel_id=1, source_target_pairs={{0,3},{1,2},{2,1},{3,0},{4,5},{5,4},{6,7},{7,6},{8,11},{9,10},{10,... | collective-permute-start | bytes 3612680 | tf_op jit(solution)/shard_map/ppermute | solution.py:38

commit v5 on v4

--- a/solution.py
+++ b/solution.py
@@ -12,7 +12,7 @@
 AXES = ("x", "zh", "zl", "core", "y")
 SIZES = (4, 2, 2, 2, 4)
 ROWS, COLS, HALF, QS, GROUP = 256, 3072, 1536, 96, 384
-CHUNK, TILE = 768, 768
+CHUNK, TILE = 512, 512
 F32, BF16 = jnp.float32, jnp.bfloat16
 
 
@@ -201,7 +201,7 @@
 
     to_mate = lambda x, zh, zl, c, y: (x, zh, zl, c, mate(y, c))
     ends = []
-    for n in range(2):
+    for n in range(HALF // CHUNK):
         ours, theirs = pl.pallas_call(
             second_kernel,
             grid=(tiles,),
@@ -220,12 +220,12 @@
         ends.append((ours, moved(theirs, to_mate)))
 
     result = []
-    for n in range(2):
+    for n in range(HALF // CHUNK):
         result = pl.pallas_call(
             final_kernel,
             grid=(tiles,),
             out_shape=jax.ShapeDtypeStruct((HALF * 3, 128), F32),
-            in_specs=[tile(GROUP + 8)] * 2 + [pl.BlockSpec(memory_space=pl.ANY)] * n,
+            in_specs=[tile(GROUP + 8)] * 2 + [pl.BlockSpec(memory_space=pl.ANY)] * (n > 0),
             out_specs=pl.BlockSpec((TILE * 3, 128), lambda t, n=n: (t + n * tiles, 0)),
             input_output_aliases={2: 0} if n else {},
             compiler_params=limit(),

time: 163 us -> 162 us (level)
  waiting for transfers between devices: 67.5 us -> 60.5 us
  starting transfers between devices: 57.1 us -> 60.6 us
  Pallas kernels: 25 us -> 27.4 us
    ppermute x17 -> x18, waiting for transfers between devices: 67.5 us -> 60.4 us  [moved(): lax.ppermute(array, AXES, [(index(*t[:5]), index(*t[5])) for t in table])]
    ppermute x17 -> x18, starting transfers between devices: 48.3 us -> 51.8 us  [moved(): lax.ppermute(array, AXES, [(index(*t[:5]), index(*t[5])) for t in table])]
    pallas_call x2 -> x3, Pallas kernels: 9.09 us -> 10.9 us  [shards(): pl.pallas_call(second_kernel, grid=(tiles,), out_shape=(jax.ShapeDtypeStr...]
    pallas_call x2 -> x3, Pallas kernels: 2.81 us -> 3.5 us  [shards(): pl.pallas_call(final_kernel, grid=(tiles,), out_shape=jax.ShapeDtypeStruc...]
  transfers between devices with their start and end apart: 19 -> 20, of which waited for: 9 -> 8; matrix products, arithmetic and copies ran while one was open for 4% -> 4% of each run, Pallas kernels for 12% -> 14%
where the time goes in v5:
time: 162 us; the launch traced here: 160 us
  starting transfers between devices  60.6 us (37%)
  waiting for transfers between devices  60.5 us (37%)
  Pallas kernels  27.4 us (17%)
  local copies, waits for them, and re-layouts  11.1 us (7%)
    ppermute x18, waiting for transfers between devices, moved(): lax.ppermute(array, AXES, [(index(*t[:5]), index(*t[5])) for t in table])  60.4 us
    ppermute x18, starting transfers between devices, moved(): lax.ppermute(array, AXES, [(index(*t[:5]), index(*t[5])) for t in table])  51.8 us
    pallas_call x3, Pallas kernels, shards(): pl.pallas_call(second_kernel, grid=(tiles,), out_shape=(jax.ShapeDtypeStr...  10.9 us
    pallas_call x1, Pallas kernels, shards(): pl.pallas_call(first_kernel, grid=(HALF // TILE,), out_shape=jax.ShapeDty...  7.94 us
    pallas_call x1, Pallas kernels, shards(): pl.pallas_call(query_kernel, out_shape=(jax.ShapeDtypeStruct((2 * GROUP,...  5.1 us
    all_to_all x1, starting transfers between devices, shards(): pieces = lax.all_to_all(slots, ('zh', 'zl', 'core'), 0, 0, tiled=True)  4.51 us
    all_to_all x1, starting transfers between devices, shards(): raw = lax.all_to_all(raw, 'x', 0, 0, tiled=True)  4.29 us
    pallas_call x3, Pallas kernels, shards(): pl.pallas_call(final_kernel, grid=(tiles,), out_shape=jax.ShapeDtypeStruc...  3.5 us
  transfers between devices with their start and end apart: 20, of which 8 were waited for; matrix products, arithmetic and copies ran while one was open for 4% of the time, Pallas kernels for 14%

profile of v5, /device:TPU:0, one launch (start us, length us, event | category | flops | bytes accessed | tf_op | source)
XLA Modules:
  0.0 160.4 jit_solution(16932624581263735568)
XLA Ops:
  0.0 3.2 %constant_dynamic-slice_fusion = (f32[256,1536]{1,0:T(8,128)}, f32[256,1536]{1,0:T(8,128)S(1)}) fusion(f32[256,3072]{1,0:T(8,128)} %param.2, s32[]{:T(128)S(6)} %select_n.64, s32[]{:T(128)S(6)} %select_n.63), kind=kLoop, calls=%fused_computation.25 | loop fusion | bytes 6291464 | tf_op jit(solution)/shard_map/dynamic_slice | solution.py:125
  3.2 4.0 %collective-permute-start.4 = (f32[256,1536]{1,0:T(8,128)}, f32[256,1536]{1,0:T(8,128)}, u32[]{:S(2)}, u32[]{:S(2)}) collective-permute-start(f32[256,1536]{1,0:T(8,128)} %get-tuple-element.39), channel_id=1, source_target_pairs={{0,16},{1,17},{2,18},{3,19},{4,20},{5,21},{6,22},{7,23},{8,24},{9,... | collective-permute-start | bytes 4718600 | tf_op jit(solution)/shard_map/ppermute | solution.py:38
  7.2 0.9 slice_bitcast_fusion
  8.1 3.1 %collective-permute-start = (f32[96,256]{0,1:T(8,128)S(1)}, f32[96,256]{0,1:T(8,128)S(1)}, u32[]{:S(2)}, u32[]{:S(2)}) collective-permute-start(f32[96,256]{0,1:T(8,128)S(1)} %slice_bitcast_fusion), channel_id=1, source_target_pairs={{0,3},{1,2},{2,1},{3,0},{4,7},{5,6},{6,5},{7,4},{8,11},{9,10},{10,... | collective-permute-start | bytes 294920 | tf_op jit(solution)/shard_map/ppermute | solution.py:38
  11.2 0.1 collective-permute-start.1
  11.4 0.1 copy.5
  11.5 2.9 %collective-permute-done = f32[96,256]{0,1:T(8,128)S(1)} collective-permute-done((f32[96,256]{0,1:T(8,128)S(1)}, f32[96,256]{0,1:T(8,128)S(1)}, u32[]{:S(2)}, u32[]{:S(2)}) %collective-permute-start) | collective-permute-done | bytes 98336 | tf_op jit(solution)/shard_map/ppermute | solution.py:38
  14.4 1.8 %collective-permute-done.1 = f32[96,256]{0,1:T(8,128)S(1)} collective-permute-done((f32[96,256]{0,1:T(8,128)S(1)}, f32[96,256]{0,1:T(8,128)S(1)}, u32[]{:S(2)}, u32[]{:S(2)}) %collective-permute-start.1) | collective-permute-done | bytes 98336 | tf_op jit(solution)/shard_map/ppermute | solution.py:38
  16.2 0.3 concatenate.13
  16.4 0.1 copy.6
  16.6 1.1 broadcast_in_dim.36
  17.7 4.3 %all-to-all-start = ((f32[4,296,256]{2,1,0:T(8,128)}), f32[4,296,256]{2,1,0:T(8,128)S(1)}, u32[]{:S(2)}, u32[]{:S(2)}) async-start(f32[4,296,256]{2,1,0:T(8,128)} %broadcast_in_dim.36), calls=%async_computation | async-start | bytes 2424832 | tf_op jit(solution)/shard_map/all_to_all | solution.py:144
  22.0 1.3 fusion.7
  23.3 1.8 %collective-permute-start.2 = (f32[128,1536]{1,0:T(8,128)}, f32[128,1536]{1,0:T(8,128)S(1)}, u32[]{:S(2)}, u32[]{:S(2)}) collective-permute-start(f32[128,1536]{1,0:T(8,128)} %get-tuple-element.44), channel_id=1, source_target_pairs={{0,0},{1,1},{2,2},{3,3},{4,4},{5,5},{6,6},{7,7},{8,8},{9,9},{10,10... | collective-permute-start | bytes 2359304 | tf_op jit(solution)/shard_map/ppermute | solution.py:38
  25.1 2.5 %collective-permute-start.3 = (f32[128,1536]{1,0:T(8,128)}, f32[128,1536]{1,0:T(8,128)}, u32[]{:S(2)}, u32[]{:S(2)}) collective-permute-start(f32[128,1536]{1,0:T(8,128)} %get-tuple-element.43), channel_id=1, source_target_pairs={{0,2},{1,3},{2,0},{3,1},{4,6},{5,7},{6,4},{7,5},{8,10},{9,11},{10,... | collective-permute-start | bytes 2359304 | tf_op jit(solution)/shard_map/ppermute | solution.py:38
  27.7 18.8 %collective-permute-done.3 = f32[128,1536]{1,0:T(8,128)} collective-permute-done((f32[128,1536]{1,0:T(8,128)}, f32[128,1536]{1,0:T(8,128)}, u32[]{:S(2)}, u32[]{:S(2)}) %collective-permute-start.3) | collective-permute-done | bytes 786464 | tf_op jit(solution)/shard_map/ppermute | solution.py:38
  46.5 0.1 slice.47
  46.7 0.1 slice_select_fusion
  46.8 0.1 fusion.3
  47.0 2.1 %broadcast_in_dim.38 = f32[4,2,896,128]{3,2,1,0:T(8,128)} broadcast(f32[2,896,128]{2,1,0:T(8,128)S(1)} %pad_maximum_fusion), dimensions={1,2,3} | broadcast | bytes 4587520 | tf_op jit(solution)/shard_map/broadcast_in_dim | solution.py:167
  49.1 4.5 %all-to-all-start.1 = ((f32[8,896,128]{2,1,0:T(8,128)}), f32[8,896,128]{2,1,0:T(8,128)}, u32[]{:S(2)}, u32[]{:S(2)}) async-start(f32[8,896,128]{2,1,0:T(8,128)} %bitcast.24), calls=%async_computation.1 | async-start | bytes 7340032 | tf_op jit(solution)/shard_map/all_to_all | solution.py:168
  53.6 1.5 fusion.6
  55.2 0.7 collective-permute-start.7
  55.9 2.6 %collective-permute-start.8 = (f32[128,1536]{1,0:T(8,128)S(1)}, f32[128,1536]{1,0:T(8,128)S(1)}, u32[]{:S(2)}, u32[]{:S(2)}) collective-permute-start(f32[128,1536]{1,0:T(8,128)S(1)} %get-tuple-element.41), channel_id=1, source_target_pairs={{0,2},{1,3},{2,0},{3,1},{4,6},{5,7},{6,4},{7,5},{8,10},{9,11},{10,... | collective-permute-start | bytes 2359304 | tf_op jit(solution)/shard_map/ppermute | solution.py:38
  58.5 1.6 collective-permute-start.5
  60.0 4.1 %collective-permute-start.6 = (f32[128,1536]{1,0:T(8,128)}, f32[128,1536]{1,0:T(8,128)}, u32[]{:S(2)}, u32[]{:S(2)}) collective-permute-start(f32[128,1536]{1,0:T(8,128)} %collective-permute-done.3), channel_id=1, source_target_pairs={{0,64},{1,97},{2,2},{3,35},{4,68},{5,101},{6,6},{7,39},{8,72},{9,1... | collective-permute-start | bytes 2359304 | tf_op jit(solution)/shard_map/ppermute | solution.py:38
  64.2 0.7 collective-permute-start.11
  64.9 14.2 %collective-permute-done.8 = f32[128,1536]{1,0:T(8,128)S(1)} collective-permute-done((f32[128,1536]{1,0:T(8,128)S(1)}, f32[128,1536]{1,0:T(8,128)S(1)}, u32[]{:S(2)}, u32[]{:S(2)}) %collective-permute-start.8) | collective-permute-done | bytes 786464 | tf_op jit(solution)/shard_map/ppermute | solution.py:38
  79.1 4.1 %collective-permute-start.12 = (f32[128,1536]{1,0:T(8,128)S(1)}, f32[128,1536]{1,0:T(8,128)S(1)}, u32[]{:S(2)}, u32[]{:S(2)}) collective-permute-start(f32[128,1536]{1,0:T(8,128)S(1)} %collective-permute-done.8), channel_id=1, source_target_pairs={{0,64},{1,97},{2,2},{3,35},{4,68},{5,101},{6,6},{7,39},{8,72},{9,1... | collective-permute-start | bytes 2359304 | tf_op jit(solution)/shard_map/ppermute | solution.py:38
  83.3 3.9 %collective-permute-start.9 = (f32[128,1536]{1,0:T(8,128)}, f32[128,1536]{1,0:T(8,128)}, u32[]{:S(2)}, u32[]{:S(2)}) collective-permute-start(f32[128,1536]{1,0:T(8,128)} %collective-permute-done.5.refs_0_), channel_id=1, source_target_pairs={{0,1},{1,0},{2,3},{3,2},{4,7},{5,6},{6,5},{7,4},{8,9},{9,8},{10,11... | collective-permute-start | bytes 2359304 | tf_op jit(solution)/shard_map/ppermute | solution.py:38
  87.2 11.4 %collective-permute-start.13 = (f32[128,1536]{1,0:T(8,128)S(1)}, f32[128,1536]{1,0:T(8,128)S(1)}, u32[]{:S(2)}, u32[]{:S(2)}) collective-permute-start(f32[128,1536]{1,0:T(8,128)S(1)} %collective-permute-done.11.refs_0_), channel_id=1, source_target_pairs={{0,1},{1,0},{2,3},{3,2},{4,7},{5,6},{6,5},{7,4},{8,9},{9,8},{10,11... | collective-permute-start | bytes 2359304 | tf_op jit(solution)/shard_map/ppermute | solution.py:38
  98.6 3.0 %collective-permute-done.12.refs_1_ = f32[128,1536]{1,0:T(8,128)S(1)} collective-permute-done((f32[128,1536]{1,0:T(8,128)S(1)}, f32[128,1536]{1,0:T(8,128)S(1)}, u32[]{:S(2)}, u32[]{:S(2)}) %collective-permute-start.12) | collective-permute-done | bytes 786464 | tf_op jit(solution)/shard_map/ppermute | solution.py:38
  101.6 2.2 %collective-permute-start.14 = (f32[128,1536]{1,0:T(8,128)S(1)}, f32[128,1536]{1,0:T(8,128)S(1)}, u32[]{:S(2)}, u32[]{:S(2)}) collective-permute-start(f32[128,1536]{1,0:T(8,128)S(1)} %collective-permute-done.12.refs_1_), channel_id=1, source_target_pairs={{0,1},{1,0},{2,3},{3,2},{4,7},{5,6},{6,5},{7,4},{8,9},{9,8},{10,11... | collective-permute-start | bytes 2359304 | tf_op jit(solution)/shard_map/ppermute | solution.py:38
  104.1 0.1 concatenate.12.at_ref
  104.2 5.1 %query_prepare.1 = (bf16[768,3072]{1,0:T(8,128)(2,1)}, f32[2,8,128]{2,1,0:T(8,128)S(1)}) custom-call(s32[19]{0:T(128)S(1)} %concatenate.12.at_ref, f32[8,896,128]{2,1,0:T(8,128)} %all-to-all-done.1.pieces_ref), custom_call_target="tpu_custom_call" | custom-call | tf_op jit(solution)/shard_map/query_prepare/pallas_call | solution.py:175
  109.3 7.9 %product_first_rows.1.before_ref = f32[776,1536]{1,0:T(8,128)} custom-call(bf16[768,3072]{1,0:T(8,128)(2,1)} %get-tuple-element.26.hilo_ref, f32[128,1536]{1,0:T(8,128)} %collective-permute-done.5.refs_0_, f32[128,1536]{1,0:T(8,128)} %collective-permute-done.6.refs_1_, f32[128,1536]{1,0:T(8,128)} %collective-permute-done.9.refs_2_, ...), custom_call_target="tpu_custom_call" | custom-call | tf_op jit(solution)/shard_map/product_first_rows/pallas_call | solution.py:191
  117.2 5.4 %collective-permute-done.14.refs_3_ = f32[128,1536]{1,0:T(8,128)S(1)} collective-permute-done((f32[128,1536]{1,0:T(8,128)S(1)}, f32[128,1536]{1,0:T(8,128)S(1)}, u32[]{:S(2)}, u32[]{:S(2)}) %collective-permute-start.14) | collective-permute-done | bytes 786464 | tf_op jit(solution)/shard_map/ppermute | solution.py:38
  122.7 3.6 %product_other_rows.5 = (f32[392,512]{1,0:T(8,128)S(1)}, f32[392,512]{1,0:T(8,128)S(1)}) custom-call(bf16[768,3072]{1,0:T(8,128)(2,1)} %get-tuple-element.26.hilo_ref, f32[2,8,128]{2,1,0:T(8,128)S(1)} %get-tuple-element.27.norms_ref, f32[776,1536]{1,0:T(8,128)} %product_first_rows.1.before_ref, f32[128,1536]{1,0:T(8,128)S(1)} %collective-permute-done.11.refs_0_, ...), custom_call_target="tpu_custom_call" | custom-call | tf_op jit(solution)/shard_map/product_other_rows/pallas_call | solution.py:205
  126.3 5.6 %collective-permute-start.17 = (f32[392,512]{1,0:T(8,128)S(1)}, f32[392,512]{1,0:T(8,128)S(1)}, u32[]{:S(2)}, u32[]{:S(2)}) collective-permute-start(f32[392,512]{1,0:T(8,128)S(1)} %get-tuple-element.38), channel_id=1, source_target_pairs={{0,3},{1,2},{2,1},{3,0},{4,5},{5,4},{6,7},{7,6},{8,11},{9,10},{10,... | collective-permute-start | bytes 2408456 | tf_op jit(solution)/shard_map/ppermute | solution.py:38
  131.9 3.6 %product_other_rows.4 = (f32[392,512]{1,0:T(8,128)S(1)}, f32[392,512]{1,0:T(8,128)S(1)}) custom-call(bf16[768,3072]{1,0:T(8,128)(2,1)} %get-tuple-element.26.hilo_ref, f32[2,8,128]{2,1,0:T(8,128)S(1)} %get-tuple-element.27.norms_ref, f32[776,1536]{1,0:T(8,128)} %product_first_rows.1.before_ref, f32[128,1536]{1,0:T(8,128)S(1)} %collective-permute-done.11.refs_0_, ...), custom_call_target="tpu_custom_call" | custom-call | tf_op jit(solution)/shard_map/product_other_rows/pallas_call | solution.py:205
  135.5 0.1 collective-permute-start.16
  135.6 3.7 %product_other_rows.3 = (f32[392,512]{1,0:T(8,128)S(1)}, f32[392,512]{1,0:T(8,128)S(1)}) custom-call(bf16[768,3072]{1,0:T(8,128)(2,1)} %get-tuple-element.26.hilo_ref, f32[2,8,128]{2,1,0:T(8,128)S(1)} %get-tuple-element.27.norms_ref, f32[776,1536]{1,0:T(8,128)} %product_first_rows.1.before_ref, f32[128,1536]{1,0:T(8,128)S(1)} %collective-permute-done.11.refs_0_, ...), custom_call_target="tpu_custom_call" | custom-call | tf_op jit(solution)/shard_map/product_other_rows/pallas_call | solution.py:205
  139.3 3.3 %collective-permute-start.15 = (f32[392,512]{1,0:T(8,128)S(1)}, f32[392,512]{1,0:T(8,128)S(1)}, u32[]{:S(2)}, u32[]{:S(2)}) collective-permute-start(f32[392,512]{1,0:T(8,128)S(1)} %get-tuple-element.34), channel_id=1, source_target_pairs={{0,3},{1,2},{2,1},{3,0},{4,5},{5,4},{6,7},{7,6},{8,11},{9,10},{10,... | collective-permute-start | bytes 2408456 | tf_op jit(solution)/shard_map/ppermute | solution.py:38
  142.6 1.2 scale_and_turn.3.refs_0_
  143.8 6.9 %collective-permute-done.16.got = f32[392,512]{1,0:T(8,128)S(1)} collective-permute-done((f32[392,512]{1,0:T(8,128)S(1)}, f32[392,512]{1,0:T(8,128)S(1)}, u32[]{:S(2)}, u32[]{:S(2)}) %collective-permute-start.16) | collective-permute-done | bytes 802848 | tf_op jit(solution)/shard_map/ppermute | solution.py:38
  150.6 1.2 scale_and_turn.4.refs_0_
  151.8 7.4 %collective-permute-done.15.got = f32[392,512]{1,0:T(8,128)S(1)} collective-permute-done((f32[392,512]{1,0:T(8,128)S(1)}, f32[392,512]{1,0:T(8,128)S(1)}, u32[]{:S(2)}, u32[]{:S(2)}) %collective-permute-start.15) | collective-permute-done | bytes 802848 | tf_op jit(solution)/shard_map/ppermute | solution.py:38
  159.2 1.2 scale_and_turn.5
  (32 shorter events, 0.6 us)
Async XLA Ops:
  0.0 11.4 %copy-start = (s32[1,4,256]{2,1,0:T(4,128)S(1)}, s32[1,4,256]{2,1,0:T(4,128)}, u32[]{:S(2)}) copy-start(s32[1,4,256]{2,1,0:T(4,128)} %param.3) | copy-start | bytes 12292
  3.2 43.2 %collective-permute-start.4 = (f32[256,1536]{1,0:T(8,128)}, f32[256,1536]{1,0:T(8,128)}, u32[]{:S(2)}, u32[]{:S(2)}) collective-permute-start(f32[256,1536]{1,0:T(8,128)} %get-tuple-element.39), channel_id=1, source_target_pairs={{0,16},{1,17},{2,18},{3,19},{4,20},{5,21},{6,22},{7,23},{8,24},{9,... | collective-permute-start | bytes 4718600 | tf_op jit(solution)/shard_map/ppermute | solution.py:38
  8.1 6.3 %collective-permute-start = (f32[96,256]{0,1:T(8,128)S(1)}, f32[96,256]{0,1:T(8,128)S(1)}, u32[]{:S(2)}, u32[]{:S(2)}) collective-permute-start(f32[96,256]{0,1:T(8,128)S(1)} %slice_bitcast_fusion), channel_id=1, source_target_pairs={{0,3},{1,2},{2,1},{3,0},{4,7},{5,6},{6,5},{7,4},{8,11},{9,10},{10,... | collective-permute-start | bytes 294920 | tf_op jit(solution)/shard_map/ppermute | solution.py:38
  11.2 5.0 %collective-permute-start.1 = (f32[96,256]{0,1:T(8,128)S(1)}, f32[96,256]{0,1:T(8,128)S(1)}, u32[]{:S(2)}, u32[]{:S(2)}) collective-permute-start(f32[96,256]{0,1:T(8,128)S(1)} %slice_bitcast_fusion), channel_id=1, source_target_pairs={{0,1},{1,0},{2,3},{3,2},{4,5},{5,4},{6,7},{7,6},{8,9},{9,8},{10,11... | collective-permute-start | bytes 294920 | tf_op jit(solution)/shard_map/ppermute | solution.py:38
  17.7 28.7 %all-to-all-start = ((f32[4,296,256]{2,1,0:T(8,128)}), f32[4,296,256]{2,1,0:T(8,128)S(1)}, u32[]{:S(2)}, u32[]{:S(2)}) async-start(f32[4,296,256]{2,1,0:T(8,128)} %broadcast_in_dim.36), calls=%async_computation | async-start | bytes 2424832 | tf_op jit(solution)/shard_map/all_to_all | solution.py:144
  23.3 4.4 %collective-permute-start.2 = (f32[128,1536]{1,0:T(8,128)}, f32[128,1536]{1,0:T(8,128)S(1)}, u32[]{:S(2)}, u32[]{:S(2)}) collective-permute-start(f32[128,1536]{1,0:T(8,128)} %get-tuple-element.44), channel_id=1, source_target_pairs={{0,0},{1,1},{2,2},{3,3},{4,4},{5,5},{6,6},{7,7},{8,8},{9,9},{10,10... | collective-permute-start | bytes 2359304 | tf_op jit(solution)/shard_map/ppermute | solution.py:38
  25.1 21.4 %collective-permute-start.3 = (f32[128,1536]{1,0:T(8,128)}, f32[128,1536]{1,0:T(8,128)}, u32[]{:S(2)}, u32[]{:S(2)}) collective-permute-start(f32[128,1536]{1,0:T(8,128)} %get-tuple-element.43), channel_id=1, source_target_pairs={{0,2},{1,3},{2,0},{3,1},{4,6},{5,7},{6,4},{7,5},{8,10},{9,11},{10,... | collective-permute-start | bytes 2359304 | tf_op jit(solution)/shard_map/ppermute | solution.py:38
  27.7 18.8 %copy-start.1 = (f32[128,1536]{1,0:T(8,128)}, f32[128,1536]{1,0:T(8,128)S(1)}, u32[]{:S(2)}) copy-start(f32[128,1536]{1,0:T(8,128)S(1)} %collective-permute-done.2) | copy-start | bytes 2359300
  49.1 55.1 %all-to-all-start.1 = ((f32[8,896,128]{2,1,0:T(8,128)}), f32[8,896,128]{2,1,0:T(8,128)}, u32[]{:S(2)}, u32[]{:S(2)}) async-start(f32[8,896,128]{2,1,0:T(8,128)} %bitcast.24), calls=%async_computation.1 | async-start | bytes 7340032 | tf_op jit(solution)/shard_map/all_to_all | solution.py:168
  53.6 4.8 %copy-start.2 = (f32[128,1536]{1,0:T(8,128)S(1)}, f32[128,1536]{1,0:T(8,128)}, u32[]{:S(2)}) copy-start(f32[128,1536]{1,0:T(8,128)} %copy-done.1) | copy-start | bytes 2359300
  55.2 9.0 %collective-permute-start.7 = (f32[128,1536]{1,0:T(8,128)S(1)}, f32[128,1536]{1,0:T(8,128)S(1)}, u32[]{:S(2)}, u32[]{:S(2)}) collective-permute-start(f32[128,1536]{1,0:T(8,128)S(1)} %get-tuple-element.42), channel_id=1, source_target_pairs={{0,0},{1,1},{2,2},{3,3},{4,4},{5,5},{6,6},{7,7},{8,8},{9,9},{10,10... | collective-permute-start | bytes 2359304 | tf_op jit(solution)/shard_map/ppermute | solution.py:38
  55.9 23.2 %collective-permute-start.8 = (f32[128,1536]{1,0:T(8,128)S(1)}, f32[128,1536]{1,0:T(8,128)S(1)}, u32[]{:S(2)}, u32[]{:S(2)}) collective-permute-start(f32[128,1536]{1,0:T(8,128)S(1)} %get-tuple-element.41), channel_id=1, source_target_pairs={{0,2},{1,3},{2,0},{3,1},{4,6},{5,7},{6,4},{7,5},{8,10},{9,11},{10,... | collective-permute-start | bytes 2359304 | tf_op jit(solution)/shard_map/ppermute | solution.py:38
  58.5 24.8 %collective-permute-start.5 = (f32[128,1536]{1,0:T(8,128)S(1)}, f32[128,1536]{1,0:T(8,128)}, u32[]{:S(2)}, u32[]{:S(2)}) collective-permute-start(f32[128,1536]{1,0:T(8,128)S(1)} %copy-done.2), channel_id=1, source_target_pairs={{0,0},{1,33},{2,66},{3,99},{4,4},{5,37},{6,70},{7,103},{8,8},{9,41... | collective-permute-start | bytes 2359304 | tf_op jit(solution)/shard_map/ppermute | solution.py:38
  60.0 23.2 %collective-permute-start.6 = (f32[128,1536]{1,0:T(8,128)}, f32[128,1536]{1,0:T(8,128)}, u32[]{:S(2)}, u32[]{:S(2)}) collective-permute-start(f32[128,1536]{1,0:T(8,128)} %collective-permute-done.3), channel_id=1, source_target_pairs={{0,64},{1,97},{2,2},{3,35},{4,68},{5,101},{6,6},{7,39},{8,72},{9,1... | collective-permute-start | bytes 2359304 | tf_op jit(solution)/shard_map/ppermute | solution.py:38
  64.2 23.1 %collective-permute-start.11 = (f32[128,1536]{1,0:T(8,128)S(1)}, f32[128,1536]{1,0:T(8,128)S(1)}, u32[]{:S(2)}, u32[]{:S(2)}) collective-permute-start(f32[128,1536]{1,0:T(8,128)S(1)} %collective-permute-done.7), channel_id=1, source_target_pairs={{0,0},{1,33},{2,66},{3,99},{4,4},{5,37},{6,70},{7,103},{8,8},{9,41... | collective-permute-start | bytes 2359304 | tf_op jit(solution)/shard_map/ppermute | solution.py:38
  79.1 22.5 %collective-permute-start.12 = (f32[128,1536]{1,0:T(8,128)S(1)}, f32[128,1536]{1,0:T(8,128)S(1)}, u32[]{:S(2)}, u32[]{:S(2)}) collective-permute-start(f32[128,1536]{1,0:T(8,128)S(1)} %collective-permute-done.8), channel_id=1, source_target_pairs={{0,64},{1,97},{2,2},{3,35},{4,68},{5,101},{6,6},{7,39},{8,72},{9,1... | collective-permute-start | bytes 2359304 | tf_op jit(solution)/shard_map/ppermute | solution.py:38
  83.3 26.0 %collective-permute-start.9 = (f32[128,1536]{1,0:T(8,128)}, f32[128,1536]{1,0:T(8,128)}, u32[]{:S(2)}, u32[]{:S(2)}) collective-permute-start(f32[128,1536]{1,0:T(8,128)} %collective-permute-done.5.refs_0_), channel_id=1, source_target_pairs={{0,1},{1,0},{2,3},{3,2},{4,7},{5,6},{6,5},{7,4},{8,9},{9,8},{10,11... | collective-permute-start | bytes 2359304 | tf_op jit(solution)/shard_map/ppermute | solution.py:38
  87.2 22.1 %collective-permute-start.10 = (f32[128,1536]{1,0:T(8,128)}, f32[128,1536]{1,0:T(8,128)}, u32[]{:S(2)}, u32[]{:S(2)}) collective-permute-start(f32[128,1536]{1,0:T(8,128)} %collective-permute-done.6.refs_1_), channel_id=1, source_target_pairs={{0,1},{1,0},{2,3},{3,2},{4,7},{5,6},{6,5},{7,4},{8,9},{9,8},{10,11... | collective-permute-start | bytes 2359304 | tf_op jit(solution)/shard_map/ppermute | solution.py:38
  87.2 30.0 %collective-permute-start.13 = (f32[128,1536]{1,0:T(8,128)S(1)}, f32[128,1536]{1,0:T(8,128)S(1)}, u32[]{:S(2)}, u32[]{:S(2)}) collective-permute-start(f32[128,1536]{1,0:T(8,128)S(1)} %collective-permute-done.11.refs_0_), channel_id=1, source_target_pairs={{0,1},{1,0},{2,3},{3,2},{4,7},{5,6},{6,5},{7,4},{8,9},{9,8},{10,11... | collective-permute-start | bytes 2359304 | tf_op jit(solution)/shard_map/ppermute | solution.py:38
  101.6 21.1 %collective-permute-start.14 = (f32[128,1536]{1,0:T(8,128)S(1)}, f32[128,1536]{1,0:T(8,128)S(1)}, u32[]{:S(2)}, u32[]{:S(2)}) collective-permute-start(f32[128,1536]{1,0:T(8,128)S(1)} %collective-permute-done.12.refs_1_), channel_id=1, source_target_pairs={{0,1},{1,0},{2,3},{3,2},{4,7},{5,6},{6,5},{7,4},{8,9},{9,8},{10,11... | collective-permute-start | bytes 2359304 | tf_op jit(solution)/shard_map/ppermute | solution.py:38
  126.3 16.3 %collective-permute-start.17 = (f32[392,512]{1,0:T(8,128)S(1)}, f32[392,512]{1,0:T(8,128)S(1)}, u32[]{:S(2)}, u32[]{:S(2)}) collective-permute-start(f32[392,512]{1,0:T(8,128)S(1)} %get-tuple-element.38), channel_id=1, source_target_pairs={{0,3},{1,2},{2,1},{3,0},{4,5},{5,4},{6,7},{7,6},{8,11},{9,10},{10,... | collective-permute-start | bytes 2408456 | tf_op jit(solution)/shard_map/ppermute | solution.py:38
  135.5 15.2 %collective-permute-start.16 = (f32[392,512]{1,0:T(8,128)S(1)}, f32[392,512]{1,0:T(8,128)S(1)}, u32[]{:S(2)}, u32[]{:S(2)}) collective-permute-start(f32[392,512]{1,0:T(8,128)S(1)} %get-tuple-element.36), channel_id=1, source_target_pairs={{0,3},{1,2},{2,1},{3,0},{4,5},{5,4},{6,7},{7,6},{8,11},{9,10},{10,... | collective-permute-start | bytes 2408456 | tf_op jit(solution)/shard_map/ppermute | solution.py:38
  139.3 19.9 %collective-permute-start.15 = (f32[392,512]{1,0:T(8,128)S(1)}, f32[392,512]{1,0:T(8,128)S(1)}, u32[]{:S(2)}, u32[]{:S(2)}) collective-permute-start(f32[392,512]{1,0:T(8,128)S(1)} %get-tuple-element.34), channel_id=1, source_target_pairs={{0,3},{1,2},{2,1},{3,0},{4,5},{5,4},{6,7},{7,6},{8,11},{9,10},{10,... | collective-permute-start | bytes 2408456 | tf_op jit(solution)/shard_map/ppermute | solution.py:38
